TPU v7x, 512 devices: a whole 4x4x16 slice. The times are simulated.
512 devices in a mesh: dp: 16 (over z_lo, core), mp: 32 (over y, z_hi, x).
Axes of the slice: x: 4, y: 4, z: 16 (z_hi: 2, z_lo: 8; z = z_hi * 8 + z_lo), core: 2. Of those that a mesh axis runs over, the one named last changes fastest.
Arguments:
- acts: bfloat16 [2048, 2688], P('dp', 'mp'), may hold values from -6 to 6
- cotangents: bfloat16 [4, 2048, 2688], P(None, 'dp', 'mp'), may hold values from -1.1953125 to 1.1953125
- w_gate: bfloat16 [2688, 10752], P('dp', 'mp'), may hold values from -0.125 to 0.125
- w_up: bfloat16 [2688, 10752], P('dp', 'mp'), may hold values from -0.125 to 0.125
- w_down: bfloat16 [10752, 2688], P('mp', 'dp'), may hold values from -0.0625 to 0.0625
- unit_rank: int32 [10752], P('mp'), may hold values from 0 to 10751, as said below
Outputs:
- grad_acts: bfloat16 [2048, 2688], P('dp', 'mp')
- grad_gate: bfloat16 [2688, 10752], P('dp', 'mp')
- grad_up: bfloat16 [2688, 10752], P('dp', 'mp')
- grad_down: bfloat16 [10752, 2688], P('mp', 'dp')
Inputs may be any that keep to these rules, and one draw needn't show every extreme that they name: unit_rank is a permutation of 0 to 10751. Every block of 336 consecutive units (the units of one index of mp) holds exactly 42 ranks below 1344, 42 ranks from 1344 to below 2688, and 84 ranks from 2688 to below 5376.
All inputs are finite; a program needn't handle non-finite values.
Results may differ from a plain program's by a relative error of at most 0.025.
Values may be sent and summed in bfloat16 or wider, within the bound.
No kernel may reach another device: no remote copies, remote signals or barrier semaphores. Data moves between devices by JAX's collectives and lax.ppermute only.
A program may use at most 64 MiB of HBM per device.

v0:
```python
import jax
import jax.numpy as jnp
from jax import lax
from jax.sharding import PartitionSpec as P

FF = 10752


gelu_scale = 0.7978845608028654


def gelu_parts(values):
    tanh_arg = gelu_scale * (values + 0.044715 * values * values * values)
    tanh_val = jnp.tanh(tanh_arg)
    activated = 0.5 * values * (1.0 + tanh_val)
    slope = 0.5 * (1.0 + tanh_val) + 0.5 * values * (1.0 - tanh_val * tanh_val) * gelu_scale * (
        1.0 + 3.0 * 0.044715 * values * values
    )
    return (activated, slope)


def contract_last(left_side, right_side):
    return lax.dot_general(
        left_side, right_side, (((1,), (1,)), ((), ())), preferred_element_type=jnp.float32
    )


def contract_first(left_side, right_side):
    return lax.dot_general(
        left_side, right_side, (((0,), (0,)), ((), ())), preferred_element_type=jnp.float32
    )


def suffix_sums(cot_all):
    third = cot_all[3].astype(jnp.float32)
    second = cot_all[2].astype(jnp.float32) + third
    first = cot_all[1].astype(jnp.float32) + second
    zeroth = cot_all[0].astype(jnp.float32) + first
    return jnp.stack([zeroth, first, second, third]).astype(jnp.bfloat16)


def per_device(acts, cotangents, w_gate, w_up, w_down, unit_rank):
    full_acts, full_cot = (
        lax.all_gather(acts, "mp", axis=1, tiled=True),
        lax.all_gather(cotangents, "mp", axis=2, tiled=True),
    )
    full_gate, full_up = (
        lax.all_gather(w_gate, "dp", axis=0, tiled=True),
        lax.all_gather(w_up, "dp", axis=0, tiled=True),
    )
    gate_proj = jnp.dot(full_acts, full_gate, preferred_element_type=jnp.float32)
    up_proj = jnp.dot(full_acts, full_up, preferred_element_type=jnp.float32)
    activated, slope = gelu_parts(gate_proj)
    hidden = (activated * up_proj).astype(jnp.bfloat16)
    suffix = suffix_sums(full_cot)
    unit_count = unit_rank.shape[0]
    token_count = full_acts.shape[0]
    band_index = (
        (unit_rank >= FF // 8).astype(jnp.int32)
        + (unit_rank >= FF // 4).astype(jnp.int32)
        + (unit_rank >= FF // 2).astype(jnp.int32)
    )
    zero_hidden = jnp.zeros((token_count, unit_count), jnp.float32)
    in_band = band_index[None, :] == jnp.arange(4, dtype=jnp.int32)[:, None]
    band_float = in_band.astype(jnp.float32)
    band_half = in_band.astype(jnp.bfloat16)
    running = zero_hidden
    weights_part = lax.all_gather(w_down, "dp", axis=1, tiled=True)
    for add_branch in range(4):
        running = running + contract_last(suffix[add_branch], weights_part) * band_float[add_branch]
    partial_down = contract_first(hidden * band_half[0], suffix[0])
    for branch in range(1, 4):
        partial_down = partial_down + contract_first(hidden * band_half[branch], suffix[branch])
    grad_gate_hidden = (running * up_proj * slope).astype(jnp.bfloat16)
    grad_up_hidden = (running * activated).astype(jnp.bfloat16)
    grad_down = lax.psum_scatter(
        partial_down.astype(jnp.bfloat16), "dp", scatter_dimension=1, tiled=True
    )
    partial_acts = contract_last(grad_gate_hidden, full_gate) + contract_last(
        grad_up_hidden, full_up
    )
    grad_acts = lax.psum_scatter(
        partial_acts.astype(jnp.bfloat16), "mp", scatter_dimension=1, tiled=True
    )
    grad_acts, grad_down = (grad_acts, grad_down)
    token_cols = lax.all_to_all(full_acts, "dp", split_axis=1, concat_axis=0, tiled=True)
    gate_total = contract_first(
        token_cols, lax.all_gather(grad_gate_hidden, "dp", axis=0, tiled=True)
    )
    up_total = contract_first(token_cols, lax.all_gather(grad_up_hidden, "dp", axis=0, tiled=True))
    grad_gate = gate_total.astype(jnp.bfloat16)
    grad_up = up_total.astype(jnp.bfloat16)
    return (grad_acts, grad_gate, grad_up, grad_down)


def solution(mesh):
    return jax.shard_map(
        per_device,
        mesh=mesh,
        in_specs=(
            P("dp", "mp"),
            P(None, "dp", "mp"),
            P("dp", "mp"),
            P("dp", "mp"),
            P("mp", "dp"),
            P("mp"),
        ),
        out_specs=(P("dp", "mp"), P("dp", "mp"), P("dp", "mp"), P("mp", "dp")),
        check_vma=False,
    )
```

profile of v0, /device:TPU:6, one launch (start us, length us, event | category | flops | bytes accessed | tf_op | source)
XLA Modules:
  0.0 757.5 jit_solution(14954325181963452215)
XLA Ops:
  10.0 144.2 %all-gather = bf16[32,84,128]{2,1,0:T(8,128)(2,1)S(1)} all-gather(bf16[1,84,128]{2,1,0:T(8,128)(2,1)} %bitcast.58), channel_id=1, replica_groups=mesh['dp'=16,'mp'=32] {'mp'}, dimensions={0}, use_global_device_ids=true | all-gather | bytes 709632 | tf_op jit(solution)/shard_map/all_gather | solution.py:44
  154.9 1.0 reshape.13
  155.9 3.4 fusion.42
  159.3 104.8 %all-gather.8.cloned.1.call-done = bf16[4,128,2688]{1,0,2:T(4,128)(2,1)} async-done(((bf16[4,128,84]{1,0,2:T(4,128)(2,1)}), bf16[4,128,2688]{1,0,2:T(4,128)(2,1)}) %all-gather.8.cloned.1.call-update) | async-done | bytes 2752528 | tf_op jit(solution)/shard_map/all_gather | solution.py:45
  264.0 10.6 %fusion.41 = (bf16[1,128,2688]{1,0,2:T(2,128)(2,1)S(1)}, bf16[1,128,2688]{1,0,2:T(2,128)(2,1)}, bf16[1,128,2688]{1,0,2:T(2,128)(2,1)}, bf16[1,128,2688]{1,0,2:T(2,128)(2,1)S(1)}) fusion(bf16[4,128,2688]{1,0,2:T(4,128)(2,1)} %all-gather.8.cloned.1.call-done), kind=kLoop, calls=%fused_computation.65 | loop fusion | bytes 5505024 | tf_op jit(solution)/shard_map/slice | solution.py:38
  274.6 1.7 copy.20
  276.3 3.4 copy.19
  279.7 3.4 copy.18
  283.1 2.9 copy.17
  286.0 1.4 fusion.12
  287.5 70.9 %all-gather.10.cloned.1.call-done = bf16[336,2688]{0,1:T(8,128)(2,1)} async-done(((bf16[336,168]{0,1:T(8,128)(2,1)}), bf16[336,2688]{0,1:T(8,128)(2,1)}) %all-gather.10.cloned.1.call-update) | async-done | bytes 1806352 | tf_op jit(solution)/shard_map/all_gather | solution.py:68
  358.4 2.6 convolution_multiply_fusion.3
  361.0 0.9 fusion.6
  361.9 0.9 fusion.5
  362.9 0.9 fusion.4
  363.8 97.8 %all-gather.12.cloned.1.call-done = bf16[2688,336]{1,0:T(8,128)(2,1)} async-done(((bf16[168,336]{1,0:T(8,128)(2,1)}), bf16[2688,336]{1,0:T(8,128)(2,1)}) %all-gather.12.cloned.1.call-update) | async-done | bytes 1806352 | tf_op jit(solution)/shard_map/all_gather | solution.py:49
  461.7 3.4 multiply_convert_fusion
  465.9 0.8 fusion.31
  466.7 0.9 convolution_add_fusion.2
  467.6 0.8 convolution_add_fusion.1
  468.4 2.2 fusion.1
  470.6 9.7 %all-to-all-start = ((bf16[128,16,168]{0,2,1:T(8,128)(2,1)}), bf16[128,16,168]{0,2,1:T(8,128)(2,1)S(1)}, u32[]{:S(2)}, u32[]{:S(2)}) async-start(bf16[128,16,168]{0,2,1:T(8,128)(2,1)} %bitcast.7), calls=%async_computation | async-start | bytes 1376256 | tf_op jit(solution)/shard_map/all_to_all | solution.py:86
  481.1 0.9 copy-done.2
  482.7 145.2 %fusion = bf16[128,96]{0,1:T(8,128)(2,1)S(1)} fusion(bf16[128,2688]{0,1:T(8,128)(2,1)S(1)} %fusion.2), kind=kCustom, calls=%all-reduce-scatter | all-reduce-scatter fusion | flops 393217 | bytes 714752
  627.9 3.6 collective-permute-start.2
  631.4 25.9 %collective-permute-start.1 = (bf16[128,96]{0,1:T(8,128)(2,1)S(1)}, bf16[128,96]{0,1:T(8,128)(2,1)S(1)}, u32[]{:S(2)}, u32[]{:S(2)}) collective-permute-start(bf16[128,96]{0,1:T(8,128)(2,1)S(1)} %fusion), channel_id=1, source_target_pairs={{0,2},{1,3},{2,4},{3,5},{4,6},{5,7},{6,8},{7,9},{8,10},{9,11},{10,... | collective-permute-start | bytes 73736
  657.3 1.9 collective-permute-start
  659.3 1.3 collective-permute-start.3
  660.6 1.3 dynamic-slice.6
  664.5 2.7 fusion.7
  667.1 2.7 fusion.8
  669.8 80.8 %reduce-scatter.7.cloned.1.call-done = bf16[336,168]{0,1:T(8,128)(2,1)} async-done(((bf16[336,2688]{0,1:T(8,128)(2,1)}), bf16[336,168]{0,1:T(8,128)(2,1)}) %reduce-scatter.7.cloned.1.call-update) | async-done | bytes 112912
  (42 shorter events, 7.7 us)
Async XLA Ops:
  7.2 148.7 %all-gather.14.cloned.1.call-start = ((), (), s32[]{:S(2)}) async-start(), calls=%async_computation.5 | async-start | bytes 2193408 | tf_op jit(solution)/shard_map/all_gather | solution.py:48
  7.9 256.1 %all-gather.8.cloned.1.call-start = ((), (), s32[]{:S(2)}) async-start(), calls=%async_computation.2 | async-start | bytes 2838528 | tf_op jit(solution)/shard_map/all_gather | solution.py:45
  8.6 349.7 %all-gather.10.cloned.1.call-start = ((), (), s32[]{:S(2)}) async-start(), calls=%async_computation.3 | async-start | bytes 2193408 | tf_op jit(solution)/shard_map/all_gather | solution.py:68
  9.4 452.3 %all-gather.12.cloned.1.call-start = ((), (), s32[]{:S(2)}) async-start(), calls=%async_computation.4 | async-start | bytes 2193408 | tf_op jit(solution)/shard_map/all_gather | solution.py:49
  10.0 654.5 %all-gather.16.cloned.1.call-start = ((), (), s32[]{:S(2)}) async-start(), calls=%async_computation.6 | async-start | bytes 1462272 | tf_op jit(solution)/shard_map/all_gather | solution.py:88
  358.4 2.6 copy-start
  362.9 98.8 %copy-start.5 = (f32[128,336]{0,1:T(8,128)S(1)}, f32[128,336]{0,1:T(8,128)}, u32[]{:S(2)}) copy-start(f32[128,336]{0,1:T(8,128)} %fusion.42) | copy-start | bytes 516100
  465.1 202.1 %all-gather.18.cloned.1.call-start = ((), (), s32[]{:S(2)}) async-start(), calls=%async_computation.7 | async-start | bytes 1462272 | tf_op jit(solution)/shard_map/all_gather | solution.py:90
  465.6 285.0 %reduce-scatter.7.cloned.1.call-start = ((), (), s32[]{:S(2)}) async-start(), calls=%async_computation.8 | async-start | bytes 2193408
  470.6 9.8 %copy-start.1 = (bf16[2688,336]{1,0:T(8,128)(2,1)S(1)}, bf16[2688,336]{1,0:T(8,128)(2,1)}, u32[]{:S(2)}) copy-start(bf16[2688,336]{1,0:T(8,128)(2,1)} %all-gather.14.cloned.1.call-done) | copy-start | bytes 5419012
  470.6 9.8 %copy-start.4 = (bf16[128,336]{0,1:T(8,128)(2,1)S(1)}, bf16[128,336]{0,1:T(8,128)(2,1)}, u32[]{:S(2)}) copy-start(bf16[128,336]{0,1:T(8,128)(2,1)} %get-tuple-element.17) | copy-start | bytes 258052
  470.6 193.8 %all-to-all-start = ((bf16[128,16,168]{0,2,1:T(8,128)(2,1)}), bf16[128,16,168]{0,2,1:T(8,128)(2,1)S(1)}, u32[]{:S(2)}, u32[]{:S(2)}) async-start(bf16[128,16,168]{0,2,1:T(8,128)(2,1)} %bitcast.7), calls=%async_computation | async-start | bytes 1376256 | tf_op jit(solution)/shard_map/all_to_all | solution.py:86
  480.4 1.6 copy-start.2
  480.4 1.6 copy-start.3
  627.9 34.7 %collective-permute-start.2 = (bf16[128,96]{0,1:T(8,128)(2,1)S(1)}, bf16[128,96]{0,1:T(8,128)(2,1)S(1)}, u32[]{:S(2)}, u32[]{:S(2)}) collective-permute-start(bf16[128,96]{0,1:T(8,128)(2,1)S(1)} %fusion), channel_id=1, source_target_pairs={{0,3},{1,4},{2,5},{3,6},{4,7},{5,8},{6,9},{7,10},{8,11},{9,12},{10... | collective-permute-start | bytes 73736
  631.4 31.1 %collective-permute-start.1 = (bf16[128,96]{0,1:T(8,128)(2,1)S(1)}, bf16[128,96]{0,1:T(8,128)(2,1)S(1)}, u32[]{:S(2)}, u32[]{:S(2)}) collective-permute-start(bf16[128,96]{0,1:T(8,128)(2,1)S(1)} %fusion), channel_id=1, source_target_pairs={{0,2},{1,3},{2,4},{3,5},{4,6},{5,7},{6,8},{7,9},{8,10},{9,11},{10,... | collective-permute-start | bytes 73736
  657.3 5.7 collective-permute-start
  659.3 3.2 collective-permute-start.3
Sparse Core Ops, SparseCore 0:
  10.1 107.3 all-gather.13
  121.8 142.2 all-gather.7
  266.1 92.2 all-gather.9
  360.3 101.3 all-gather.11
  465.2 90.6 all-gather.15
  557.7 78.8 all-gather.17
  640.0 110.5 reduce-scatter.6
where the time goes:
time: 758 us; the launch traced here: 757 us
  waiting for transfers between devices  358 us (47%)
  blocking collectives  289 us (38%)
  starting transfers between devices  42.8 us (6%)
  local copies, waits for them, and re-layouts  26.6 us (4%)
  matrix products  23.5 us (3%)
  between operations  15 us (2%)
    unnamed x1, blocking collectives  145 us
    all_gather x1, blocking collectives, per_device(): lax.all_gather(acts, 'mp', axis=1, tiled=True)  144 us
    all_gather x1, waiting for transfers between devices, per_device(): lax.all_gather(cotangents, 'mp', axis=2, tiled=True)  105 us
    all_gather x1, waiting for transfers between devices, per_device(): lax.all_gather(w_up, 'dp', axis=0, tiled=True)  97.8 us
    unnamed x12, waiting for transfers between devices  84.5 us
    all_gather x1, waiting for transfers between devices, per_device(): weights_part = lax.all_gather(w_down, 'dp', axis=1, tiled=True)  70.9 us
    unnamed x5, starting transfers between devices  32.9 us
    unnamed x21, local copies, waits for them, and re-layouts  15.9 us
  transfers between devices with their start and end apart: 12, of which 5 were waited for; matrix products, arithmetic and copies ran while one was open for 26% of the time, Pallas kernels for 0%

commit v1 on v0

v1 whole, which is shorter than its diff:
```python
import jax
import jax.numpy as jnp
from jax import lax
from jax.sharding import Mesh, PartitionSpec as P

FF = 10752
ZL = 8
GELU_SCALE = 0.7978845608028654


def gelu_parts(values):
    tanh_arg = GELU_SCALE * (values + 0.044715 * values * values * values)
    tanh_val = jnp.tanh(tanh_arg)
    activated = 0.5 * values * (1.0 + tanh_val)
    slope = 0.5 * (1.0 + tanh_val) + 0.5 * values * (1.0 - tanh_val * tanh_val) * GELU_SCALE * (
        1.0 + 3.0 * 0.044715 * values * values
    )
    return activated, slope


def dot(left, right, left_dim, right_dim):
    return lax.dot_general(
        left, right, (((left_dim,), (right_dim,)), ((), ())), preferred_element_type=jnp.float32
    )


def suffix_sums(cot_all):
    third = cot_all[3].astype(jnp.float32)
    second = cot_all[2].astype(jnp.float32) + third
    first = cot_all[1].astype(jnp.float32) + second
    zeroth = cot_all[0].astype(jnp.float32) + first
    return [part.astype(jnp.bfloat16) for part in (zeroth, first, second, third)]


def in_order(mine, other, index, axis):
    first = jnp.where(index == 0, mine, other)
    second = jnp.where(index == 0, other, mine)
    return jnp.stack([first, second], axis)


def swap(values, axis_name):
    return lax.ppermute(values, axis_name, [(0, 1), (1, 0)])


def line_gather(shard, place):
    from_left, from_right = [], []
    right = left = shard
    for step in range(ZL - 1):
        right = lax.ppermute(right, "zl", [(i, i + 1) for i in range(step, ZL - 1)])
        left = lax.ppermute(left, "zl", [(i, i - 1) for i in range(1, ZL - step)])
        from_left.append(right)
        from_right.append(left)
    slots = jnp.stack(from_left[::-1] + [shard] + from_right)
    return lax.dynamic_slice_in_dim(slots, ZL - 1 - place, ZL, 0)


def line_scatter(parts, place):
    right = left = None
    for step in range(ZL - 1):
        to_right = parts[jnp.clip(place + ZL - 1 - step, 0, ZL - 1)]
        to_left = parts[jnp.clip(place - ZL + 1 + step, 0, ZL - 1)]
        if step:
            to_right = to_right + right.astype(jnp.float32)
            to_left = to_left + left.astype(jnp.float32)
        right = lax.ppermute(
            to_right.astype(jnp.bfloat16), "zl", [(i, i + 1) for i in range(step + 1)]
        )
        left = lax.ppermute(
            to_left.astype(jnp.bfloat16), "zl", [(i, i - 1) for i in range(ZL - 1 - step, ZL)]
        )
    return parts[place] + right.astype(jnp.float32) + left.astype(jnp.float32)


def per_device(acts, cotangents, w_gate, w_up, w_down, unit_rank):
    place = lax.axis_index("zl")
    core = lax.axis_index("co")
    half = lax.axis_index("zh")
    tokens, features = acts.shape
    units = unit_rank.shape[0]
    rows = w_gate.shape[0]

    weights = jnp.concatenate([w_gate, w_up, w_down.T], 1)
    mine = line_gather(weights, place)
    weights = in_order(mine, swap(mine, "co"), core, 1).reshape(2 * ZL * rows, 3 * units)

    local = jnp.concatenate([acts.T] + [part.T for part in suffix_sums(cotangents)], 1)
    far = swap(local, "zh")

    def spread(values):
        copies = jnp.broadcast_to(values[None], (16,) + values.shape)
        return lax.all_to_all(copies, ("y", "x"), 0, 0).reshape((4, 4) + values.shape)

    near, far = spread(local), spread(far)
    inputs = in_order(near, far, half, 1).reshape(32 * features, 5 * tokens)

    products = dot(inputs, weights, 0, 0)
    gate_proj = products[:tokens, :units]
    up_proj = products[:tokens, units : 2 * units]
    activated, slope = gelu_parts(gate_proj)
    hidden = (activated * up_proj).astype(jnp.bfloat16)
    band = (
        (unit_rank >= FF // 8).astype(jnp.int32)
        + (unit_rank >= FF // 4).astype(jnp.int32)
        + (unit_rank >= FF // 2).astype(jnp.int32)
    )[None, :]
    grad_hidden = jnp.zeros((tokens, units), jnp.float32)
    masked = []
    for branch in range(4):
        rows_of = slice((branch + 1) * tokens, (branch + 2) * tokens)
        grad_hidden = jnp.where(band == branch, products[rows_of, 2 * units :], grad_hidden)
        masked.append(jnp.where(band == branch, hidden, jnp.zeros_like(hidden)))
    masked = jnp.concatenate(masked, 0)
    grad_gate_hidden = (grad_hidden * up_proj * slope).astype(jnp.bfloat16)
    grad_up_hidden = (grad_hidden * activated).astype(jnp.bfloat16)
    both = jnp.concatenate([grad_gate_hidden, grad_up_hidden], 1)

    partial_acts = dot(weights[:, : 2 * units], both, 1, 1).astype(jnp.bfloat16)
    partial_acts = partial_acts.reshape(4, 2, 4, features, tokens).transpose(0, 2, 1, 3, 4)
    partial_acts = partial_acts.reshape(16, 2, features, tokens)
    shares = lax.all_to_all(partial_acts, ("y", "x"), 0, 0)
    shares = jnp.sum(shares.astype(jnp.float32), 0)
    away = swap(shares[1 - half].astype(jnp.bfloat16), "zh")
    grad_acts = (shares[half] + away.astype(jnp.float32)).astype(jnp.bfloat16).T

    wide = jnp.concatenate(
        [
            jnp.pad(both, ((0, 0), (0, units))),
            jnp.pad(masked, ((0, 0), (2 * units, 0))),
        ],
        0,
    )
    partial = dot(inputs, wide, 1, 0).astype(jnp.bfloat16).reshape(ZL, 2, rows, 3 * units)
    kept = jnp.where(core == 0, partial[:, 0], partial[:, 1])
    given = jnp.where(core == 0, partial[:, 1], partial[:, 0])
    parts = kept.astype(jnp.float32) + swap(given, "co").astype(jnp.float32)
    grads = line_scatter(parts, place).astype(jnp.bfloat16)
    return (
        grad_acts,
        grads[:, :units],
        grads[:, units : 2 * units],
        grads[:, 2 * units :].T,
    )


def solution(mesh):
    fine = Mesh(mesh.devices.reshape(ZL, 2, 4, 2, 4), ("zl", "co", "y", "zh", "x"))
    dp, mp = ("zl", "co"), ("y", "zh", "x")
    return jax.shard_map(
        per_device,
        mesh=fine,
        in_specs=(P(dp, mp), P(None, dp, mp), P(dp, mp), P(dp, mp), P(mp, dp), P(mp)),
        out_specs=(P(dp, mp), P(dp, mp), P(dp, mp), P(mp, dp)),
        check_vma=False,
    )
```

time: 758 us -> 340 us (0.45)
  the two profiles are of different devices: /device:TPU:6 before, /device:TPU:98 now
where the time goes in v1:
time: 340 us; the launch traced here: 337 us
  waiting for transfers between devices  142 us (42%)
  starting transfers between devices  110 us (32%)
  other arithmetic  34.4 us (10%)
  local copies, waits for them, and re-layouts  33.8 us (10%)
  matrix products  14.8 us (4%)
    ppermute x7, waiting for transfers between devices, line_scatter(): lax.ppermute(to_right.astype(jnp.bfloat16), 'zl', [(i, i + 1) for i in ra...  54.5 us
    ppermute x7, waiting for transfers between devices, line_scatter(): lax.ppermute(to_left.astype(jnp.bfloat16), 'zl', [(i, i - 1) for i in ran...  31.9 us
    ppermute x7, starting transfers between devices, line_gather(): right = lax.ppermute(right, 'zl', [(i, i + 1) for i in range(step, ZL - 1)])  25.3 us
    all_to_all x2, waiting for transfers between devices, spread(): lax.all_to_all(copies, ('y', 'x'), 0, 0).reshape((4, 4) + values.shape)  23.8 us
    ppermute x4, starting transfers between devices, swap(): return lax.ppermute(values, axis_name, [(0, 1), (1, 0)])  23.5 us
    ppermute x7, starting transfers between devices, line_scatter(): lax.ppermute(to_right.astype(jnp.bfloat16), 'zl', [(i, i + 1) for i in ra...  18.7 us
    ppermute x7, waiting for transfers between devices, line_gather(): right = lax.ppermute(right, 'zl', [(i, i + 1) for i in range(step, ZL - 1)])  16.2 us
    dot_general x3, matrix products, dot(): lax.dot_general(left, right, (((left_dim,), (right_dim,)), ((), ())), pre...  14.8 us
  transfers between devices with their start and end apart: 35, of which 17 were waited for; matrix products, arithmetic and copies ran while one was open for 10% of the time, Pallas kernels for 0%

profile of v1, /device:TPU:98, one launch (start us, length us, event | category | flops | bytes accessed | tf_op | source)
XLA Modules:
  0.0 337.5 jit_solution(7749760644069152563)
XLA Ops:
  1.8 5.0 %collective-permute-start = (bf16[168,1008]{1,0:T(8,128)(2,1)S(1)}, bf16[168,1008]{1,0:T(8,128)(2,1)S(1)}, u32[]{:S(2)}, u32[]{:S(2)}) collective-permute-start(bf16[168,1008]{1,0:T(8,128)(2,1)S(1)} %pad_maximum_fusion.2), channel_id=1, source_target_pairs={{0,64},{64,128},{128,192},{192,256},{256,320},{320,384},{384,448},... | collective-permute-start | bytes 1016072 | tf_op jit(solution)/shard_map/ppermute | solution.py:49
  8.8 5.4 %collective-permute-done = bf16[168,1008]{1,0:T(8,128)(2,1)S(1)} collective-permute-done((bf16[168,1008]{1,0:T(8,128)(2,1)S(1)}, bf16[168,1008]{1,0:T(8,128)(2,1)S(1)}, u32[]{:S(2)}, u32[]{:S(2)}) %collective-permute-start) | collective-permute-done | bytes 338720 | tf_op jit(solution)/shard_map/ppermute | solution.py:49
  14.2 5.6 %collective-permute-start.1 = (bf16[168,1008]{1,0:T(8,128)(2,1)S(1)}, bf16[168,1008]{1,0:T(8,128)(2,1)S(1)}, u32[]{:S(2)}, u32[]{:S(2)}) collective-permute-start(bf16[168,1008]{1,0:T(8,128)(2,1)S(1)} %collective-permute-done), channel_id=1, source_target_pairs={{64,128},{128,192},{192,256},{256,320},{320,384},{384,448},{65,129... | collective-permute-start | bytes 1016072 | tf_op jit(solution)/shard_map/ppermute | solution.py:49
  21.7 4.5 %collective-permute-done.1 = bf16[168,1008]{1,0:T(8,128)(2,1)S(1)} collective-permute-done((bf16[168,1008]{1,0:T(8,128)(2,1)S(1)}, bf16[168,1008]{1,0:T(8,128)(2,1)S(1)}, u32[]{:S(2)}, u32[]{:S(2)}) %collective-permute-start.1) | collective-permute-done | bytes 338720 | tf_op jit(solution)/shard_map/ppermute | solution.py:49
  26.2 5.6 %collective-permute-start.2 = (bf16[168,1008]{1,0:T(8,128)(2,1)S(1)}, bf16[168,1008]{1,0:T(8,128)(2,1)S(1)}, u32[]{:S(2)}, u32[]{:S(2)}) collective-permute-start(bf16[168,1008]{1,0:T(8,128)(2,1)S(1)} %collective-permute-done.1), channel_id=1, source_target_pairs={{128,192},{192,256},{256,320},{320,384},{384,448},{129,193},{193,2... | collective-permute-start | bytes 1016072 | tf_op jit(solution)/shard_map/ppermute | solution.py:49
  33.7 3.6 %collective-permute-done.2 = bf16[168,1008]{1,0:T(8,128)(2,1)S(1)} collective-permute-done((bf16[168,1008]{1,0:T(8,128)(2,1)S(1)}, bf16[168,1008]{1,0:T(8,128)(2,1)S(1)}, u32[]{:S(2)}, u32[]{:S(2)}) %collective-permute-start.2) | collective-permute-done | bytes 338720 | tf_op jit(solution)/shard_map/ppermute | solution.py:49
  37.3 5.6 %collective-permute-start.3 = (bf16[168,1008]{1,0:T(8,128)(2,1)S(1)}, bf16[168,1008]{1,0:T(8,128)(2,1)S(1)}, u32[]{:S(2)}, u32[]{:S(2)}) collective-permute-start(bf16[168,1008]{1,0:T(8,128)(2,1)S(1)} %collective-permute-done.2), channel_id=1, source_target_pairs={{192,256},{256,320},{320,384},{384,448},{193,257},{257,321},{321,3... | collective-permute-start | bytes 1016072 | tf_op jit(solution)/shard_map/ppermute | solution.py:49
  63.6 7.5 %all-to-all-start = ((bf16[16,84,640]{2,1,0:T(8,128)(2,1)}), bf16[16,84,640]{2,1,0:T(8,128)(2,1)S(1)}, u32[]{:S(2)}, u32[]{:S(2)}) async-start(bf16[16,84,640]{2,1,0:T(8,128)(2,1)} %broadcast_in_dim.55), calls=%async_computation | async-start | bytes 3604480 | tf_op jit(solution)/shard_map/all_to_all | solution.py:91
  84.4 10.9 %collective-permute-start.15 = (bf16[84,640]{1,0:T(8,128)(2,1)S(1)}, bf16[84,640]{1,0:T(8,128)(2,1)S(1)}, u32[]{:S(2)}, u32[]{:S(2)}) collective-permute-start(bf16[84,640]{1,0:T(8,128)(2,1)S(1)} %constant_dynamic-update-slice_fusion), channel_id=1, source_target_pairs={{0,4},{4,0},{1,5},{5,1},{2,6},{6,2},{3,7},{7,3},{8,12},{12,8},{9,1... | collective-permute-start | bytes 322568 | tf_op jit(solution)/shard_map/ppermute | solution.py:42
  95.3 5.3 %collective-permute-done.15 = bf16[84,640]{1,0:T(8,128)(2,1)S(1)} collective-permute-done((bf16[84,640]{1,0:T(8,128)(2,1)S(1)}, bf16[84,640]{1,0:T(8,128)(2,1)S(1)}, u32[]{:S(2)}, u32[]{:S(2)}) %collective-permute-start.15) | collective-permute-done | bytes 107552 | tf_op jit(solution)/shard_map/ppermute | solution.py:42
  102.1 7.2 %all-to-all-start.1 = ((bf16[16,84,640]{2,1,0:T(8,128)(2,1)}), bf16[16,84,640]{2,1,0:T(8,128)(2,1)}, u32[]{:S(2)}, u32[]{:S(2)}) async-start(bf16[16,84,640]{2,1,0:T(8,128)(2,1)} %broadcast_in_dim.56), calls=%async_computation.1 | async-start | bytes 3604480 | tf_op jit(solution)/shard_map/all_to_all | solution.py:91
  109.3 23.8 %all-to-all-done.1 = bf16[16,84,640]{2,1,0:T(8,128)(2,1)} async-done(((bf16[16,84,640]{2,1,0:T(8,128)(2,1)}), bf16[16,84,640]{2,1,0:T(8,128)(2,1)}, u32[]{:S(2)}, u32[]{:S(2)}) %all-to-all-start.1) | async-done | bytes 1720352 | tf_op jit(solution)/shard_map/all_to_all | solution.py:91
  137.2 3.8 %reshape.89 = bf16[2688,640]{1,0:T(8,128)(2,1)S(1)} reshape(bf16[4,2,4,84,640]{4,3,2,1,0:T(8,128)(2,1)} %pad_maximum_fusion.1) | data formatting | bytes 6881280 | tf_op jit(solution)/shard_map/reshape | solution.py:94
  145.4 4.9 %fusion.60 = f32[640,1008]{0,1:T(8,128)S(1)} fusion(bf16[2688,640]{1,0:T(8,128)(2,1)S(1)} %reshape.89, bf16[2688,1008]{1,0:T(8,128)(2,1)S(1)} %bitcast.182), kind=kOutput, calls=%fused_computation.133 | convolution fusion | flops 3468165120 | bytes 11440128 | tf_op jit(solution)/shard_map/dot_general | solution.py:22
  151.4 6.4 %convolution_convert_fusion = bf16[2688,1008]{0,1:T(8,128)(2,1)} fusion(bf16[2688,640]{1,0:T(8,128)(2,1)S(1)} %reshape.89, bf16[128,672]{0,1:T(8,128)(2,1)S(1)} %pad_maximum_fusion.3, bf16[512,1008]{0,1:T(8,128)(2,1)S(1)} %fusion.19), kind=kOutput, calls=%fused_computation | convolution fusion | flops 3474745344 | bytes 10063872 | tf_op jit(solution)/shard_map/dot_general | solution.py:22
  157.9 8.2 %copy.69 = bf16[2688,1008]{1,0:T(8,128)(2,1)} copy(bf16[2688,1008]{0,1:T(8,128)(2,1)} %convolution_convert_fusion) | data formatting | bytes 10838016 | tf_op jit(solution)/shard_map/convert_element_type | solution.py:132
  166.1 4.5 %fusion.5 = bf16[8,168,1008]{2,1,0:T(8,128)(2,1)} fusion(pred[]{:T(512)S(6)} %eq.30, bf16[8,2,168,1008]{3,2,1,0:T(8,128)(2,1)} %bitcast.178), kind=kLoop, calls=%fused_computation.8 | loop fusion | flops 1354752 | bytes 8128513 | tf_op jit(solution)/shard_map/jit(_where)/select_n | solution.py:134
  172.7 5.0 %collective-permute-done.17 = bf16[8,168,1008]{2,1,0:T(8,128)(2,1)S(1)} collective-permute-done((bf16[8,168,1008]{2,1,0:T(8,128)(2,1)}, bf16[8,168,1008]{2,1,0:T(8,128)(2,1)S(1)}, u32[]{:S(2)}, u32[]{:S(2)}) %collective-permute-start.17) | collective-permute-done | bytes 2709536 | tf_op jit(solution)/shard_map/ppermute | solution.py:42
  177.8 4.5 %convert_add_fusion = f32[8,168,1008]{2,1,0:T(8,128)S(1)} fusion(bf16[8,168,1008]{2,1,0:T(8,128)(2,1)S(1)} %collective-permute-done.17, pred[]{:T(512)S(6)} %eq.30, bf16[8,2,168,1008]{3,2,1,0:T(8,128)(2,1)} %bitcast.179), kind=kLoop, calls=%fused_computation.2 | loop fusion | flops 5419008 | bytes 13547521 | tf_op jit(solution)/shard_map/add | solution.py:135
  190.1 35.6 %collective-permute-done.20 = bf16[168,1008]{1,0:T(8,128)(2,1)S(1)} collective-permute-done((bf16[168,1008]{1,0:T(8,128)(2,1)S(1)}, bf16[168,1008]{1,0:T(8,128)(2,1)S(1)}, u32[]{:S(2)}, u32[]{:S(2)}) %collective-permute-start.20) | collective-permute-done | bytes 338720 | tf_op jit(solution)/shard_map/ppermute | solution.py:65
  228.8 8.0 %collective-permute-done.21 = bf16[168,1008]{1,0:T(8,128)(2,1)S(1)} collective-permute-done((bf16[168,1008]{1,0:T(8,128)(2,1)S(1)}, bf16[168,1008]{1,0:T(8,128)(2,1)S(1)}, u32[]{:S(2)}, u32[]{:S(2)}) %collective-permute-start.21) | collective-permute-done | bytes 338720 | tf_op jit(solution)/shard_map/ppermute | solution.py:65
  238.0 3.4 %collective-permute-start.22 = (bf16[168,1008]{1,0:T(8,128)(2,1)S(1)}, bf16[168,1008]{1,0:T(8,128)(2,1)S(1)}, u32[]{:S(2)}, u32[]{:S(2)}) collective-permute-start(bf16[168,1008]{1,0:T(8,128)(2,1)S(1)} %fusion.29), channel_id=1, source_target_pairs={{0,64},{64,128},{128,192},{192,256},{256,320},{1,65},{65,129},{129... | collective-permute-start | bytes 1016072 | tf_op jit(solution)/shard_map/ppermute | solution.py:65
  242.1 5.0 %collective-permute-done.22 = bf16[168,1008]{1,0:T(8,128)(2,1)S(1)} collective-permute-done((bf16[168,1008]{1,0:T(8,128)(2,1)S(1)}, bf16[168,1008]{1,0:T(8,128)(2,1)S(1)}, u32[]{:S(2)}, u32[]{:S(2)}) %collective-permute-start.22) | collective-permute-done | bytes 338720 | tf_op jit(solution)/shard_map/ppermute | solution.py:65
  248.3 4.7 %collective-permute-start.23 = (bf16[168,1008]{1,0:T(8,128)(2,1)S(1)}, bf16[168,1008]{1,0:T(8,128)(2,1)S(1)}, u32[]{:S(2)}, u32[]{:S(2)}) collective-permute-start(bf16[168,1008]{1,0:T(8,128)(2,1)S(1)} %fusion.30), channel_id=1, source_target_pairs={{0,64},{64,128},{128,192},{192,256},{256,320},{320,384},{1,65},{65... | collective-permute-start | bytes 1016072 | tf_op jit(solution)/shard_map/ppermute | solution.py:65
  253.1 4.7 %collective-permute-done.23 = bf16[168,1008]{1,0:T(8,128)(2,1)S(1)} collective-permute-done((bf16[168,1008]{1,0:T(8,128)(2,1)S(1)}, bf16[168,1008]{1,0:T(8,128)(2,1)S(1)}, u32[]{:S(2)}, u32[]{:S(2)}) %collective-permute-start.23) | collective-permute-done | bytes 338720 | tf_op jit(solution)/shard_map/ppermute | solution.py:65
  264.4 3.4 %fusion.2 = bf16[2688,128]{1,0:T(8,128)(2,1)S(1)} fusion(bf16[2688,1008]{1,0:T(8,128)(2,1)} %bitcast.183, bf16[128,336]{0,1:T(8,128)(2,1)S(1)} %multiply_convert_fusion.1, bf16[128,336]{0,1:T(8,128)(2,1)S(1)} %copy-done.15), kind=kOutput, calls=%fused_computation.6 | convolution fusion | flops 463110144 | bytes 4988928 | tf_op jit(solution)/shard_map/dot_general | solution.py:22
  269.8 7.2 %all-to-all-start.2 = ((bf16[16,2,84,128]{3,1,2,0:T(2,128)(2,1)}), bf16[16,2,84,128]{3,1,2,0:T(2,128)(2,1)S(1)}, u32[]{:S(2)}, u32[]{:S(2)}) async-start(bf16[16,2,84,128]{3,1,2,0:T(2,128)(2,1)} %copy.68), calls=%async_computation.2 | async-start | bytes 1376256 | tf_op jit(solution)/shard_map/all_to_all | solution.py:120
  277.1 11.2 %collective-permute-done.28 = bf16[168,1008]{1,0:T(8,128)(2,1)S(1)} collective-permute-done((bf16[168,1008]{1,0:T(8,128)(2,1)S(1)}, bf16[168,1008]{1,0:T(8,128)(2,1)S(1)}, u32[]{:S(2)}, u32[]{:S(2)}) %collective-permute-start.28) | collective-permute-done | bytes 338720 | tf_op jit(solution)/shard_map/ppermute | solution.py:68
  291.4 14.2 %collective-permute-done.29 = bf16[168,1008]{1,0:T(8,128)(2,1)S(1)} collective-permute-done((bf16[168,1008]{1,0:T(8,128)(2,1)S(1)}, bf16[168,1008]{1,0:T(8,128)(2,1)S(1)}, u32[]{:S(2)}, u32[]{:S(2)}) %collective-permute-start.29) | collective-permute-done | bytes 338720 | tf_op jit(solution)/shard_map/ppermute | solution.py:68
  309.4 8.6 %collective-permute-start.16 = (bf16[84,128]{1,0:T(8,128)(2,1)S(1)}, bf16[84,128]{1,0:T(8,128)(2,1)S(1)}, u32[]{:S(2)}, u32[]{:S(2)}) collective-permute-start(bf16[84,128]{1,0:T(8,128)(2,1)S(1)} %bitcast.188), channel_id=1, source_target_pairs={{0,4},{4,0},{1,5},{5,1},{2,6},{6,2},{3,7},{7,3},{8,12},{12,8},{9,1... | collective-permute-start | bytes 64520 | tf_op jit(solution)/shard_map/ppermute | solution.py:42
  317.9 5.9 %collective-permute-start.24 = (bf16[168,1008]{1,0:T(8,128)(2,1)S(1)}, bf16[168,1008]{1,0:T(8,128)(2,1)S(1)}, u32[]{:S(2)}, u32[]{:S(2)}) collective-permute-start(bf16[168,1008]{1,0:T(8,128)(2,1)S(1)} %get-tuple-element.10), channel_id=1, source_target_pairs={{0,64},{64,128},{128,192},{192,256},{256,320},{320,384},{384,448},... | collective-permute-start | bytes 1016072 | tf_op jit(solution)/shard_map/ppermute | solution.py:65
  328.8 6.6 %collective-permute-done.31 = bf16[168,1008]{1,0:T(8,128)(2,1)S(1)} collective-permute-done((bf16[168,1008]{1,0:T(8,128)(2,1)S(1)}, bf16[168,1008]{1,0:T(8,128)(2,1)S(1)}, u32[]{:S(2)}, u32[]{:S(2)}) %collective-permute-start.31) | collective-permute-done | bytes 338720 | tf_op jit(solution)/shard_map/ppermute | solution.py:68
  (138 shorter events, 90.0 us)
Async XLA Ops:
  1.8 12.3 %collective-permute-start = (bf16[168,1008]{1,0:T(8,128)(2,1)S(1)}, bf16[168,1008]{1,0:T(8,128)(2,1)S(1)}, u32[]{:S(2)}, u32[]{:S(2)}) collective-permute-start(bf16[168,1008]{1,0:T(8,128)(2,1)S(1)} %pad_maximum_fusion.2), channel_id=1, source_target_pairs={{0,64},{64,128},{128,192},{192,256},{256,320},{320,384},{384,448},... | collective-permute-start | bytes 1016072 | tf_op jit(solution)/shard_map/ppermute | solution.py:49
  6.9 12.9 %collective-permute-start.7 = (bf16[168,1008]{1,0:T(8,128)(2,1)S(1)}, bf16[168,1008]{1,0:T(8,128)(2,1)S(1)}, u32[]{:S(2)}, u32[]{:S(2)}) collective-permute-start(bf16[168,1008]{1,0:T(8,128)(2,1)S(1)} %pad_maximum_fusion.2), channel_id=1, source_target_pairs={{64,0},{128,64},{192,128},{256,192},{320,256},{384,320},{448,384},... | collective-permute-start | bytes 1016072 | tf_op jit(solution)/shard_map/ppermute | solution.py:50
  14.2 12.0 %collective-permute-start.1 = (bf16[168,1008]{1,0:T(8,128)(2,1)S(1)}, bf16[168,1008]{1,0:T(8,128)(2,1)S(1)}, u32[]{:S(2)}, u32[]{:S(2)}) collective-permute-start(bf16[168,1008]{1,0:T(8,128)(2,1)S(1)} %collective-permute-done), channel_id=1, source_target_pairs={{64,128},{128,192},{192,256},{256,320},{320,384},{384,448},{65,129... | collective-permute-start | bytes 1016072 | tf_op jit(solution)/shard_map/ppermute | solution.py:49
  19.8 12.0 %collective-permute-start.8 = (bf16[168,1008]{1,0:T(8,128)(2,1)S(1)}, bf16[168,1008]{1,0:T(8,128)(2,1)S(1)}, u32[]{:S(2)}, u32[]{:S(2)}) collective-permute-start(bf16[168,1008]{1,0:T(8,128)(2,1)S(1)} %collective-permute-done.7), channel_id=1, source_target_pairs={{64,0},{128,64},{192,128},{256,192},{320,256},{384,320},{65,1},{12... | collective-permute-start | bytes 1016072 | tf_op jit(solution)/shard_map/ppermute | solution.py:50
  26.2 11.1 %collective-permute-start.2 = (bf16[168,1008]{1,0:T(8,128)(2,1)S(1)}, bf16[168,1008]{1,0:T(8,128)(2,1)S(1)}, u32[]{:S(2)}, u32[]{:S(2)}) collective-permute-start(bf16[168,1008]{1,0:T(8,128)(2,1)S(1)} %collective-permute-done.1), channel_id=1, source_target_pairs={{128,192},{192,256},{256,320},{320,384},{384,448},{129,193},{193,2... | collective-permute-start | bytes 1016072 | tf_op jit(solution)/shard_map/ppermute | solution.py:49
  31.8 11.1 %collective-permute-start.9 = (bf16[168,1008]{1,0:T(8,128)(2,1)S(1)}, bf16[168,1008]{1,0:T(8,128)(2,1)S(1)}, u32[]{:S(2)}, u32[]{:S(2)}) collective-permute-start(bf16[168,1008]{1,0:T(8,128)(2,1)S(1)} %collective-permute-done.8), channel_id=1, source_target_pairs={{64,0},{128,64},{192,128},{256,192},{320,256},{65,1},{129,65},{193... | collective-permute-start | bytes 1016072 | tf_op jit(solution)/shard_map/ppermute | solution.py:50
  37.3 10.3 %collective-permute-start.3 = (bf16[168,1008]{1,0:T(8,128)(2,1)S(1)}, bf16[168,1008]{1,0:T(8,128)(2,1)S(1)}, u32[]{:S(2)}, u32[]{:S(2)}) collective-permute-start(bf16[168,1008]{1,0:T(8,128)(2,1)S(1)} %collective-permute-done.2), channel_id=1, source_target_pairs={{192,256},{256,320},{320,384},{384,448},{193,257},{257,321},{321,3... | collective-permute-start | bytes 1016072 | tf_op jit(solution)/shard_map/ppermute | solution.py:49
  42.9 10.4 %collective-permute-start.10 = (bf16[168,1008]{1,0:T(8,128)(2,1)S(1)}, bf16[168,1008]{1,0:T(8,128)(2,1)S(1)}, u32[]{:S(2)}, u32[]{:S(2)}) collective-permute-start(bf16[168,1008]{1,0:T(8,128)(2,1)S(1)} %collective-permute-done.9), channel_id=1, source_target_pairs={{64,0},{128,64},{192,128},{256,192},{65,1},{129,65},{193,129},{257... | collective-permute-start | bytes 1016072 | tf_op jit(solution)/shard_map/ppermute | solution.py:50
  47.6 7.7 %collective-permute-start.4 = (bf16[168,1008]{1,0:T(8,128)(2,1)S(1)}, bf16[168,1008]{1,0:T(8,128)(2,1)S(1)}, u32[]{:S(2)}, u32[]{:S(2)}) collective-permute-start(bf16[168,1008]{1,0:T(8,128)(2,1)S(1)} %collective-permute-done.3), channel_id=1, source_target_pairs={{256,320},{320,384},{384,448},{257,321},{321,385},{385,449},{258,3... | collective-permute-start | bytes 1016072 | tf_op jit(solution)/shard_map/ppermute | solution.py:49
  53.3 6.0 %collective-permute-start.11 = (bf16[168,1008]{1,0:T(8,128)(2,1)S(1)}, bf16[168,1008]{1,0:T(8,128)(2,1)}, u32[]{:S(2)}, u32[]{:S(2)}) collective-permute-start(bf16[168,1008]{1,0:T(8,128)(2,1)S(1)} %collective-permute-done.10), channel_id=1, source_target_pairs={{64,0},{128,64},{192,128},{65,1},{129,65},{193,129},{66,2},{130,66... | collective-permute-start | bytes 1016072 | tf_op jit(solution)/shard_map/ppermute | solution.py:50
  55.3 5.4 %collective-permute-start.5 = (bf16[168,1008]{1,0:T(8,128)(2,1)S(1)}, bf16[168,1008]{1,0:T(8,128)(2,1)}, u32[]{:S(2)}, u32[]{:S(2)}) collective-permute-start(bf16[168,1008]{1,0:T(8,128)(2,1)S(1)} %collective-permute-done.4), channel_id=1, source_target_pairs={{320,384},{384,448},{321,385},{385,449},{322,386},{386,450},{323,3... | collective-permute-start | bytes 1016072 | tf_op jit(solution)/shard_map/ppermute | solution.py:49
  59.3 11.7 %collective-permute-start.12 = (bf16[168,1008]{1,0:T(8,128)(2,1)}, bf16[168,1008]{1,0:T(8,128)(2,1)}, u32[]{:S(2)}, u32[]{:S(2)}) collective-permute-start(bf16[168,1008]{1,0:T(8,128)(2,1)} %collective-permute-done.11), channel_id=1, source_target_pairs={{64,0},{128,64},{65,1},{129,65},{66,2},{130,66},{67,3},{131,67},{6... | collective-permute-start | bytes 1016072 | tf_op jit(solution)/shard_map/ppermute | solution.py:50
  60.7 11.2 %collective-permute-start.6 = (bf16[168,1008]{1,0:T(8,128)(2,1)}, bf16[168,1008]{1,0:T(8,128)(2,1)}, u32[]{:S(2)}, u32[]{:S(2)}) collective-permute-start(bf16[168,1008]{1,0:T(8,128)(2,1)} %collective-permute-done.5), channel_id=1, source_target_pairs={{384,448},{385,449},{386,450},{387,451},{388,452},{389,453},{390,4... | collective-permute-start | bytes 1016072 | tf_op jit(solution)/shard_map/ppermute | solution.py:49
  63.6 37.1 %all-to-all-start = ((bf16[16,84,640]{2,1,0:T(8,128)(2,1)}), bf16[16,84,640]{2,1,0:T(8,128)(2,1)S(1)}, u32[]{:S(2)}, u32[]{:S(2)}) async-start(bf16[16,84,640]{2,1,0:T(8,128)(2,1)} %broadcast_in_dim.55), calls=%async_computation | async-start | bytes 3604480 | tf_op jit(solution)/shard_map/all_to_all | solution.py:91
  71.1 9.3 %collective-permute-start.13 = (bf16[168,1008]{1,0:T(8,128)(2,1)}, bf16[168,1008]{1,0:T(8,128)(2,1)S(1)}, u32[]{:S(2)}, u32[]{:S(2)}) collective-permute-start(bf16[168,1008]{1,0:T(8,128)(2,1)} %collective-permute-done.12), channel_id=1, source_target_pairs={{64,0},{65,1},{66,2},{67,3},{68,4},{69,5},{70,6},{71,7},{72,8},{73... | collective-permute-start | bytes 1016072 | tf_op jit(solution)/shard_map/ppermute | solution.py:50
  82.5 58.5 %collective-permute-start.14 = (bf16[8,168,1008]{2,1,0:T(8,128)(2,1)}, bf16[8,168,1008]{2,1,0:T(8,128)(2,1)}, u32[]{:S(2)}, u32[]{:S(2)}) collective-permute-start(bf16[8,168,1008]{2,1,0:T(8,128)(2,1)} %constant_dynamic-slice_fusion.1), channel_id=1, source_target_pairs={{0,32},{32,0},{1,33},{33,1},{2,34},{34,2},{3,35},{35,3},{4,36},{36... | collective-permute-start | bytes 8128520 | tf_op jit(solution)/shard_map/ppermute | solution.py:42
  84.4 16.2 %collective-permute-start.15 = (bf16[84,640]{1,0:T(8,128)(2,1)S(1)}, bf16[84,640]{1,0:T(8,128)(2,1)S(1)}, u32[]{:S(2)}, u32[]{:S(2)}) collective-permute-start(bf16[84,640]{1,0:T(8,128)(2,1)S(1)} %constant_dynamic-update-slice_fusion), channel_id=1, source_target_pairs={{0,4},{4,0},{1,5},{5,1},{2,6},{6,2},{3,7},{7,3},{8,12},{12,8},{9,1... | collective-permute-start | bytes 322568 | tf_op jit(solution)/shard_map/ppermute | solution.py:42
  102.1 31.1 %all-to-all-start.1 = ((bf16[16,84,640]{2,1,0:T(8,128)(2,1)}), bf16[16,84,640]{2,1,0:T(8,128)(2,1)}, u32[]{:S(2)}, u32[]{:S(2)}) async-start(bf16[16,84,640]{2,1,0:T(8,128)(2,1)} %broadcast_in_dim.56), calls=%async_computation.1 | async-start | bytes 3604480 | tf_op jit(solution)/shard_map/all_to_all | solution.py:91
  170.6 7.2 %collective-permute-start.17 = (bf16[8,168,1008]{2,1,0:T(8,128)(2,1)}, bf16[8,168,1008]{2,1,0:T(8,128)(2,1)S(1)}, u32[]{:S(2)}, u32[]{:S(2)}) collective-permute-start(bf16[8,168,1008]{2,1,0:T(8,128)(2,1)} %fusion.5), channel_id=1, source_target_pairs={{0,32},{32,0},{1,33},{33,1},{2,34},{34,2},{3,35},{35,3},{4,36},{36... | collective-permute-start | bytes 8128520 | tf_op jit(solution)/shard_map/ppermute | solution.py:42
  188.6 37.1 %collective-permute-start.20 = (bf16[168,1008]{1,0:T(8,128)(2,1)S(1)}, bf16[168,1008]{1,0:T(8,128)(2,1)S(1)}, u32[]{:S(2)}, u32[]{:S(2)}) collective-permute-start(bf16[168,1008]{1,0:T(8,128)(2,1)S(1)} %fusion.27), channel_id=1, source_target_pairs={{0,64},{64,128},{128,192},{1,65},{65,129},{129,193},{2,66},{66,130... | collective-permute-start | bytes 1016072 | tf_op jit(solution)/shard_map/ppermute | solution.py:65
  226.9 9.9 %collective-permute-start.21 = (bf16[168,1008]{1,0:T(8,128)(2,1)S(1)}, bf16[168,1008]{1,0:T(8,128)(2,1)S(1)}, u32[]{:S(2)}, u32[]{:S(2)}) collective-permute-start(bf16[168,1008]{1,0:T(8,128)(2,1)S(1)} %fusion.28), channel_id=1, source_target_pairs={{0,64},{64,128},{128,192},{192,256},{1,65},{65,129},{129,193},{193... | collective-permute-start | bytes 1016072 | tf_op jit(solution)/shard_map/ppermute | solution.py:65
  238.0 9.1 %collective-permute-start.22 = (bf16[168,1008]{1,0:T(8,128)(2,1)S(1)}, bf16[168,1008]{1,0:T(8,128)(2,1)S(1)}, u32[]{:S(2)}, u32[]{:S(2)}) collective-permute-start(bf16[168,1008]{1,0:T(8,128)(2,1)S(1)} %fusion.29), channel_id=1, source_target_pairs={{0,64},{64,128},{128,192},{192,256},{256,320},{1,65},{65,129},{129... | collective-permute-start | bytes 1016072 | tf_op jit(solution)/shard_map/ppermute | solution.py:65
  241.4 11.7 %collective-permute-start.25 = (bf16[168,1008]{1,0:T(8,128)(2,1)S(1)}, bf16[168,1008]{1,0:T(8,128)(2,1)S(1)}, u32[]{:S(2)}, u32[]{:S(2)}) collective-permute-start(bf16[168,1008]{1,0:T(8,128)(2,1)S(1)} %get-tuple-element.13), channel_id=1, source_target_pairs={{448,384},{449,385},{450,386},{451,387},{452,388},{453,389},{454,3... | collective-permute-start | bytes 1016072 | tf_op jit(solution)/shard_map/ppermute | solution.py:68
  248.3 9.5 %collective-permute-start.23 = (bf16[168,1008]{1,0:T(8,128)(2,1)S(1)}, bf16[168,1008]{1,0:T(8,128)(2,1)S(1)}, u32[]{:S(2)}, u32[]{:S(2)}) collective-permute-start(bf16[168,1008]{1,0:T(8,128)(2,1)S(1)} %fusion.30), channel_id=1, source_target_pairs={{0,64},{64,128},{128,192},{192,256},{256,320},{320,384},{1,65},{65... | collective-permute-start | bytes 1016072 | tf_op jit(solution)/shard_map/ppermute | solution.py:65
  261.2 0.7 collective-permute-start.27
  263.1 25.1 %collective-permute-start.28 = (bf16[168,1008]{1,0:T(8,128)(2,1)S(1)}, bf16[168,1008]{1,0:T(8,128)(2,1)S(1)}, u32[]{:S(2)}, u32[]{:S(2)}) collective-permute-start(bf16[168,1008]{1,0:T(8,128)(2,1)S(1)} %fusion.22), channel_id=1, source_target_pairs={{256,192},{320,256},{384,320},{448,384},{257,193},{321,257},{385,3... | collective-permute-start | bytes 1016072 | tf_op jit(solution)/shard_map/ppermute | solution.py:68
  269.8 38.9 %all-to-all-start.2 = ((bf16[16,2,84,128]{3,1,2,0:T(2,128)(2,1)}), bf16[16,2,84,128]{3,1,2,0:T(2,128)(2,1)S(1)}, u32[]{:S(2)}, u32[]{:S(2)}) async-start(bf16[16,2,84,128]{3,1,2,0:T(2,128)(2,1)} %copy.68), calls=%async_computation.2 | async-start | bytes 1376256 | tf_op jit(solution)/shard_map/all_to_all | solution.py:120
  289.4 16.1 %collective-permute-start.29 = (bf16[168,1008]{1,0:T(8,128)(2,1)S(1)}, bf16[168,1008]{1,0:T(8,128)(2,1)S(1)}, u32[]{:S(2)}, u32[]{:S(2)}) collective-permute-start(bf16[168,1008]{1,0:T(8,128)(2,1)S(1)} %fusion.23), channel_id=1, source_target_pairs={{192,128},{256,192},{320,256},{384,320},{448,384},{193,129},{257,1... | collective-permute-start | bytes 1016072 | tf_op jit(solution)/shard_map/ppermute | solution.py:68
  306.7 17.0 %collective-permute-start.30 = (bf16[168,1008]{1,0:T(8,128)(2,1)S(1)}, bf16[168,1008]{1,0:T(8,128)(2,1)S(1)}, u32[]{:S(2)}, u32[]{:S(2)}) collective-permute-start(bf16[168,1008]{1,0:T(8,128)(2,1)S(1)} %fusion.24), channel_id=1, source_target_pairs={{128,64},{192,128},{256,192},{320,256},{384,320},{448,384},{129,65... | collective-permute-start | bytes 1016072 | tf_op jit(solution)/shard_map/ppermute | solution.py:68
  309.4 17.6 %collective-permute-start.16 = (bf16[84,128]{1,0:T(8,128)(2,1)S(1)}, bf16[84,128]{1,0:T(8,128)(2,1)S(1)}, u32[]{:S(2)}, u32[]{:S(2)}) collective-permute-start(bf16[84,128]{1,0:T(8,128)(2,1)S(1)} %bitcast.188), channel_id=1, source_target_pairs={{0,4},{4,0},{1,5},{5,1},{2,6},{6,2},{3,7},{7,3},{8,12},{12,8},{9,1... | collective-permute-start | bytes 64520 | tf_op jit(solution)/shard_map/ppermute | solution.py:42
  317.9 10.8 %collective-permute-start.24 = (bf16[168,1008]{1,0:T(8,128)(2,1)S(1)}, bf16[168,1008]{1,0:T(8,128)(2,1)S(1)}, u32[]{:S(2)}, u32[]{:S(2)}) collective-permute-start(bf16[168,1008]{1,0:T(8,128)(2,1)S(1)} %get-tuple-element.10), channel_id=1, source_target_pairs={{0,64},{64,128},{128,192},{192,256},{256,320},{320,384},{384,448},... | collective-permute-start | bytes 1016072 | tf_op jit(solution)/shard_map/ppermute | solution.py:65
  325.0 10.4 %collective-permute-start.31 = (bf16[168,1008]{1,0:T(8,128)(2,1)S(1)}, bf16[168,1008]{1,0:T(8,128)(2,1)S(1)}, u32[]{:S(2)}, u32[]{:S(2)}) collective-permute-start(bf16[168,1008]{1,0:T(8,128)(2,1)S(1)} %fusion.25), channel_id=1, source_target_pairs={{64,0},{128,64},{192,128},{256,192},{320,256},{384,320},{448,384},... | collective-permute-start | bytes 1016072 | tf_op jit(solution)/shard_map/ppermute | solution.py:68
  (20 other events, 259.9 us)

commit v2 on v1

v2 whole, which is shorter than its diff:
```python
import jax
import jax.numpy as jnp
from jax import lax
from jax.sharding import Mesh, PartitionSpec as P

FF = 10752
ZL = 8
GELU_SCALE = 0.7978845608028654


def gelu_parts(values):
    tanh_arg = GELU_SCALE * (values + 0.044715 * values * values * values)
    tanh_val = jnp.tanh(tanh_arg)
    activated = 0.5 * values * (1.0 + tanh_val)
    slope = 0.5 * (1.0 + tanh_val) + 0.5 * values * (1.0 - tanh_val * tanh_val) * GELU_SCALE * (
        1.0 + 3.0 * 0.044715 * values * values
    )
    return activated, slope


def dot(left, right, left_dim, right_dim):
    return lax.dot_general(
        left, right, (((left_dim,), (right_dim,)), ((), ())), preferred_element_type=jnp.float32
    )


def suffix_sums(cot_all):
    third = cot_all[3].astype(jnp.float32)
    second = cot_all[2].astype(jnp.float32) + third
    first = cot_all[1].astype(jnp.float32) + second
    zeroth = cot_all[0].astype(jnp.float32) + first
    return [part.astype(jnp.bfloat16) for part in (zeroth, first, second, third)]


def in_order(mine, other, index, axis):
    first = jnp.where(index == 0, mine, other)
    second = jnp.where(index == 0, other, mine)
    return jnp.stack([first, second], axis)


def swap(values, axis_name):
    return lax.ppermute(values, axis_name, [(0, 1), (1, 0)])


def line_gather(shard, place, ties):
    from_left, from_right = [], []
    right = left = shard
    for step in range(ZL - 1):
        right, left, _ = lax.optimization_barrier((right, left, ties.get(step, ())))
        right = lax.ppermute(right, "zl", [(i, i + 1) for i in range(step, ZL - 1)])
        left = lax.ppermute(left, "zl", [(i, i - 1) for i in range(1, ZL - step)])
        from_left.append(right)
        from_right.append(left)
    slots = jnp.stack(from_left[::-1] + [shard] + from_right)
    return lax.dynamic_slice_in_dim(slots, ZL - 1 - place, ZL, 0)


def line_scatter(parts, place, ties):
    right = left = None
    for step in range(ZL - 1):
        to_right = parts[jnp.clip(place + ZL - 1 - step, 0, ZL - 1)]
        to_left = parts[jnp.clip(place - ZL + 1 + step, 0, ZL - 1)]
        if step:
            to_right = to_right.astype(jnp.float32) + right.astype(jnp.float32)
            to_left = to_left.astype(jnp.float32) + left.astype(jnp.float32)
        to_right, to_left = to_right.astype(jnp.bfloat16), to_left.astype(jnp.bfloat16)
        to_right, to_left, _ = lax.optimization_barrier((to_right, to_left, ties.get(step, ())))
        right = lax.ppermute(to_right, "zl", [(i, i + 1) for i in range(step + 1)])
        left = lax.ppermute(to_left, "zl", [(i, i - 1) for i in range(ZL - 1 - step, ZL)])
    return (
        parts[place].astype(jnp.float32) + right.astype(jnp.float32) + left.astype(jnp.float32)
    )


def per_device(acts, cotangents, w_gate, w_up, w_down, unit_rank):
    place = lax.axis_index("zl")
    core = lax.axis_index("co")
    half = lax.axis_index("zh")
    tokens, features = acts.shape
    units = unit_rank.shape[0]
    rows = w_gate.shape[0]

    local = jnp.concatenate([acts.T] + [part.T for part in suffix_sums(cotangents)], 1)
    far_local = swap(local, "zh")

    def spread(values):
        copies = jnp.broadcast_to(values[None], (16,) + values.shape)
        got = lax.all_to_all(copies, ("y", "x"), 0, 0)
        return got.reshape((4, 2, 2) + values.shape)

    def both_tokens(values):
        kept = lax.dynamic_index_in_dim(values, core, 1, False)
        given = lax.dynamic_index_in_dim(values, 1 - core, 1, False)
        return kept, swap(given, "co")

    near = spread(local)
    near_parts = both_tokens(near)
    far = spread(far_local)
    far_parts = both_tokens(far)
    ties = {1: (far_local,), 3: (near,), 4: near_parts, 5: (far,), 6: far_parts}

    weights = line_gather(jnp.concatenate([w_gate, w_up, w_down.T], 1), place, ties)
    weights = weights.reshape(ZL * rows, 3 * units)
    inputs = in_order(
        jnp.concatenate(near_parts, -1), jnp.concatenate(far_parts, -1), half, 1
    ).reshape(ZL * rows, 10 * tokens)

    band = (
        (unit_rank >= FF // 8).astype(jnp.int32)
        + (unit_rank >= FF // 4).astype(jnp.int32)
        + (unit_rank >= FF // 2).astype(jnp.int32)
    )[None, :]
    products = dot(inputs, weights, 0, 0).reshape(2, 5, tokens, 3 * units)

    def of_bands(group):
        total = jnp.zeros((tokens, units), jnp.float32)
        for branch in range(4):
            total = jnp.where(band == branch, products[group, branch + 1, :, 2 * units :], total)
        return jnp.concatenate([products[group, 0, :, : 2 * units], total], 1)

    sums = of_bands(0) + swap(of_bands(1), "co")
    gate_proj, up_proj, grad_hidden = jnp.split(sums, 3, 1)
    activated, slope = gelu_parts(gate_proj)
    hidden = (activated * up_proj).astype(jnp.bfloat16)
    grad_gate_hidden = (grad_hidden * up_proj * slope).astype(jnp.bfloat16)
    grad_up_hidden = (grad_hidden * activated).astype(jnp.bfloat16)
    own = jnp.concatenate([grad_gate_hidden, grad_up_hidden, hidden], 1)
    other = swap(own, "co")

    def widened(values):
        up_to = jnp.pad(values[:, : 2 * units], ((0, 0), (0, units)))
        masked = [
            jnp.where(band == branch, values[:, 2 * units :], jnp.zeros((), values.dtype))
            for branch in range(4)
        ]
        return [up_to, jnp.pad(jnp.concatenate(masked, 0), ((0, 0), (2 * units, 0)))]

    wide = jnp.concatenate(widened(own) + widened(other), 0)
    parts = dot(inputs, wide, 1, 0).astype(jnp.bfloat16).reshape(ZL, rows, 3 * units)

    gate_up = jnp.concatenate([own[:, : 2 * units], other[:, : 2 * units]], 0)
    partial_acts = dot(weights[:, : 2 * units], gate_up, 1, 1).astype(jnp.bfloat16)
    kept, given = partial_acts[:, :tokens], partial_acts[:, tokens:]
    partial_acts = in_order(kept, swap(given, "co"), core, 0)
    partial_acts = partial_acts.reshape(2, 4, 2, 2, features, tokens)
    partial_acts = partial_acts.transpose(1, 0, 3, 2, 4, 5).reshape(16, 2, features, tokens)
    shares = lax.all_to_all(partial_acts, ("y", "x"), 0, 0)
    shares = jnp.sum(shares.astype(jnp.float32), 0)
    away = swap(shares[1 - half].astype(jnp.bfloat16), "zh")
    grad_acts = (shares[half] + away.astype(jnp.float32)).astype(jnp.bfloat16).T

    grads = line_scatter(parts, place, {3: (shares,), 5: (away,)}).astype(jnp.bfloat16)
    return (
        grad_acts,
        grads[:, :units],
        grads[:, units : 2 * units],
        grads[:, 2 * units :].T,
    )


def solution(mesh):
    fine = Mesh(mesh.devices.reshape(ZL, 2, 4, 2, 4), ("zl", "co", "y", "zh", "x"))
    dp, mp = ("zl", "co"), ("y", "zh", "x")
    return jax.shard_map(
        per_device,
        mesh=fine,
        in_specs=(P(dp, mp), P(None, dp, mp), P(dp, mp), P(dp, mp), P(mp, dp), P(mp)),
        out_specs=(P(dp, mp), P(dp, mp), P(dp, mp), P(mp, dp)),
        check_vma=False,
    )
```

time: 340 us -> 278 us (0.82)
  the two profiles are of different devices: /device:TPU:98 before, /device:TPU:6 now
where the time goes in v2:
time: 278 us; the launch traced here: 275 us
  starting transfers between devices  124 us (45%)
  waiting for transfers between devices  81.5 us (29%)
  local copies, waits for them, and re-layouts  36.6 us (13%)
  other arithmetic  22.8 us (8%)
  matrix products  9.36 us (3%)
    ppermute x7, waiting for transfers between devices, line_gather(): left = lax.ppermute(left, 'zl', [(i, i - 1) for i in range(1, ZL - step)])  42.7 us
    ppermute x7, starting transfers between devices, swap(): return lax.ppermute(values, axis_name, [(0, 1), (1, 0)])  35 us
    ppermute x7, starting transfers between devices, line_scatter(): right = lax.ppermute(to_right, 'zl', [(i, i + 1) for i in range(step + 1)])  34 us
    all_to_all x2, starting transfers between devices, spread(): got = lax.all_to_all(copies, ('y', 'x'), 0, 0)  16.6 us
    unnamed x77, local copies, waits for them, and re-layouts  13.4 us
    ppermute x7, waiting for transfers between devices, line_scatter(): right = lax.ppermute(to_right, 'zl', [(i, i + 1) for i in range(step + 1)])  12.8 us
    ppermute x7, starting transfers between devices, line_gather(): right = lax.ppermute(right, 'zl', [(i, i + 1) for i in range(step, ZL - 1)])  12.6 us
    ppermute x7, waiting for transfers between devices, swap(): return lax.ppermute(values, axis_name, [(0, 1), (1, 0)])  12.1 us
  transfers between devices with their start and end apart: 38, of which 17 were waited for; matrix products, arithmetic and copies ran while one was open for 14% of the time, Pallas kernels for 0%

profile of v2, /device:TPU:6, one launch (start us, length us, event | category | flops | bytes accessed | tf_op | source)
XLA Modules:
  0.0 275.3 jit_solution(518979441819895468)
XLA Ops:
  4.1 9.4 %all-to-all-start = ((bf16[16,84,640]{2,1,0:T(8,128)(2,1)}), bf16[16,84,640]{2,1,0:T(8,128)(2,1)S(1)}, u32[]{:S(2)}, u32[]{:S(2)}) async-start(bf16[16,84,640]{2,1,0:T(8,128)(2,1)} %broadcast_in_dim.86), calls=%async_computation | async-start | bytes 3604480 | tf_op jit(solution)/shard_map/all_to_all | solution.py:88
  13.5 13.9 %collective-permute-start.2 = (bf16[84,640]{1,0:T(8,128)(2,1)S(1)}, bf16[84,640]{1,0:T(8,128)(2,1)S(1)}, u32[]{:S(2)}, u32[]{:S(2)}) collective-permute-start(bf16[84,640]{1,0:T(8,128)(2,1)S(1)} %constant_dynamic-update-slice_fusion), channel_id=1, source_target_pairs={{0,4},{4,0},{1,5},{5,1},{2,6},{6,2},{3,7},{7,3},{8,12},{12,8},{9,1... | collective-permute-start | bytes 322568 | tf_op jit(solution)/shard_map/ppermute | solution.py:42
  27.4 7.6 %collective-permute-done.2 = bf16[84,640]{1,0:T(8,128)(2,1)S(1)} collective-permute-done((bf16[84,640]{1,0:T(8,128)(2,1)S(1)}, bf16[84,640]{1,0:T(8,128)(2,1)S(1)}, u32[]{:S(2)}, u32[]{:S(2)}) %collective-permute-start.2) | collective-permute-done | bytes 107552 | tf_op jit(solution)/shard_map/ppermute | solution.py:42
  36.8 7.2 %all-to-all-start.1 = ((bf16[16,84,640]{2,1,0:T(8,128)(2,1)}), bf16[16,84,640]{2,1,0:T(8,128)(2,1)S(1)}, u32[]{:S(2)}, u32[]{:S(2)}) async-start(bf16[16,84,640]{2,1,0:T(8,128)(2,1)} %broadcast_in_dim.87), calls=%async_computation.1 | async-start | bytes 3604480 | tf_op jit(solution)/shard_map/all_to_all | solution.py:88
  44.2 4.2 %collective-permute-start = (bf16[168,1008]{1,0:T(8,128)(2,1)S(1)}, bf16[168,1008]{1,0:T(8,128)(2,1)S(1)}, u32[]{:S(2)}, u32[]{:S(2)}) collective-permute-start(bf16[168,1008]{1,0:T(8,128)(2,1)S(1)} %pad_maximum_fusion.4), channel_id=1, source_target_pairs={{0,64},{64,128},{128,192},{192,256},{256,320},{320,384},{384,448},... | collective-permute-start | bytes 1016072 | tf_op jit(solution)/shard_map/ppermute | solution.py:50
  49.7 5.1 %collective-permute-done = bf16[168,1008]{1,0:T(8,128)(2,1)S(1)} collective-permute-done((bf16[168,1008]{1,0:T(8,128)(2,1)S(1)}, bf16[168,1008]{1,0:T(8,128)(2,1)S(1)}, u32[]{:S(2)}, u32[]{:S(2)}) %collective-permute-start) | collective-permute-done | bytes 338720 | tf_op jit(solution)/shard_map/ppermute | solution.py:50
  54.8 4.3 %collective-permute-done.1 = bf16[168,1008]{1,0:T(8,128)(2,1)S(1)} collective-permute-done((bf16[168,1008]{1,0:T(8,128)(2,1)S(1)}, bf16[168,1008]{1,0:T(8,128)(2,1)S(1)}, u32[]{:S(2)}, u32[]{:S(2)}) %collective-permute-start.1) | collective-permute-done | bytes 338720 | tf_op jit(solution)/shard_map/ppermute | solution.py:51
  66.6 8.2 %collective-permute-done.4 = bf16[168,1008]{1,0:T(8,128)(2,1)} collective-permute-done((bf16[168,1008]{1,0:T(8,128)(2,1)S(1)}, bf16[168,1008]{1,0:T(8,128)(2,1)}, u32[]{:S(2)}, u32[]{:S(2)}) %collective-permute-start.4) | collective-permute-done | bytes 338720 | tf_op jit(solution)/shard_map/ppermute | solution.py:51
  80.8 5.0 %collective-permute-done.6 = bf16[168,1008]{1,0:T(8,128)(2,1)} collective-permute-done((bf16[168,1008]{1,0:T(8,128)(2,1)}, bf16[168,1008]{1,0:T(8,128)(2,1)}, u32[]{:S(2)}, u32[]{:S(2)}) %collective-permute-start.6) | collective-permute-done | bytes 338720 | tf_op jit(solution)/shard_map/ppermute | solution.py:51
  88.5 11.2 %collective-permute-done.8 = bf16[168,1008]{1,0:T(8,128)(2,1)S(1)} collective-permute-done((bf16[168,1008]{1,0:T(8,128)(2,1)}, bf16[168,1008]{1,0:T(8,128)(2,1)S(1)}, u32[]{:S(2)}, u32[]{:S(2)}) %collective-permute-start.8) | collective-permute-done | bytes 338720 | tf_op jit(solution)/shard_map/ppermute | solution.py:51
  105.1 5.2 %collective-permute-done.11 = bf16[168,1008]{1,0:T(8,128)(2,1)S(1)} collective-permute-done((bf16[168,1008]{1,0:T(8,128)(2,1)S(1)}, bf16[168,1008]{1,0:T(8,128)(2,1)S(1)}, u32[]{:S(2)}, u32[]{:S(2)}) %collective-permute-start.11) | collective-permute-done | bytes 338720 | tf_op jit(solution)/shard_map/ppermute | solution.py:51
  113.8 8.8 %collective-permute-done.13 = bf16[168,1008]{1,0:T(8,128)(2,1)S(1)} collective-permute-done((bf16[168,1008]{1,0:T(8,128)(2,1)S(1)}, bf16[168,1008]{1,0:T(8,128)(2,1)S(1)}, u32[]{:S(2)}, u32[]{:S(2)}) %collective-permute-start.13) | collective-permute-done | bytes 338720 | tf_op jit(solution)/shard_map/ppermute | solution.py:51
  126.1 3.0 %reshape.181 = bf16[1344,1280]{1,0:T(8,128)(2,1)S(1)} reshape(bf16[4,2,2,84,1280]{4,3,2,1,0:T(8,128)(2,1)} %pad_maximum_fusion) | data formatting | bytes 6881280 | tf_op jit(solution)/shard_map/reshape | solution.py:106
  129.1 3.6 %copy.83 = bf16[1280,1344]{1,0:T(8,128)(2,1)} copy(bf16[1280,1344]{0,1:T(8,128)(2,1)S(1)} %bitcast.203) | data formatting | bytes 6881280 | tf_op jit(solution)/shard_map/dot_general | solution.py:22
  143.1 2.6 copy-done.3
  145.7 4.6 %fusion.71 = f32[2,5,128,1008]{2,3,1,0:T(8,128)S(1)} fusion(bf16[2,5,128,1344]{3,2,1,0:T(8,128)(2,1)S(1)} %bitcast.214, bf16[1344,1008,1,1]{1,0,3,2:T(8,128)(2,1)S(1)} %bitcast.217), kind=kOutput, calls=%fused_computation.170 | convolution fusion | flops 3468165120 | bytes 11311104 | tf_op jit(solution)/shard_map/dot_general | solution.py:22
  165.0 4.0 %convolution_convert_fusion = bf16[1344,1008]{1,0:T(8,128)(2,1)S(1)} fusion(bf16[1344,1280]{1,0:T(8,128)(2,1)S(1)} %reshape.181, bf16[512,1008]{0,1:T(8,128)(2,1)S(1)} %get-tuple-element.116, bf16[128,1008]{0,1:T(8,128)(2,1)S(1)} %broadcast_select_fusion.4, bf16[512,1008]{0,1:T(8,128)(2,1)S(1)} %get-tuple-element.115, bf16[128,1008]{0,1:T(8,128)(2,1)S(1)} %copy-done.28), kind=kOutput, calls=%fused_computation | convolution fusion | flops 3479841792 | bytes 8730624 | tf_op jit(solution)/shard_map/dot_general | solution.py:22
  169.1 4.6 %collective-permute-start.21 = (bf16[168,1008]{1,0:T(8,128)(2,1)S(1)}, bf16[168,1008]{1,0:T(8,128)(2,1)S(1)}, u32[]{:S(2)}, u32[]{:S(2)}) collective-permute-start(bf16[168,1008]{1,0:T(8,128)(2,1)S(1)} %get-tuple-element.46), channel_id=1, source_target_pairs={{0,64},{1,65},{2,66},{3,67},{4,68},{5,69},{6,70},{7,71},{8,72},{9,... | collective-permute-start | bytes 1016072 | tf_op jit(solution)/shard_map/ppermute | solution.py:68
  178.0 3.2 %collective-permute-done.21 = bf16[168,1008]{1,0:T(8,128)(2,1)S(1)} collective-permute-done((bf16[168,1008]{1,0:T(8,128)(2,1)S(1)}, bf16[168,1008]{1,0:T(8,128)(2,1)S(1)}, u32[]{:S(2)}, u32[]{:S(2)}) %collective-permute-start.21) | collective-permute-done | bytes 338720 | tf_op jit(solution)/shard_map/ppermute | solution.py:68
  181.3 2.2 fusion.27
  183.5 5.1 %collective-permute-start.23 = (bf16[168,1008]{1,0:T(8,128)(2,1)}, bf16[168,1008]{1,0:T(8,128)(2,1)}, u32[]{:S(2)}, u32[]{:S(2)}) collective-permute-start(bf16[168,1008]{1,0:T(8,128)(2,1)} %get-tuple-element.48), channel_id=1, source_target_pairs={{0,64},{64,128},{1,65},{65,129},{2,66},{66,130},{3,67},{67,131},{4... | collective-permute-start | bytes 1016072 | tf_op jit(solution)/shard_map/ppermute | solution.py:68
  194.2 7.3 %all-to-all-start.2 = ((bf16[16,2,84,128]{3,1,2,0:T(2,128)(2,1)}), bf16[16,2,84,128]{3,1,2,0:T(2,128)(2,1)S(1)}, u32[]{:S(2)}, u32[]{:S(2)}) async-start(bf16[16,2,84,128]{3,1,2,0:T(2,128)(2,1)} %copy.86), calls=%async_computation.2 | async-start | bytes 1376256 | tf_op jit(solution)/shard_map/all_to_all | solution.py:147
  207.1 4.2 %all-to-all-done.2 = bf16[16,2,84,128]{3,1,2,0:T(2,128)(2,1)S(1)} async-done(((bf16[16,2,84,128]{3,1,2,0:T(2,128)(2,1)}), bf16[16,2,84,128]{3,1,2,0:T(2,128)(2,1)S(1)}, u32[]{:S(2)}, u32[]{:S(2)}) %all-to-all-start.2) | async-done | bytes 688160 | tf_op jit(solution)/shard_map/all_to_all | solution.py:147
  214.0 3.9 %collective-permute-start.27 = (bf16[168,1008]{1,0:T(8,128)(2,1)}, bf16[168,1008]{1,0:T(8,128)(2,1)S(1)}, u32[]{:S(2)}, u32[]{:S(2)}) collective-permute-start(bf16[168,1008]{1,0:T(8,128)(2,1)} %get-tuple-element.52), channel_id=1, source_target_pairs={{0,64},{64,128},{128,192},{192,256},{1,65},{65,129},{129,193},{193... | collective-permute-start | bytes 1016072 | tf_op jit(solution)/shard_map/ppermute | solution.py:68
  219.4 4.2 %collective-permute-done.27 = bf16[168,1008]{1,0:T(8,128)(2,1)S(1)} collective-permute-done((bf16[168,1008]{1,0:T(8,128)(2,1)}, bf16[168,1008]{1,0:T(8,128)(2,1)S(1)}, u32[]{:S(2)}, u32[]{:S(2)}) %collective-permute-start.27) | collective-permute-done | bytes 338720 | tf_op jit(solution)/shard_map/ppermute | solution.py:68
  225.5 4.3 %collective-permute-start.29 = (bf16[168,1008]{1,0:T(8,128)(2,1)}, bf16[168,1008]{1,0:T(8,128)(2,1)S(1)}, u32[]{:S(2)}, u32[]{:S(2)}) collective-permute-start(bf16[168,1008]{1,0:T(8,128)(2,1)} %get-tuple-element.54), channel_id=1, source_target_pairs={{0,64},{64,128},{128,192},{192,256},{256,320},{1,65},{65,129},{129... | collective-permute-start | bytes 1016072 | tf_op jit(solution)/shard_map/ppermute | solution.py:68
  231.3 11.2 %collective-permute-start.20 = (bf16[84,128]{1,0:T(8,128)(2,1)S(1)}, bf16[84,128]{1,0:T(8,128)(2,1)S(1)}, u32[]{:S(2)}, u32[]{:S(2)}) collective-permute-start(bf16[84,128]{1,0:T(8,128)(2,1)S(1)} %bitcast.222), channel_id=1, source_target_pairs={{0,4},{4,0},{1,5},{5,1},{2,6},{6,2},{3,7},{7,3},{8,12},{12,8},{9,1... | collective-permute-start | bytes 64520 | tf_op jit(solution)/shard_map/ppermute | solution.py:42
  245.7 3.1 %collective-permute-start.31 = (bf16[168,1008]{1,0:T(8,128)(2,1)S(1)}, bf16[168,1008]{1,0:T(8,128)(2,1)}, u32[]{:S(2)}, u32[]{:S(2)}) collective-permute-start(bf16[168,1008]{1,0:T(8,128)(2,1)S(1)} %get-tuple-element.56), channel_id=1, source_target_pairs={{0,64},{64,128},{128,192},{192,256},{256,320},{320,384},{1,65},{65... | collective-permute-start | bytes 1016072 | tf_op jit(solution)/shard_map/ppermute | solution.py:68
  250.2 2.6 collective-permute-done.31
  254.2 10.9 %collective-permute-start.33 = (bf16[168,1008]{1,0:T(8,128)(2,1)S(1)}, bf16[168,1008]{1,0:T(8,128)(2,1)S(1)}, u32[]{:S(2)}, u32[]{:S(2)}) collective-permute-start(bf16[168,1008]{1,0:T(8,128)(2,1)S(1)} %get-tuple-element.58), channel_id=1, source_target_pairs={{0,64},{64,128},{128,192},{192,256},{256,320},{320,384},{384,448},... | collective-permute-start | bytes 1016072 | tf_op jit(solution)/shard_map/ppermute | solution.py:68
  267.1 2.8 %collective-permute-done.33 = bf16[168,1008]{1,0:T(8,128)(2,1)S(1)} collective-permute-done((bf16[168,1008]{1,0:T(8,128)(2,1)S(1)}, bf16[168,1008]{1,0:T(8,128)(2,1)S(1)}, u32[]{:S(2)}, u32[]{:S(2)}) %collective-permute-start.33) | collective-permute-done | bytes 338720 | tf_op jit(solution)/shard_map/ppermute | solution.py:68
  269.8 4.4 %collective-permute-done.34 = bf16[168,1008]{1,0:T(8,128)(2,1)S(1)} collective-permute-done((bf16[168,1008]{1,0:T(8,128)(2,1)S(1)}, bf16[168,1008]{1,0:T(8,128)(2,1)S(1)}, u32[]{:S(2)}, u32[]{:S(2)}) %collective-permute-start.34) | collective-permute-done | bytes 338720 | tf_op jit(solution)/shard_map/ppermute | solution.py:69
  (177 shorter events, 91.7 us)
Async XLA Ops:
  4.1 30.9 %all-to-all-start = ((bf16[16,84,640]{2,1,0:T(8,128)(2,1)}), bf16[16,84,640]{2,1,0:T(8,128)(2,1)S(1)}, u32[]{:S(2)}, u32[]{:S(2)}) async-start(bf16[16,84,640]{2,1,0:T(8,128)(2,1)} %broadcast_in_dim.86), calls=%async_computation | async-start | bytes 3604480 | tf_op jit(solution)/shard_map/all_to_all | solution.py:88
  13.5 21.5 %collective-permute-start.2 = (bf16[84,640]{1,0:T(8,128)(2,1)S(1)}, bf16[84,640]{1,0:T(8,128)(2,1)S(1)}, u32[]{:S(2)}, u32[]{:S(2)}) collective-permute-start(bf16[84,640]{1,0:T(8,128)(2,1)S(1)} %constant_dynamic-update-slice_fusion), channel_id=1, source_target_pairs={{0,4},{4,0},{1,5},{5,1},{2,6},{6,2},{3,7},{7,3},{8,12},{12,8},{9,1... | collective-permute-start | bytes 322568 | tf_op jit(solution)/shard_map/ppermute | solution.py:42
  36.8 40.7 %all-to-all-start.1 = ((bf16[16,84,640]{2,1,0:T(8,128)(2,1)}), bf16[16,84,640]{2,1,0:T(8,128)(2,1)S(1)}, u32[]{:S(2)}, u32[]{:S(2)}) async-start(bf16[16,84,640]{2,1,0:T(8,128)(2,1)} %broadcast_in_dim.87), calls=%async_computation.1 | async-start | bytes 3604480 | tf_op jit(solution)/shard_map/all_to_all | solution.py:88
  44.2 10.6 %collective-permute-start = (bf16[168,1008]{1,0:T(8,128)(2,1)S(1)}, bf16[168,1008]{1,0:T(8,128)(2,1)S(1)}, u32[]{:S(2)}, u32[]{:S(2)}) collective-permute-start(bf16[168,1008]{1,0:T(8,128)(2,1)S(1)} %pad_maximum_fusion.4), channel_id=1, source_target_pairs={{0,64},{64,128},{128,192},{192,256},{256,320},{320,384},{384,448},... | collective-permute-start | bytes 1016072 | tf_op jit(solution)/shard_map/ppermute | solution.py:50
  48.4 10.7 %collective-permute-start.1 = (bf16[168,1008]{1,0:T(8,128)(2,1)S(1)}, bf16[168,1008]{1,0:T(8,128)(2,1)S(1)}, u32[]{:S(2)}, u32[]{:S(2)}) collective-permute-start(bf16[168,1008]{1,0:T(8,128)(2,1)S(1)} %pad_maximum_fusion.4), channel_id=1, source_target_pairs={{64,0},{128,64},{192,128},{256,192},{320,256},{384,320},{448,384},... | collective-permute-start | bytes 1016072 | tf_op jit(solution)/shard_map/ppermute | solution.py:51
  59.1 7.5 %collective-permute-start.3 = (bf16[168,1008]{1,0:T(8,128)(2,1)S(1)}, bf16[168,1008]{1,0:T(8,128)(2,1)}, u32[]{:S(2)}, u32[]{:S(2)}) collective-permute-start(bf16[168,1008]{1,0:T(8,128)(2,1)S(1)} %collective-permute-done), channel_id=1, source_target_pairs={{64,128},{128,192},{192,256},{256,320},{320,384},{384,448},{65,129... | collective-permute-start | bytes 1016072 | tf_op jit(solution)/shard_map/ppermute | solution.py:50
  60.5 14.3 %collective-permute-start.4 = (bf16[168,1008]{1,0:T(8,128)(2,1)S(1)}, bf16[168,1008]{1,0:T(8,128)(2,1)}, u32[]{:S(2)}, u32[]{:S(2)}) collective-permute-start(bf16[168,1008]{1,0:T(8,128)(2,1)S(1)} %collective-permute-done.1), channel_id=1, source_target_pairs={{64,0},{128,64},{192,128},{256,192},{320,256},{384,320},{65,1},{12... | collective-permute-start | bytes 1016072 | tf_op jit(solution)/shard_map/ppermute | solution.py:51
  64.6 35.1 %collective-permute-start.9 = (bf16[4,2,84,640]{3,0,2,1:T(4,128)(2,1)}, bf16[4,2,84,640]{3,0,2,1:T(4,128)(2,1)}, u32[]{:S(2)}, u32[]{:S(2)}) collective-permute-start(bf16[4,2,84,640]{3,0,2,1:T(4,128)(2,1)} %copy.79), channel_id=1, source_target_pairs={{0,32},{32,0},{1,33},{33,1},{2,34},{34,2},{3,35},{35,3},{4,36},{36... | collective-permute-start | bytes 2580488 | tf_op jit(solution)/shard_map/ppermute | solution.py:42
  74.7 6.1 %collective-permute-start.5 = (bf16[168,1008]{1,0:T(8,128)(2,1)}, bf16[168,1008]{1,0:T(8,128)(2,1)}, u32[]{:S(2)}, u32[]{:S(2)}) collective-permute-start(bf16[168,1008]{1,0:T(8,128)(2,1)} %collective-permute-done.3), channel_id=1, source_target_pairs={{128,192},{192,256},{256,320},{320,384},{384,448},{129,193},{193,2... | collective-permute-start | bytes 1016072 | tf_op jit(solution)/shard_map/ppermute | solution.py:50
  76.1 9.7 %collective-permute-start.6 = (bf16[168,1008]{1,0:T(8,128)(2,1)}, bf16[168,1008]{1,0:T(8,128)(2,1)}, u32[]{:S(2)}, u32[]{:S(2)}) collective-permute-start(bf16[168,1008]{1,0:T(8,128)(2,1)} %collective-permute-done.4), channel_id=1, source_target_pairs={{64,0},{128,64},{192,128},{256,192},{320,256},{65,1},{129,65},{193... | collective-permute-start | bytes 1016072 | tf_op jit(solution)/shard_map/ppermute | solution.py:51
  78.9 24.9 %collective-permute-start.14 = (bf16[4,2,84,640]{3,0,2,1:T(4,128)(2,1)S(1)}, bf16[4,2,84,640]{3,0,2,1:T(4,128)(2,1)}, u32[]{:S(2)}, u32[]{:S(2)}) collective-permute-start(bf16[4,2,84,640]{3,0,2,1:T(4,128)(2,1)S(1)} %copy.80), channel_id=1, source_target_pairs={{0,32},{32,0},{1,33},{33,1},{2,34},{34,2},{3,35},{35,3},{4,36},{36... | collective-permute-start | bytes 2580488 | tf_op jit(solution)/shard_map/ppermute | solution.py:42
  87.2 12.5 %collective-permute-start.8 = (bf16[168,1008]{1,0:T(8,128)(2,1)}, bf16[168,1008]{1,0:T(8,128)(2,1)S(1)}, u32[]{:S(2)}, u32[]{:S(2)}) collective-permute-start(bf16[168,1008]{1,0:T(8,128)(2,1)} %collective-permute-done.6), channel_id=1, source_target_pairs={{64,0},{128,64},{192,128},{256,192},{65,1},{129,65},{193,129},{257... | collective-permute-start | bytes 1016072 | tf_op jit(solution)/shard_map/ppermute | solution.py:51
  101.2 9.1 %collective-permute-start.11 = (bf16[168,1008]{1,0:T(8,128)(2,1)S(1)}, bf16[168,1008]{1,0:T(8,128)(2,1)S(1)}, u32[]{:S(2)}, u32[]{:S(2)}) collective-permute-start(bf16[168,1008]{1,0:T(8,128)(2,1)S(1)} %collective-permute-done.8), channel_id=1, source_target_pairs={{64,0},{128,64},{192,128},{65,1},{129,65},{193,129},{66,2},{130,66... | collective-permute-start | bytes 1016072 | tf_op jit(solution)/shard_map/ppermute | solution.py:51
  111.7 10.8 %collective-permute-start.13 = (bf16[168,1008]{1,0:T(8,128)(2,1)S(1)}, bf16[168,1008]{1,0:T(8,128)(2,1)S(1)}, u32[]{:S(2)}, u32[]{:S(2)}) collective-permute-start(bf16[168,1008]{1,0:T(8,128)(2,1)S(1)} %collective-permute-done.11), channel_id=1, source_target_pairs={{64,0},{128,64},{65,1},{129,65},{66,2},{130,66},{67,3},{131,67},{6... | collective-permute-start | bytes 1016072 | tf_op jit(solution)/shard_map/ppermute | solution.py:51
  122.5 11.6 %collective-permute-start.15 = (bf16[168,1008]{1,0:T(8,128)(2,1)}, bf16[168,1008]{1,0:T(8,128)(2,1)}, u32[]{:S(2)}, u32[]{:S(2)}) collective-permute-start(bf16[168,1008]{1,0:T(8,128)(2,1)} %collective-permute-done.12), channel_id=1, source_target_pairs={{384,448},{385,449},{386,450},{387,451},{388,452},{389,453},{390,4... | collective-permute-start | bytes 1016072 | tf_op jit(solution)/shard_map/ppermute | solution.py:50
  132.7 10.1 %collective-permute-start.16 = (bf16[168,1008]{1,0:T(8,128)(2,1)}, bf16[168,1008]{1,0:T(8,128)(2,1)S(1)}, u32[]{:S(2)}, u32[]{:S(2)}) collective-permute-start(bf16[168,1008]{1,0:T(8,128)(2,1)} %copy-done.22), channel_id=1, source_target_pairs={{64,0},{65,1},{66,2},{67,3},{68,4},{69,5},{70,6},{71,7},{72,8},{73... | collective-permute-start | bytes 1016072 | tf_op jit(solution)/shard_map/ppermute | solution.py:51
  169.1 12.2 %collective-permute-start.21 = (bf16[168,1008]{1,0:T(8,128)(2,1)S(1)}, bf16[168,1008]{1,0:T(8,128)(2,1)S(1)}, u32[]{:S(2)}, u32[]{:S(2)}) collective-permute-start(bf16[168,1008]{1,0:T(8,128)(2,1)S(1)} %get-tuple-element.46), channel_id=1, source_target_pairs={{0,64},{1,65},{2,66},{3,67},{4,68},{5,69},{6,70},{7,71},{8,72},{9,... | collective-permute-start | bytes 1016072 | tf_op jit(solution)/shard_map/ppermute | solution.py:68
  173.7 7.6 %collective-permute-start.22 = (bf16[168,1008]{1,0:T(8,128)(2,1)S(1)}, bf16[168,1008]{1,0:T(8,128)(2,1)S(1)}, u32[]{:S(2)}, u32[]{:S(2)}) collective-permute-start(bf16[168,1008]{1,0:T(8,128)(2,1)S(1)} %get-tuple-element.47), channel_id=1, source_target_pairs={{448,384},{449,385},{450,386},{451,387},{452,388},{453,389},{454,3... | collective-permute-start | bytes 1016072 | tf_op jit(solution)/shard_map/ppermute | solution.py:69
  176.1 13.9 %collective-permute-start.19 = (bf16[1344,128]{1,0:T(8,128)(2,1)S(1)}, bf16[1344,128]{1,0:T(8,128)(2,1)S(1)}, u32[]{:S(2)}, u32[]{:S(2)}) collective-permute-start(bf16[1344,128]{1,0:T(8,128)(2,1)S(1)} %slice.109), channel_id=1, source_target_pairs={{0,32},{32,0},{1,33},{33,1},{2,34},{34,2},{3,35},{35,3},{4,36},{36... | collective-permute-start | bytes 1032200 | tf_op jit(solution)/shard_map/ppermute | solution.py:42
  183.5 18.0 %collective-permute-start.23 = (bf16[168,1008]{1,0:T(8,128)(2,1)}, bf16[168,1008]{1,0:T(8,128)(2,1)}, u32[]{:S(2)}, u32[]{:S(2)}) collective-permute-start(bf16[168,1008]{1,0:T(8,128)(2,1)} %get-tuple-element.48), channel_id=1, source_target_pairs={{0,64},{64,128},{1,65},{65,129},{2,66},{66,130},{3,67},{67,131},{4... | collective-permute-start | bytes 1016072 | tf_op jit(solution)/shard_map/ppermute | solution.py:68
  188.6 12.9 %collective-permute-start.24 = (bf16[168,1008]{1,0:T(8,128)(2,1)}, bf16[168,1008]{1,0:T(8,128)(2,1)}, u32[]{:S(2)}, u32[]{:S(2)}) collective-permute-start(bf16[168,1008]{1,0:T(8,128)(2,1)} %get-tuple-element.49), channel_id=1, source_target_pairs={{384,320},{448,384},{385,321},{449,385},{386,322},{450,386},{387,3... | collective-permute-start | bytes 1016072 | tf_op jit(solution)/shard_map/ppermute | solution.py:69
  194.2 17.1 %all-to-all-start.2 = ((bf16[16,2,84,128]{3,1,2,0:T(2,128)(2,1)}), bf16[16,2,84,128]{3,1,2,0:T(2,128)(2,1)S(1)}, u32[]{:S(2)}, u32[]{:S(2)}) async-start(bf16[16,2,84,128]{3,1,2,0:T(2,128)(2,1)} %copy.86), calls=%async_computation.2 | async-start | bytes 1376256 | tf_op jit(solution)/shard_map/all_to_all | solution.py:147
  203.7 8.2 %collective-permute-start.25 = (bf16[168,1008]{1,0:T(8,128)(2,1)}, bf16[168,1008]{1,0:T(8,128)(2,1)}, u32[]{:S(2)}, u32[]{:S(2)}) collective-permute-start(bf16[168,1008]{1,0:T(8,128)(2,1)} %get-tuple-element.50), channel_id=1, source_target_pairs={{0,64},{64,128},{128,192},{1,65},{65,129},{129,193},{2,66},{66,130... | collective-permute-start | bytes 1016072 | tf_op jit(solution)/shard_map/ppermute | solution.py:68
  205.7 6.2 %collective-permute-start.26 = (bf16[168,1008]{1,0:T(8,128)(2,1)}, bf16[168,1008]{1,0:T(8,128)(2,1)}, u32[]{:S(2)}, u32[]{:S(2)}) collective-permute-start(bf16[168,1008]{1,0:T(8,128)(2,1)} %get-tuple-element.51), channel_id=1, source_target_pairs={{320,256},{384,320},{448,384},{321,257},{385,321},{449,385},{322,2... | collective-permute-start | bytes 1016072 | tf_op jit(solution)/shard_map/ppermute | solution.py:69
  214.0 9.5 %collective-permute-start.27 = (bf16[168,1008]{1,0:T(8,128)(2,1)}, bf16[168,1008]{1,0:T(8,128)(2,1)S(1)}, u32[]{:S(2)}, u32[]{:S(2)}) collective-permute-start(bf16[168,1008]{1,0:T(8,128)(2,1)} %get-tuple-element.52), channel_id=1, source_target_pairs={{0,64},{64,128},{128,192},{192,256},{1,65},{65,129},{129,193},{193... | collective-permute-start | bytes 1016072 | tf_op jit(solution)/shard_map/ppermute | solution.py:68
  218.0 5.6 %collective-permute-start.28 = (bf16[168,1008]{1,0:T(8,128)(2,1)S(1)}, bf16[168,1008]{1,0:T(8,128)(2,1)}, u32[]{:S(2)}, u32[]{:S(2)}) collective-permute-start(bf16[168,1008]{1,0:T(8,128)(2,1)S(1)} %get-tuple-element.53), channel_id=1, source_target_pairs={{256,192},{320,256},{384,320},{448,384},{257,193},{321,257},{385,3... | collective-permute-start | bytes 1016072 | tf_op jit(solution)/shard_map/ppermute | solution.py:69
  225.5 17.0 %collective-permute-start.29 = (bf16[168,1008]{1,0:T(8,128)(2,1)}, bf16[168,1008]{1,0:T(8,128)(2,1)S(1)}, u32[]{:S(2)}, u32[]{:S(2)}) collective-permute-start(bf16[168,1008]{1,0:T(8,128)(2,1)} %get-tuple-element.54), channel_id=1, source_target_pairs={{0,64},{64,128},{128,192},{192,256},{256,320},{1,65},{65,129},{129... | collective-permute-start | bytes 1016072 | tf_op jit(solution)/shard_map/ppermute | solution.py:68
  229.8 13.4 %collective-permute-start.30 = (bf16[168,1008]{1,0:T(8,128)(2,1)S(1)}, bf16[168,1008]{1,0:T(8,128)(2,1)}, u32[]{:S(2)}, u32[]{:S(2)}) collective-permute-start(bf16[168,1008]{1,0:T(8,128)(2,1)S(1)} %get-tuple-element.55), channel_id=1, source_target_pairs={{192,128},{256,192},{320,256},{384,320},{448,384},{193,129},{257,1... | collective-permute-start | bytes 1016072 | tf_op jit(solution)/shard_map/ppermute | solution.py:69
  231.3 14.4 %collective-permute-start.20 = (bf16[84,128]{1,0:T(8,128)(2,1)S(1)}, bf16[84,128]{1,0:T(8,128)(2,1)S(1)}, u32[]{:S(2)}, u32[]{:S(2)}) collective-permute-start(bf16[84,128]{1,0:T(8,128)(2,1)S(1)} %bitcast.222), channel_id=1, source_target_pairs={{0,4},{4,0},{1,5},{5,1},{2,6},{6,2},{3,7},{7,3},{8,12},{12,8},{9,1... | collective-permute-start | bytes 64520 | tf_op jit(solution)/shard_map/ppermute | solution.py:42
  245.7 7.1 %collective-permute-start.31 = (bf16[168,1008]{1,0:T(8,128)(2,1)S(1)}, bf16[168,1008]{1,0:T(8,128)(2,1)}, u32[]{:S(2)}, u32[]{:S(2)}) collective-permute-start(bf16[168,1008]{1,0:T(8,128)(2,1)S(1)} %get-tuple-element.56), channel_id=1, source_target_pairs={{0,64},{64,128},{128,192},{192,256},{256,320},{320,384},{1,65},{65... | collective-permute-start | bytes 1016072 | tf_op jit(solution)/shard_map/ppermute | solution.py:68
  254.2 15.7 %collective-permute-start.33 = (bf16[168,1008]{1,0:T(8,128)(2,1)S(1)}, bf16[168,1008]{1,0:T(8,128)(2,1)S(1)}, u32[]{:S(2)}, u32[]{:S(2)}) collective-permute-start(bf16[168,1008]{1,0:T(8,128)(2,1)S(1)} %get-tuple-element.58), channel_id=1, source_target_pairs={{0,64},{64,128},{128,192},{192,256},{256,320},{320,384},{384,448},... | collective-permute-start | bytes 1016072 | tf_op jit(solution)/shard_map/ppermute | solution.py:68
  265.1 9.1 %collective-permute-start.34 = (bf16[168,1008]{1,0:T(8,128)(2,1)S(1)}, bf16[168,1008]{1,0:T(8,128)(2,1)S(1)}, u32[]{:S(2)}, u32[]{:S(2)}) collective-permute-start(bf16[168,1008]{1,0:T(8,128)(2,1)S(1)} %get-tuple-element.59), channel_id=1, source_target_pairs={{64,0},{128,64},{192,128},{256,192},{320,256},{384,320},{448,384},... | collective-permute-start | bytes 1016072 | tf_op jit(solution)/shard_map/ppermute | solution.py:69
  (37 other events, 391.1 us)

commit v3 on v2

--- a/solution.py
+++ b/solution.py
@@ -45,31 +45,46 @@
 def line_gather(shard, place, ties):
     from_left, from_right = [], []
     right = left = shard
+    carried = {}
     for step in range(ZL - 1):
-        right, left, _ = lax.optimization_barrier((right, left, ties.get(step, ())))
+        if step in ties:
+            names, make = ties[step]
+            arrays = make(carried)
+            right, left, arrays = lax.optimization_barrier((right, left, arrays))
+            carried.update(zip(names, arrays))
+        else:
+            right, left = lax.optimization_barrier((right, left))
         right = lax.ppermute(right, "zl", [(i, i + 1) for i in range(step, ZL - 1)])
         left = lax.ppermute(left, "zl", [(i, i - 1) for i in range(1, ZL - step)])
         from_left.append(right)
         from_right.append(left)
     slots = jnp.stack(from_left[::-1] + [shard] + from_right)
-    return lax.dynamic_slice_in_dim(slots, ZL - 1 - place, ZL, 0)
+    return lax.dynamic_slice_in_dim(slots, ZL - 1 - place, ZL, 0), carried
 
 
 def line_scatter(parts, place, ties):
-    right = left = None
+    rows = parts.shape[1]
+    cut = rows // 16 * 8
+    cuts = ((0, cut), (cut, rows))
+    right, left = [None, None], [None, None]
+    before = ()
     for step in range(ZL - 1):
-        to_right = parts[jnp.clip(place + ZL - 1 - step, 0, ZL - 1)]
-        to_left = parts[jnp.clip(place - ZL + 1 + step, 0, ZL - 1)]
-        if step:
-            to_right = to_right.astype(jnp.float32) + right.astype(jnp.float32)
-            to_left = to_left.astype(jnp.float32) + left.astype(jnp.float32)
-        to_right, to_left = to_right.astype(jnp.bfloat16), to_left.astype(jnp.bfloat16)
-        to_right, to_left, _ = lax.optimization_barrier((to_right, to_left, ties.get(step, ())))
-        right = lax.ppermute(to_right, "zl", [(i, i + 1) for i in range(step + 1)])
-        left = lax.ppermute(to_left, "zl", [(i, i - 1) for i in range(ZL - 1 - step, ZL)])
-    return (
-        parts[place].astype(jnp.float32) + right.astype(jnp.float32) + left.astype(jnp.float32)
-    )
+        for which, (low, high) in enumerate(cuts):
+            to_right = parts[jnp.clip(place + ZL - 1 - step, 0, ZL - 1), low:high]
+            to_left = parts[jnp.clip(place - ZL + 1 + step, 0, ZL - 1), low:high]
+            if step:
+                to_right = to_right.astype(jnp.float32) + right[which].astype(jnp.float32)
+                to_left = to_left.astype(jnp.float32) + left[which].astype(jnp.float32)
+            to_right, to_left = to_right.astype(jnp.bfloat16), to_left.astype(jnp.bfloat16)
+            tie = (before, ties.get(step, ()) if which == 0 else ())
+            to_right, to_left, _ = lax.optimization_barrier((to_right, to_left, tie))
+            before = (right[1 - which], left[1 - which]) if step else ()
+            right[which] = lax.ppermute(to_right, "zl", [(i, i + 1) for i in range(step + 1)])
+            left[which] = lax.ppermute(
+                to_left, "zl", [(i, i - 1) for i in range(ZL - 1 - step, ZL)]
+            )
+    own = parts[place].astype(jnp.float32)
+    return own + sum(jnp.concatenate(side, 0).astype(jnp.float32) for side in (right, left))
 
 
 def per_device(acts, cotangents, w_gate, w_up, w_down, unit_rank):
@@ -93,16 +108,21 @@
         given = lax.dynamic_index_in_dim(values, 1 - core, 1, False)
         return kept, swap(given, "co")
 
+    down = lax.all_gather(w_down.T, "zl").reshape(ZL * rows, units)
     near = spread(local)
-    near_parts = both_tokens(near)
-    far = spread(far_local)
-    far_parts = both_tokens(far)
-    ties = {1: (far_local,), 3: (near,), 4: near_parts, 5: (far,), 6: far_parts}
-
-    weights = line_gather(jnp.concatenate([w_gate, w_up, w_down.T], 1), place, ties)
-    weights = weights.reshape(ZL * rows, 3 * units)
+    ties = {
+        2: (("near", "far_local"), lambda done: (near, far_local)),
+        4: (("kept", "given"), lambda done: both_tokens(done["near"])),
+        5: (("far",), lambda done: (spread(done["far_local"]),)),
+        6: (("far_kept", "far_given"), lambda done: both_tokens(done["far"])),
+    }
+    gate_up_weights, done = line_gather(jnp.concatenate([w_gate, w_up], 1), place, ties)
+    gate_up_weights = gate_up_weights.reshape(ZL * rows, 2 * units)
     inputs = in_order(
-        jnp.concatenate(near_parts, -1), jnp.concatenate(far_parts, -1), half, 1
+        jnp.concatenate([done["kept"], done["given"]], -1),
+        jnp.concatenate([done["far_kept"], done["far_given"]], -1),
+        half,
+        1,
     ).reshape(ZL * rows, 10 * tokens)
 
     band = (
@@ -110,15 +130,18 @@
         + (unit_rank >= FF // 4).astype(jnp.int32)
         + (unit_rank >= FF // 2).astype(jnp.int32)
     )[None, :]
-    products = dot(inputs, weights, 0, 0).reshape(2, 5, tokens, 3 * units)
 
-    def of_bands(group):
+    def products(group):
+        first = group * 5 * tokens
+        gate_up = dot(inputs[:, first : first + tokens], gate_up_weights, 0, 0)
         total = jnp.zeros((tokens, units), jnp.float32)
+        by_branch = dot(inputs[:, first + tokens : first + 5 * tokens], down, 0, 0)
         for branch in range(4):
-            total = jnp.where(band == branch, products[group, branch + 1, :, 2 * units :], total)
-        return jnp.concatenate([products[group, 0, :, : 2 * units], total], 1)
+            here = by_branch[branch * tokens : (branch + 1) * tokens]
+            total = jnp.where(band == branch, here, total)
+        return jnp.concatenate([gate_up, total], 1)
 
-    sums = of_bands(0) + swap(of_bands(1), "co")
+    sums = products(0) + swap(products(1), "co")
     gate_proj, up_proj, grad_hidden = jnp.split(sums, 3, 1)
     activated, slope = gelu_parts(gate_proj)
     hidden = (activated * up_proj).astype(jnp.bfloat16)
@@ -139,7 +162,7 @@
     parts = dot(inputs, wide, 1, 0).astype(jnp.bfloat16).reshape(ZL, rows, 3 * units)
 
     gate_up = jnp.concatenate([own[:, : 2 * units], other[:, : 2 * units]], 0)
-    partial_acts = dot(weights[:, : 2 * units], gate_up, 1, 1).astype(jnp.bfloat16)
+    partial_acts = dot(gate_up_weights, gate_up, 1, 1).astype(jnp.bfloat16)
     kept, given = partial_acts[:, :tokens], partial_acts[:, tokens:]
     partial_acts = in_order(kept, swap(given, "co"), core, 0)
     partial_acts = partial_acts.reshape(2, 4, 2, 2, features, tokens)

time: 278 us -> 373 us (1.34)
  starting transfers between devices: 124 us -> 203 us
  blocking collectives: 0 us -> 53 us
  waiting for transfers between devices: 81.5 us -> 62.5 us
  local copies, waits for them, and re-layouts: 36.6 us -> 23.5 us
  other arithmetic: 22.8 us -> 13.8 us
    ppermute x7 -> x14, starting transfers between devices: 8.94 us -> 65.6 us  [line_scatter(): lax.ppermute(to_left, 'zl', [(i, i - 1) for i in range(ZL - 1 - step, ZL)])]
    all_gather x0 -> x1, blocking collectives: none -> 53 us  [per_device(): down = lax.all_gather(w_down.T, 'zl').reshape(ZL * rows, units)]
    ppermute x7 -> x14, starting transfers between devices: 34 us -> 58.3 us  [line_scatter(): lax.ppermute(to_right, 'zl', [(i, i + 1) for i in range(step + 1)])]
    ppermute x7 -> x14, waiting for transfers between devices: 12.8 us -> 2.51 us  [line_scatter(): lax.ppermute(to_right, 'zl', [(i, i + 1) for i in range(step + 1)])]
    unnamed x77, local copies, waits for them, and re-layouts: 13.4 us -> 5.27 us
    ppermute x7, starting transfers between devices: 12.6 us -> 7.47 us  [line_gather(): right = lax.ppermute(right, 'zl', [(i, i + 1) for i in range(step, ZL - 1)])]
    all_to_all x1, waiting for transfers between devices: 4.23 us -> 0.01 us  [per_device(): shares = lax.all_to_all(partial_acts, ('y', 'x'), 0, 0)]
    convert_element_type x6 -> x12, other arithmetic: 11.1 us -> 7.28 us  [line_scatter(): to_left.astype(jnp.bfloat16)]
  transfers between devices with their start and end apart: 38 -> 52, of which waited for: 17 -> 15; matrix products, arithmetic and copies ran while one was open for 14% -> 6% of each run, Pallas kernels for 0% -> 0%
where the time goes in v3:
time: 373 us; the launch traced here: 369 us
  starting transfers between devices  203 us (54%)
  waiting for transfers between devices  62.5 us (17%)
  blocking collectives  53 us (14%)
  local copies, waits for them, and re-layouts  23.5 us (6%)
  other arithmetic  13.8 us (4%)
  matrix products  12.1 us (3%)
    ppermute x14, starting transfers between devices, line_scatter(): lax.ppermute(to_left, 'zl', [(i, i - 1) for i in range(ZL - 1 - step, ZL)])  65.6 us
    ppermute x14, starting transfers between devices, line_scatter(): lax.ppermute(to_right, 'zl', [(i, i + 1) for i in range(step + 1)])  58.3 us
    all_gather x1, blocking collectives, per_device(): down = lax.all_gather(w_down.T, 'zl').reshape(ZL * rows, units)  53 us
    ppermute x7, waiting for transfers between devices, line_gather(): left = lax.ppermute(left, 'zl', [(i, i - 1) for i in range(1, ZL - step)])  39 us
    ppermute x7, starting transfers between devices, swap(): return lax.ppermute(values, axis_name, [(0, 1), (1, 0)])  38.3 us
    all_to_all x2, starting transfers between devices, spread(): got = lax.all_to_all(copies, ('y', 'x'), 0, 0)  16.6 us
    ppermute x7, waiting for transfers between devices, swap(): return lax.ppermute(values, axis_name, [(0, 1), (1, 0)])  12.3 us
    dot_general x6, matrix products, dot(): lax.dot_general(left, right, (((left_dim,), (right_dim,)), ((), ())), pre...  12.1 us
  transfers between devices with their start and end apart: 52, of which 15 were waited for; matrix products, arithmetic and copies ran while one was open for 6% of the time, Pallas kernels for 0%

profile of v3, /device:TPU:6, one launch (start us, length us, event | category | flops | bytes accessed | tf_op | source)
XLA Modules:
  0.0 369.4 jit_solution(10076119671469132759)
XLA Ops:
  4.1 9.4 %all-to-all-start = ((bf16[16,84,640]{2,1,0:T(8,128)(2,1)}), bf16[16,84,640]{2,1,0:T(8,128)(2,1)S(1)}, u32[]{:S(2)}, u32[]{:S(2)}) async-start(bf16[16,84,640]{2,1,0:T(8,128)(2,1)} %broadcast_in_dim.86), calls=%async_computation | async-start | bytes 3604480 | tf_op jit(solution)/shard_map/all_to_all | solution.py:103
  16.8 3.6 collective-permute-done
  20.4 4.3 %collective-permute-done.1 = bf16[168,672]{1,0:T(8,128)(2,1)S(1)} collective-permute-done((bf16[168,672]{1,0:T(8,128)(2,1)S(1)}, bf16[168,672]{1,0:T(8,128)(2,1)S(1)}, u32[]{:S(2)}, u32[]{:S(2)}) %collective-permute-start.1) | collective-permute-done | bytes 225824 | tf_op jit(solution)/shard_map/ppermute | solution.py:58
  26.6 14.7 %collective-permute-start.4 = (bf16[84,640]{1,0:T(8,128)(2,1)S(1)}, bf16[84,640]{1,0:T(8,128)(2,1)S(1)}, u32[]{:S(2)}, u32[]{:S(2)}) collective-permute-start(bf16[84,640]{1,0:T(8,128)(2,1)S(1)} %constant_dynamic-update-slice_fusion), channel_id=1, source_target_pairs={{0,4},{4,0},{1,5},{5,1},{2,6},{6,2},{3,7},{7,3},{8,12},{12,8},{9,1... | collective-permute-start | bytes 322568 | tf_op jit(solution)/shard_map/ppermute | solution.py:42
  41.3 9.5 %collective-permute-done.4 = bf16[84,640]{1,0:T(8,128)(2,1)S(1)} collective-permute-done((bf16[84,640]{1,0:T(8,128)(2,1)S(1)}, bf16[84,640]{1,0:T(8,128)(2,1)S(1)}, u32[]{:S(2)}, u32[]{:S(2)}) %collective-permute-start.4) | collective-permute-done | bytes 107552 | tf_op jit(solution)/shard_map/ppermute | solution.py:42
  52.7 7.2 %all-to-all-start.1 = ((bf16[16,84,640]{2,1,0:T(8,128)(2,1)}), bf16[16,84,640]{2,1,0:T(8,128)(2,1)S(1)}, u32[]{:S(2)}, u32[]{:S(2)}) async-start(bf16[16,84,640]{2,1,0:T(8,128)(2,1)} %broadcast_in_dim.87), calls=%async_computation.1 | async-start | bytes 3604480 | tf_op jit(solution)/shard_map/all_to_all | solution.py:103
  65.9 11.5 %collective-permute-done.6 = bf16[168,672]{1,0:T(8,128)(2,1)S(1)} collective-permute-done((bf16[168,672]{1,0:T(8,128)(2,1)S(1)}, bf16[168,672]{1,0:T(8,128)(2,1)S(1)}, u32[]{:S(2)}, u32[]{:S(2)}) %collective-permute-start.6) | collective-permute-done | bytes 225824 | tf_op jit(solution)/shard_map/ppermute | solution.py:58
  79.3 12.9 %collective-permute-done.8 = bf16[168,672]{1,0:T(8,128)(2,1)S(1)} collective-permute-done((bf16[168,672]{1,0:T(8,128)(2,1)S(1)}, bf16[168,672]{1,0:T(8,128)(2,1)S(1)}, u32[]{:S(2)}, u32[]{:S(2)}) %collective-permute-start.8) | collective-permute-done | bytes 225824 | tf_op jit(solution)/shard_map/ppermute | solution.py:58
  94.9 7.9 %collective-permute-done.11 = bf16[168,672]{1,0:T(8,128)(2,1)} collective-permute-done((bf16[168,672]{1,0:T(8,128)(2,1)S(1)}, bf16[168,672]{1,0:T(8,128)(2,1)}, u32[]{:S(2)}, u32[]{:S(2)}) %collective-permute-start.11) | collective-permute-done | bytes 225824 | tf_op jit(solution)/shard_map/ppermute | solution.py:58
  109.8 53.0 %all-gather = bf16[1344,336]{1,0:T(8,128)(2,1)} all-gather(bf16[168,336]{1,0:T(8,128)(2,1)} %bitcast.223), channel_id=2, replica_groups=mesh['zl'=8,'co'=2,'y'=4,'zh'=2,'x'=4] {'zl'}, dimensions={0}, use_global_device_ids=true | all-gather | bytes 1016064 | tf_op jit(solution)/shard_map/all_gather | solution.py:111
  166.1 3.0 reshape.214
  169.2 2.8 fusion.15
  179.6 2.5 collective-permute-done.16
  188.4 2.6 collective-permute-start.18
  194.4 4.1 %convolution_convert_fusion = bf16[1344,1008]{1,0:T(8,128)(2,1)S(1)} fusion(bf16[1344,1280]{1,0:T(8,128)(2,1)S(1)} %copy-done.4, bf16[512,1008]{0,1:T(8,128)(2,1)S(1)} %get-tuple-element.170, bf16[128,1008]{0,1:T(8,128)(2,1)S(1)} %broadcast_select_fusion.4, bf16[512,1008]{0,1:T(8,128)(2,1)S(1)} %get-tuple-element.169, bf16[128,1008]{0,1:T(8,128)(2,1)S(1)} %get-tuple-element.151), kind=kOutput, calls=%fused_computation | convolution fusion | flops 3479841792 | bytes 8730624 | tf_op jit(solution)/shard_map/dot_general | solution.py:22
  198.5 2.1 collective-permute-start.21
  206.5 2.6 collective-permute-start.23
  210.6 4.4 %collective-permute-start.36 = (bf16[88,1008]{1,0:T(8,128)(2,1)S(1)}, bf16[88,1008]{1,0:T(8,128)(2,1)S(1)}, u32[]{:S(2)}, u32[]{:S(2)}) collective-permute-start(bf16[88,1008]{1,0:T(8,128)(2,1)S(1)} %get-tuple-element.89), channel_id=1, source_target_pairs={{0,64},{64,128},{1,65},{65,129},{2,66},{66,130},{3,67},{67,131},{4... | collective-permute-start | bytes 532232 | tf_op jit(solution)/shard_map/ppermute | solution.py:82
  216.6 2.9 collective-permute-start.25
  221.7 2.5 collective-permute-start.38
  229.7 7.2 %all-to-all-start.2 = ((bf16[16,2,84,128]{3,1,2,0:T(2,128)(2,1)}), bf16[16,2,84,128]{3,1,2,0:T(2,128)(2,1)S(1)}, u32[]{:S(2)}, u32[]{:S(2)}) async-start(bf16[16,2,84,128]{3,1,2,0:T(2,128)(2,1)} %copy.73), calls=%async_computation.2 | async-start | bytes 1376256 | tf_op jit(solution)/shard_map/all_to_all | solution.py:170
  243.4 5.0 %collective-permute-start.42 = (bf16[88,1008]{1,0:T(8,128)(2,1)}, bf16[88,1008]{1,0:T(8,128)(2,1)}, u32[]{:S(2)}, u32[]{:S(2)}) collective-permute-start(bf16[88,1008]{1,0:T(8,128)(2,1)} %get-tuple-element.95), channel_id=1, source_target_pairs={{0,64},{64,128},{128,192},{192,256},{256,320},{1,65},{65,129},{129... | collective-permute-start | bytes 532232 | tf_op jit(solution)/shard_map/ppermute | solution.py:82
  253.9 4.4 %collective-permute-start.44 = (bf16[88,1008]{1,0:T(8,128)(2,1)S(1)}, bf16[88,1008]{1,0:T(8,128)(2,1)S(1)}, u32[]{:S(2)}, u32[]{:S(2)}) collective-permute-start(bf16[88,1008]{1,0:T(8,128)(2,1)S(1)} %get-tuple-element.97), channel_id=1, source_target_pairs={{0,64},{64,128},{128,192},{192,256},{256,320},{320,384},{1,65},{65... | collective-permute-start | bytes 532232 | tf_op jit(solution)/shard_map/ppermute | solution.py:82
  258.3 18.7 %collective-permute-start.45 = (bf16[88,1008]{1,0:T(8,128)(2,1)S(1)}, bf16[88,1008]{1,0:T(8,128)(2,1)S(1)}, u32[]{:S(2)}, u32[]{:S(2)}) collective-permute-start(bf16[88,1008]{1,0:T(8,128)(2,1)S(1)} %get-tuple-element.98), channel_id=1, source_target_pairs={{128,64},{192,128},{256,192},{320,256},{384,320},{448,384},{129,65... | collective-permute-start | bytes 532232 | tf_op jit(solution)/shard_map/ppermute | solution.py:83
  277.1 3.5 collective-permute-start.29
  281.3 13.3 %collective-permute-start.20 = (bf16[84,128]{1,0:T(8,128)(2,1)S(1)}, bf16[84,128]{1,0:T(8,128)(2,1)S(1)}, u32[]{:S(2)}, u32[]{:S(2)}) collective-permute-start(bf16[84,128]{1,0:T(8,128)(2,1)S(1)} %bitcast.224), channel_id=1, source_target_pairs={{0,4},{4,0},{1,5},{5,1},{2,6},{6,2},{3,7},{7,3},{8,12},{12,8},{9,1... | collective-permute-start | bytes 64520 | tf_op jit(solution)/shard_map/ppermute | solution.py:42
  296.8 3.3 collective-permute-start.31
  300.1 18.6 %collective-permute-start.32 = (bf16[80,1008]{1,0:T(8,128)(2,1)S(1)}, bf16[80,1008]{1,0:T(8,128)(2,1)S(1)}, u32[]{:S(2)}, u32[]{:S(2)}) collective-permute-start(bf16[80,1008]{1,0:T(8,128)(2,1)S(1)} %get-tuple-element.85), channel_id=1, source_target_pairs={{128,64},{192,128},{256,192},{320,256},{384,320},{448,384},{129,65... | collective-permute-start | bytes 483848 | tf_op jit(solution)/shard_map/ppermute | solution.py:83
  318.8 19.0 %collective-permute-start.46 = (bf16[88,1008]{1,0:T(8,128)(2,1)S(1)}, bf16[88,1008]{1,0:T(8,128)(2,1)S(1)}, u32[]{:S(2)}, u32[]{:S(2)}) collective-permute-start(bf16[88,1008]{1,0:T(8,128)(2,1)S(1)} %get-tuple-element.99), channel_id=1, source_target_pairs={{0,64},{64,128},{128,192},{192,256},{256,320},{320,384},{384,448},... | collective-permute-start | bytes 532232 | tf_op jit(solution)/shard_map/ppermute | solution.py:82
  337.8 18.4 %collective-permute-start.48 = (bf16[88,1008]{1,0:T(8,128)(2,1)S(1)}, bf16[88,1008]{1,0:T(8,128)(2,1)S(1)}, u32[]{:S(2)}, u32[]{:S(2)}) collective-permute-start(bf16[88,1008]{1,0:T(8,128)(2,1)S(1)} %get-tuple-element.101), channel_id=1, source_target_pairs={{64,0},{128,64},{192,128},{256,192},{320,256},{384,320},{448,384},... | collective-permute-start | bytes 532232 | tf_op jit(solution)/shard_map/ppermute | solution.py:83
  356.3 4.2 %collective-permute-start.33 = (bf16[80,1008]{1,0:T(8,128)(2,1)S(1)}, bf16[80,1008]{1,0:T(8,128)(2,1)S(1)}, u32[]{:S(2)}, u32[]{:S(2)}) collective-permute-start(bf16[80,1008]{1,0:T(8,128)(2,1)S(1)} %get-tuple-element.86), channel_id=1, source_target_pairs={{0,64},{64,128},{128,192},{192,256},{256,320},{320,384},{384,448},... | collective-permute-start | bytes 483848 | tf_op jit(solution)/shard_map/ppermute | solution.py:82
  364.2 4.1 %collective-permute-done.47 = bf16[80,1008]{1,0:T(8,128)(2,1)S(1)} collective-permute-done((bf16[80,1008]{1,0:T(8,128)(2,1)S(1)}, bf16[80,1008]{1,0:T(8,128)(2,1)S(1)}, u32[]{:S(2)}, u32[]{:S(2)}) %collective-permute-start.47) | collective-permute-done | bytes 161312 | tf_op jit(solution)/shard_map/ppermute | solution.py:83
  (215 shorter events, 84.4 us)
Async XLA Ops:
  4.1 46.8 %all-to-all-start = ((bf16[16,84,640]{2,1,0:T(8,128)(2,1)}), bf16[16,84,640]{2,1,0:T(8,128)(2,1)S(1)}, u32[]{:S(2)}, u32[]{:S(2)}) async-start(bf16[16,84,640]{2,1,0:T(8,128)(2,1)} %broadcast_in_dim.86), calls=%async_computation | async-start | bytes 3604480 | tf_op jit(solution)/shard_map/all_to_all | solution.py:103
  24.7 26.2 %collective-permute-start.2 = (bf16[168,672]{1,0:T(8,128)(2,1)S(1)}, bf16[168,672]{1,0:T(8,128)(2,1)S(1)}, u32[]{:S(2)}, u32[]{:S(2)}) collective-permute-start(bf16[168,672]{1,0:T(8,128)(2,1)S(1)} %collective-permute-done), channel_id=1, source_target_pairs={{64,128},{128,192},{192,256},{256,320},{320,384},{384,448},{65,129... | collective-permute-start | bytes 677384 | tf_op jit(solution)/shard_map/ppermute | solution.py:57
  25.3 25.5 %collective-permute-start.3 = (bf16[168,672]{1,0:T(8,128)(2,1)S(1)}, bf16[168,672]{1,0:T(8,128)(2,1)S(1)}, u32[]{:S(2)}, u32[]{:S(2)}) collective-permute-start(bf16[168,672]{1,0:T(8,128)(2,1)S(1)} %collective-permute-done.1), channel_id=1, source_target_pairs={{64,0},{128,64},{192,128},{256,192},{320,256},{384,320},{65,1},{12... | collective-permute-start | bytes 677384 | tf_op jit(solution)/shard_map/ppermute | solution.py:58
  26.6 24.2 %collective-permute-start.4 = (bf16[84,640]{1,0:T(8,128)(2,1)S(1)}, bf16[84,640]{1,0:T(8,128)(2,1)S(1)}, u32[]{:S(2)}, u32[]{:S(2)}) collective-permute-start(bf16[84,640]{1,0:T(8,128)(2,1)S(1)} %constant_dynamic-update-slice_fusion), channel_id=1, source_target_pairs={{0,4},{4,0},{1,5},{5,1},{2,6},{6,2},{3,7},{7,3},{8,12},{12,8},{9,1... | collective-permute-start | bytes 322568 | tf_op jit(solution)/shard_map/ppermute | solution.py:42
  52.7 50.1 %all-to-all-start.1 = ((bf16[16,84,640]{2,1,0:T(8,128)(2,1)}), bf16[16,84,640]{2,1,0:T(8,128)(2,1)S(1)}, u32[]{:S(2)}, u32[]{:S(2)}) async-start(bf16[16,84,640]{2,1,0:T(8,128)(2,1)} %broadcast_in_dim.87), calls=%async_computation.1 | async-start | bytes 3604480 | tf_op jit(solution)/shard_map/all_to_all | solution.py:103
  61.9 30.3 %collective-permute-start.9 = (bf16[4,2,84,640]{3,0,2,1:T(4,128)(2,1)S(1)}, bf16[4,2,84,640]{3,0,2,1:T(4,128)(2,1)S(1)}, u32[]{:S(2)}, u32[]{:S(2)}) collective-permute-start(bf16[4,2,84,640]{3,0,2,1:T(4,128)(2,1)S(1)} %copy.67), channel_id=1, source_target_pairs={{0,32},{32,0},{1,33},{33,1},{2,34},{34,2},{3,35},{35,3},{4,36},{36... | collective-permute-start | bytes 2580488 | tf_op jit(solution)/shard_map/ppermute | solution.py:42
  64.5 12.8 %collective-permute-start.6 = (bf16[168,672]{1,0:T(8,128)(2,1)S(1)}, bf16[168,672]{1,0:T(8,128)(2,1)S(1)}, u32[]{:S(2)}, u32[]{:S(2)}) collective-permute-start(bf16[168,672]{1,0:T(8,128)(2,1)S(1)} %collective-permute-done.3), channel_id=1, source_target_pairs={{64,0},{128,64},{192,128},{256,192},{320,256},{65,1},{129,65},{193... | collective-permute-start | bytes 677384 | tf_op jit(solution)/shard_map/ppermute | solution.py:58
  78.0 14.2 %collective-permute-start.8 = (bf16[168,672]{1,0:T(8,128)(2,1)S(1)}, bf16[168,672]{1,0:T(8,128)(2,1)S(1)}, u32[]{:S(2)}, u32[]{:S(2)}) collective-permute-start(bf16[168,672]{1,0:T(8,128)(2,1)S(1)} %collective-permute-done.6), channel_id=1, source_target_pairs={{64,0},{128,64},{192,128},{256,192},{65,1},{129,65},{193,129},{257... | collective-permute-start | bytes 677384 | tf_op jit(solution)/shard_map/ppermute | solution.py:58
  93.6 9.3 %collective-permute-start.11 = (bf16[168,672]{1,0:T(8,128)(2,1)S(1)}, bf16[168,672]{1,0:T(8,128)(2,1)}, u32[]{:S(2)}, u32[]{:S(2)}) collective-permute-start(bf16[168,672]{1,0:T(8,128)(2,1)S(1)} %collective-permute-done.8), channel_id=1, source_target_pairs={{64,0},{128,64},{192,128},{65,1},{129,65},{193,129},{66,2},{130,66... | collective-permute-start | bytes 677384 | tf_op jit(solution)/shard_map/ppermute | solution.py:58
  105.2 57.7 %collective-permute-start.14 = (bf16[4,2,84,640]{3,0,2,1:T(4,128)(2,1)}, bf16[4,2,84,640]{3,0,2,1:T(4,128)(2,1)S(1)}, u32[]{:S(2)}, u32[]{:S(2)}) collective-permute-start(bf16[4,2,84,640]{3,0,2,1:T(4,128)(2,1)} %copy.68), channel_id=1, source_target_pairs={{0,32},{32,0},{1,33},{33,1},{2,34},{34,2},{3,35},{35,3},{4,36},{36... | collective-permute-start | bytes 2580488 | tf_op jit(solution)/shard_map/ppermute | solution.py:42
  107.1 55.8 %collective-permute-start.12 = (bf16[168,672]{1,0:T(8,128)(2,1)}, bf16[168,672]{1,0:T(8,128)(2,1)}, u32[]{:S(2)}, u32[]{:S(2)}) collective-permute-start(bf16[168,672]{1,0:T(8,128)(2,1)} %collective-permute-done.10), channel_id=1, source_target_pairs={{320,384},{384,448},{321,385},{385,449},{322,386},{386,450},{323,3... | collective-permute-start | bytes 677384 | tf_op jit(solution)/shard_map/ppermute | solution.py:57
  108.5 54.4 %collective-permute-start.13 = (bf16[168,672]{1,0:T(8,128)(2,1)}, bf16[168,672]{1,0:T(8,128)(2,1)}, u32[]{:S(2)}, u32[]{:S(2)}) collective-permute-start(bf16[168,672]{1,0:T(8,128)(2,1)} %collective-permute-done.11), channel_id=1, source_target_pairs={{64,0},{128,64},{65,1},{129,65},{66,2},{130,66},{67,3},{131,67},{6... | collective-permute-start | bytes 677384 | tf_op jit(solution)/shard_map/ppermute | solution.py:58
  202.1 23.4 %collective-permute-start.19 = (bf16[1344,128]{1,0:T(8,128)(2,1)S(1)}, bf16[1344,128]{1,0:T(8,128)(2,1)S(1)}, u32[]{:S(2)}, u32[]{:S(2)}) collective-permute-start(bf16[1344,128]{1,0:T(8,128)(2,1)S(1)} %slice.114), channel_id=1, source_target_pairs={{0,32},{32,0},{1,33},{33,1},{2,34},{34,2},{3,35},{35,3},{4,36},{36... | collective-permute-start | bytes 1032200 | tf_op jit(solution)/shard_map/ppermute | solution.py:42
  206.5 9.2 %collective-permute-start.23 = (bf16[80,1008]{1,0:T(8,128)(2,1)S(1)}, bf16[80,1008]{1,0:T(8,128)(2,1)S(1)}, u32[]{:S(2)}, u32[]{:S(2)}) collective-permute-start(bf16[80,1008]{1,0:T(8,128)(2,1)S(1)} %get-tuple-element.76), channel_id=1, source_target_pairs={{0,64},{64,128},{1,65},{65,129},{2,66},{66,130},{3,67},{67,131},{4... | collective-permute-start | bytes 483848 | tf_op jit(solution)/shard_map/ppermute | solution.py:82
  210.6 10.1 %collective-permute-start.36 = (bf16[88,1008]{1,0:T(8,128)(2,1)S(1)}, bf16[88,1008]{1,0:T(8,128)(2,1)S(1)}, u32[]{:S(2)}, u32[]{:S(2)}) collective-permute-start(bf16[88,1008]{1,0:T(8,128)(2,1)S(1)} %get-tuple-element.89), channel_id=1, source_target_pairs={{0,64},{64,128},{1,65},{65,129},{2,66},{66,130},{3,67},{67,131},{4... | collective-permute-start | bytes 532232 | tf_op jit(solution)/shard_map/ppermute | solution.py:82
  216.6 23.7 %collective-permute-start.25 = (bf16[80,1008]{1,0:T(8,128)(2,1)}, bf16[80,1008]{1,0:T(8,128)(2,1)}, u32[]{:S(2)}, u32[]{:S(2)}) collective-permute-start(bf16[80,1008]{1,0:T(8,128)(2,1)} %get-tuple-element.78), channel_id=1, source_target_pairs={{0,64},{64,128},{128,192},{1,65},{65,129},{129,193},{2,66},{66,130... | collective-permute-start | bytes 483848 | tf_op jit(solution)/shard_map/ppermute | solution.py:82
  219.5 20.8 %collective-permute-start.26 = (bf16[80,1008]{1,0:T(8,128)(2,1)}, bf16[80,1008]{1,0:T(8,128)(2,1)}, u32[]{:S(2)}, u32[]{:S(2)}) collective-permute-start(bf16[80,1008]{1,0:T(8,128)(2,1)} %get-tuple-element.79), channel_id=1, source_target_pairs={{320,256},{384,320},{448,384},{321,257},{385,321},{449,385},{322,2... | collective-permute-start | bytes 483848 | tf_op jit(solution)/shard_map/ppermute | solution.py:83
  221.7 15.2 %collective-permute-start.38 = (bf16[88,1008]{1,0:T(8,128)(2,1)}, bf16[88,1008]{1,0:T(8,128)(2,1)}, u32[]{:S(2)}, u32[]{:S(2)}) collective-permute-start(bf16[88,1008]{1,0:T(8,128)(2,1)} %get-tuple-element.91), channel_id=1, source_target_pairs={{0,64},{64,128},{128,192},{1,65},{65,129},{129,193},{2,66},{66,130... | collective-permute-start | bytes 532232 | tf_op jit(solution)/shard_map/ppermute | solution.py:82
  224.1 12.8 %collective-permute-start.39 = (bf16[88,1008]{1,0:T(8,128)(2,1)}, bf16[88,1008]{1,0:T(8,128)(2,1)}, u32[]{:S(2)}, u32[]{:S(2)}) collective-permute-start(bf16[88,1008]{1,0:T(8,128)(2,1)} %get-tuple-element.92), channel_id=1, source_target_pairs={{320,256},{384,320},{448,384},{321,257},{385,321},{449,385},{322,2... | collective-permute-start | bytes 532232 | tf_op jit(solution)/shard_map/ppermute | solution.py:83
  229.7 20.2 %all-to-all-start.2 = ((bf16[16,2,84,128]{3,1,2,0:T(2,128)(2,1)}), bf16[16,2,84,128]{3,1,2,0:T(2,128)(2,1)S(1)}, u32[]{:S(2)}, u32[]{:S(2)}) async-start(bf16[16,2,84,128]{3,1,2,0:T(2,128)(2,1)} %copy.73), calls=%async_computation.2 | async-start | bytes 1376256 | tf_op jit(solution)/shard_map/all_to_all | solution.py:170
  243.4 9.3 %collective-permute-start.42 = (bf16[88,1008]{1,0:T(8,128)(2,1)}, bf16[88,1008]{1,0:T(8,128)(2,1)}, u32[]{:S(2)}, u32[]{:S(2)}) collective-permute-start(bf16[88,1008]{1,0:T(8,128)(2,1)} %get-tuple-element.95), channel_id=1, source_target_pairs={{0,64},{64,128},{128,192},{192,256},{256,320},{1,65},{65,129},{129... | collective-permute-start | bytes 532232 | tf_op jit(solution)/shard_map/ppermute | solution.py:82
  250.4 26.5 %collective-permute-start.27 = (bf16[80,1008]{1,0:T(8,128)(2,1)}, bf16[80,1008]{1,0:T(8,128)(2,1)S(1)}, u32[]{:S(2)}, u32[]{:S(2)}) collective-permute-start(bf16[80,1008]{1,0:T(8,128)(2,1)} %get-tuple-element.80), channel_id=1, source_target_pairs={{0,64},{64,128},{128,192},{192,256},{1,65},{65,129},{129,193},{193... | collective-permute-start | bytes 483848 | tf_op jit(solution)/shard_map/ppermute | solution.py:82
  251.7 25.2 %collective-permute-start.28 = (bf16[80,1008]{1,0:T(8,128)(2,1)}, bf16[80,1008]{1,0:T(8,128)(2,1)S(1)}, u32[]{:S(2)}, u32[]{:S(2)}) collective-permute-start(bf16[80,1008]{1,0:T(8,128)(2,1)} %get-tuple-element.81), channel_id=1, source_target_pairs={{256,192},{320,256},{384,320},{448,384},{257,193},{321,257},{385,3... | collective-permute-start | bytes 483848 | tf_op jit(solution)/shard_map/ppermute | solution.py:83
  253.9 64.8 %collective-permute-start.44 = (bf16[88,1008]{1,0:T(8,128)(2,1)S(1)}, bf16[88,1008]{1,0:T(8,128)(2,1)S(1)}, u32[]{:S(2)}, u32[]{:S(2)}) collective-permute-start(bf16[88,1008]{1,0:T(8,128)(2,1)S(1)} %get-tuple-element.97), channel_id=1, source_target_pairs={{0,64},{64,128},{128,192},{192,256},{256,320},{320,384},{1,65},{65... | collective-permute-start | bytes 532232 | tf_op jit(solution)/shard_map/ppermute | solution.py:82
  258.3 60.4 %collective-permute-start.45 = (bf16[88,1008]{1,0:T(8,128)(2,1)S(1)}, bf16[88,1008]{1,0:T(8,128)(2,1)S(1)}, u32[]{:S(2)}, u32[]{:S(2)}) collective-permute-start(bf16[88,1008]{1,0:T(8,128)(2,1)S(1)} %get-tuple-element.98), channel_id=1, source_target_pairs={{128,64},{192,128},{256,192},{320,256},{384,320},{448,384},{129,65... | collective-permute-start | bytes 532232 | tf_op jit(solution)/shard_map/ppermute | solution.py:83
  277.1 17.7 %collective-permute-start.29 = (bf16[80,1008]{1,0:T(8,128)(2,1)S(1)}, bf16[80,1008]{1,0:T(8,128)(2,1)S(1)}, u32[]{:S(2)}, u32[]{:S(2)}) collective-permute-start(bf16[80,1008]{1,0:T(8,128)(2,1)S(1)} %get-tuple-element.82), channel_id=1, source_target_pairs={{0,64},{64,128},{128,192},{192,256},{256,320},{1,65},{65,129},{129... | collective-permute-start | bytes 483848 | tf_op jit(solution)/shard_map/ppermute | solution.py:82
  280.6 14.2 %collective-permute-start.30 = (bf16[80,1008]{1,0:T(8,128)(2,1)S(1)}, bf16[80,1008]{1,0:T(8,128)(2,1)S(1)}, u32[]{:S(2)}, u32[]{:S(2)}) collective-permute-start(bf16[80,1008]{1,0:T(8,128)(2,1)S(1)} %get-tuple-element.83), channel_id=1, source_target_pairs={{192,128},{256,192},{320,256},{384,320},{448,384},{193,129},{257,1... | collective-permute-start | bytes 483848 | tf_op jit(solution)/shard_map/ppermute | solution.py:83
  281.3 15.4 %collective-permute-start.20 = (bf16[84,128]{1,0:T(8,128)(2,1)S(1)}, bf16[84,128]{1,0:T(8,128)(2,1)S(1)}, u32[]{:S(2)}, u32[]{:S(2)}) collective-permute-start(bf16[84,128]{1,0:T(8,128)(2,1)S(1)} %bitcast.224), channel_id=1, source_target_pairs={{0,4},{4,0},{1,5},{5,1},{2,6},{6,2},{3,7},{7,3},{8,12},{12,8},{9,1... | collective-permute-start | bytes 64520 | tf_op jit(solution)/shard_map/ppermute | solution.py:42
  296.8 59.4 %collective-permute-start.31 = (bf16[80,1008]{1,0:T(8,128)(2,1)S(1)}, bf16[80,1008]{1,0:T(8,128)(2,1)S(1)}, u32[]{:S(2)}, u32[]{:S(2)}) collective-permute-start(bf16[80,1008]{1,0:T(8,128)(2,1)S(1)} %get-tuple-element.84), channel_id=1, source_target_pairs={{0,64},{64,128},{128,192},{192,256},{256,320},{320,384},{1,65},{65... | collective-permute-start | bytes 483848 | tf_op jit(solution)/shard_map/ppermute | solution.py:82
  300.1 56.1 %collective-permute-start.32 = (bf16[80,1008]{1,0:T(8,128)(2,1)S(1)}, bf16[80,1008]{1,0:T(8,128)(2,1)S(1)}, u32[]{:S(2)}, u32[]{:S(2)}) collective-permute-start(bf16[80,1008]{1,0:T(8,128)(2,1)S(1)} %get-tuple-element.85), channel_id=1, source_target_pairs={{128,64},{192,128},{256,192},{320,256},{384,320},{448,384},{129,65... | collective-permute-start | bytes 483848 | tf_op jit(solution)/shard_map/ppermute | solution.py:83
  318.8 43.6 %collective-permute-start.46 = (bf16[88,1008]{1,0:T(8,128)(2,1)S(1)}, bf16[88,1008]{1,0:T(8,128)(2,1)S(1)}, u32[]{:S(2)}, u32[]{:S(2)}) collective-permute-start(bf16[88,1008]{1,0:T(8,128)(2,1)S(1)} %get-tuple-element.99), channel_id=1, source_target_pairs={{0,64},{64,128},{128,192},{192,256},{256,320},{320,384},{384,448},... | collective-permute-start | bytes 532232 | tf_op jit(solution)/shard_map/ppermute | solution.py:82
  337.8 25.5 %collective-permute-start.48 = (bf16[88,1008]{1,0:T(8,128)(2,1)S(1)}, bf16[88,1008]{1,0:T(8,128)(2,1)S(1)}, u32[]{:S(2)}, u32[]{:S(2)}) collective-permute-start(bf16[88,1008]{1,0:T(8,128)(2,1)S(1)} %get-tuple-element.101), channel_id=1, source_target_pairs={{64,0},{128,64},{192,128},{256,192},{320,256},{384,320},{448,384},... | collective-permute-start | bytes 532232 | tf_op jit(solution)/shard_map/ppermute | solution.py:83
  (51 other events, 676.2 us)

commit v4 on v2

--- a/solution.py
+++ b/solution.py
@@ -42,11 +42,96 @@
     return lax.ppermute(values, axis_name, [(0, 1), (1, 0)])
 
 
-def line_gather(shard, place, ties):
+def step_round(values, axis_name, by):
+    return lax.ppermute(values, axis_name, [(i, (i + by) % 4) for i in range(4)])
+
+
+def around(blocks, place):
+    twice = jnp.concatenate([blocks, blocks[:3]], 0)
+    return lax.dynamic_slice_in_dim(twice, (4 - place) % 4, 4, 0)
+
+
+class Beside:
+    def __init__(self, stages):
+        self.stages = stages
+        self.result = None
+        self.waiting = next(stages)
+
+    def resume(self, arrays):
+        if self.result is not None:
+            return
+        try:
+            self.waiting = self.stages.send(arrays)
+        except StopIteration as stop:
+            self.waiting, self.result = (), stop.value
+
+    def finish(self):
+        while self.result is None:
+            self.resume(self.waiting)
+        return self.result
+
+
+def gather_inputs(local, core):
+    y, x = lax.axis_index("y"), lax.axis_index("x")
+
+    def halves(blocks):
+        kept = lax.dynamic_slice_in_dim(blocks, 2 * core, 2, 1)
+        return kept, swap(lax.dynamic_slice_in_dim(blocks, 2 - 2 * core, 2, 1), "co")
+
+    far = swap(local, "zh")
+    right, left = step_round(local, "x", 1), step_round(local, "x", -1)
+    right, left = yield right, left
+    over = step_round(right, "x", 1)
+    over, far = yield over, far
+    near = around(jnp.stack([local, left, over, right]), x)
+    up, down = step_round(near, "y", 1), step_round(near, "y", -1)
+    right = step_round(far, "x", 1)
+    up, down, right = yield up, down, right
+    over_y = step_round(up, "y", 1)
+    left, over = step_round(far, "x", -1), step_round(right, "x", 1)
+    over_y, left, over = yield over_y, left, over
+    far = around(jnp.stack([far, left, over, right]), x)
+    kept, got = halves(jnp.stack([near, down, over_y, up]))
+    up, down = step_round(far, "y", 1), step_round(far, "y", -1)
+    up, down, got = yield up, down, got
+    over_y = step_round(up, "y", 1)
+    near = around(jnp.concatenate([kept, got], -1), y)
+    over_y, near = yield over_y, near
+    kept, got = halves(jnp.stack([far, down, over_y, up]))
+    (got,) = yield (got,)
+    return near, around(jnp.concatenate([kept, got], -1), y)
+
+
+def scatter_acts(partial, core):
+    tokens = partial.shape[1] // 2
+    half = lax.axis_index("zh")
+    kept, got = partial[:, :tokens], swap(partial[:, tokens:], "co")
+    (got,) = yield (got,)
+    blocks = in_order(kept, got, core, 0).reshape(2, 4, 2, 2, -1, tokens)
+    blocks = blocks.transpose(1, 0, 3, 2, 4, 5).reshape(4, 4, 2, -1, tokens)
+    for axis_name in ("y", "x"):
+        place = lax.axis_index(axis_name)
+        left = step_round(blocks[(place + 3) % 4].astype(jnp.bfloat16), axis_name, -1)
+        (left,) = yield (left,)
+        over = step_round(blocks[(place + 2) % 4].astype(jnp.bfloat16), axis_name, 1)
+        (over,) = yield (over,)
+        right = blocks[(place + 1) % 4].astype(jnp.float32) + over.astype(jnp.float32)
+        right = step_round(right.astype(jnp.bfloat16), axis_name, 1)
+        (right,) = yield (right,)
+        blocks = blocks[place].astype(jnp.float32) + left.astype(jnp.float32)
+        blocks = blocks + right.astype(jnp.float32)
+    away = swap(blocks[1 - half].astype(jnp.bfloat16), "zh")
+    (away,) = yield (away,)
+    return (blocks[half] + away.astype(jnp.float32)).astype(jnp.bfloat16).T
+
+
+def line_gather(shard, place, beside):
     from_left, from_right = [], []
     right = left = shard
     for step in range(ZL - 1):
-        right, left, _ = lax.optimization_barrier((right, left, ties.get(step, ())))
+        if step:
+            right, left, tied = lax.optimization_barrier((right, left, beside.waiting))
+            beside.resume(tied)
         right = lax.ppermute(right, "zl", [(i, i + 1) for i in range(step, ZL - 1)])
         left = lax.ppermute(left, "zl", [(i, i - 1) for i in range(1, ZL - step)])
         from_left.append(right)
@@ -55,55 +140,51 @@
     return lax.dynamic_slice_in_dim(slots, ZL - 1 - place, ZL, 0)
 
 
-def line_scatter(parts, place, ties):
-    right = left = None
-    for step in range(ZL - 1):
-        to_right = parts[jnp.clip(place + ZL - 1 - step, 0, ZL - 1)]
-        to_left = parts[jnp.clip(place - ZL + 1 + step, 0, ZL - 1)]
+def line_scatter(parts, place, beside):
+    rows = parts.shape[1]
+    cut = rows // 16 * 8
+    sent = []
+    for turn in range(2 * (ZL - 1)):
+        step = turn // 2
+        low, high = ((0, cut), (cut, rows))[turn % 2]
+        to_right = parts[jnp.clip(place + ZL - 1 - step, 0, ZL - 1), low:high]
+        to_left = parts[jnp.clip(place - ZL + 1 + step, 0, ZL - 1), low:high]
         if step:
-            to_right = to_right.astype(jnp.float32) + right.astype(jnp.float32)
-            to_left = to_left.astype(jnp.float32) + left.astype(jnp.float32)
+            to_right = to_right.astype(jnp.float32) + sent[turn - 2][0].astype(jnp.float32)
+            to_left = to_left.astype(jnp.float32) + sent[turn - 2][1].astype(jnp.float32)
         to_right, to_left = to_right.astype(jnp.bfloat16), to_left.astype(jnp.bfloat16)
-        to_right, to_left, _ = lax.optimization_barrier((to_right, to_left, ties.get(step, ())))
-        right = lax.ppermute(to_right, "zl", [(i, i + 1) for i in range(step + 1)])
-        left = lax.ppermute(to_left, "zl", [(i, i - 1) for i in range(ZL - 1 - step, ZL)])
-    return (
-        parts[place].astype(jnp.float32) + right.astype(jnp.float32) + left.astype(jnp.float32)
-    )
+        before = sent[turn - 3] if turn > 2 else ()
+        if turn:
+            to_right, to_left, before, tied = lax.optimization_barrier(
+                (to_right, to_left, before, beside.waiting)
+            )
+            beside.resume(tied)
+        sent.append(
+            (
+                lax.ppermute(to_right, "zl", [(i, i + 1) for i in range(step + 1)]),
+                lax.ppermute(to_left, "zl", [(i, i - 1) for i in range(ZL - 1 - step, ZL)]),
+            )
+        )
+    total = parts[place].astype(jnp.float32)
+    for way in range(2):
+        total = total + jnp.concatenate([sent[-2][way], sent[-1][way]], 0).astype(jnp.float32)
+    return total
 
 
 def per_device(acts, cotangents, w_gate, w_up, w_down, unit_rank):
     place = lax.axis_index("zl")
     core = lax.axis_index("co")
     half = lax.axis_index("zh")
-    tokens, features = acts.shape
+    tokens = acts.shape[0]
     units = unit_rank.shape[0]
     rows = w_gate.shape[0]
 
     local = jnp.concatenate([acts.T] + [part.T for part in suffix_sums(cotangents)], 1)
-    far_local = swap(local, "zh")
-
-    def spread(values):
-        copies = jnp.broadcast_to(values[None], (16,) + values.shape)
-        got = lax.all_to_all(copies, ("y", "x"), 0, 0)
-        return got.reshape((4, 2, 2) + values.shape)
-
-    def both_tokens(values):
-        kept = lax.dynamic_index_in_dim(values, core, 1, False)
-        given = lax.dynamic_index_in_dim(values, 1 - core, 1, False)
-        return kept, swap(given, "co")
-
-    near = spread(local)
-    near_parts = both_tokens(near)
-    far = spread(far_local)
-    far_parts = both_tokens(far)
-    ties = {1: (far_local,), 3: (near,), 4: near_parts, 5: (far,), 6: far_parts}
-
-    weights = line_gather(jnp.concatenate([w_gate, w_up, w_down.T], 1), place, ties)
+    beside = Beside(gather_inputs(local, core))
+    weights = line_gather(jnp.concatenate([w_gate, w_up, w_down.T], 1), place, beside)
     weights = weights.reshape(ZL * rows, 3 * units)
-    inputs = in_order(
-        jnp.concatenate(near_parts, -1), jnp.concatenate(far_parts, -1), half, 1
-    ).reshape(ZL * rows, 10 * tokens)
+    near, far = beside.finish()
+    inputs = in_order(near, far, half, 1).reshape(ZL * rows, 10 * tokens)
 
     band = (
         (unit_rank >= FF // 8).astype(jnp.int32)
@@ -140,16 +221,9 @@
 
     gate_up = jnp.concatenate([own[:, : 2 * units], other[:, : 2 * units]], 0)
     partial_acts = dot(weights[:, : 2 * units], gate_up, 1, 1).astype(jnp.bfloat16)
-    kept, given = partial_acts[:, :tokens], partial_acts[:, tokens:]
-    partial_acts = in_order(kept, swap(given, "co"), core, 0)
-    partial_acts = partial_acts.reshape(2, 4, 2, 2, features, tokens)
-    partial_acts = partial_acts.transpose(1, 0, 3, 2, 4, 5).reshape(16, 2, features, tokens)
-    shares = lax.all_to_all(partial_acts, ("y", "x"), 0, 0)
-    shares = jnp.sum(shares.astype(jnp.float32), 0)
-    away = swap(shares[1 - half].astype(jnp.bfloat16), "zh")
-    grad_acts = (shares[half] + away.astype(jnp.float32)).astype(jnp.bfloat16).T
-
-    grads = line_scatter(parts, place, {3: (shares,), 5: (away,)}).astype(jnp.bfloat16)
+    beside = Beside(scatter_acts(partial_acts, core))
+    grads = line_scatter(parts, place, beside).astype(jnp.bfloat16)
+    grad_acts = beside.finish()
     return (
         grad_acts,
         grads[:, :units],

time: 278 us -> 439 us (1.58)
  starting transfers between devices: 124 us -> 310 us
  local copies, waits for them, and re-layouts: 36.6 us -> 22.6 us
  waiting for transfers between devices: 81.5 us -> 70.4 us
  other arithmetic: 22.8 us -> 17.1 us
  matrix products: 9.36 us -> 13.9 us
    ppermute x7 -> x32, starting transfers between devices: 34 us -> 141 us  [the longest x14 81.7 us: line_scatter(): lax.ppermute(to_right, 'zl', [(i, i + 1) for i in range(step + 1)])]
    ppermute x7 -> x14, starting transfers between devices: 8.94 us -> 91.2 us  [line_scatter(): lax.ppermute(to_left, 'zl', [(i, i - 1) for i in range(ZL - 1 - step, ZL)])]
    all_to_all x3 -> x0, starting transfers between devices: 23.9 us -> none  [the longest x2 16.6 us: spread(): got = lax.all_to_all(copies, ('y', 'x'), 0, 0)]
    ppermute x7, starting transfers between devices: 9.12 us -> 26.1 us  [line_gather(): left = lax.ppermute(left, 'zl', [(i, i - 1) for i in range(1, ZL - step)])]
    ppermute x7 -> x32, waiting for transfers between devices: 12.8 us -> 23.4 us  [the longest x18 23.4 us: step_round(): lax.ppermute(values, axis_name, [(i, (i + by) % 4) for i in range(4)])]
    ppermute x7, waiting for transfers between devices: 42.7 us -> 33.9 us  [line_gather(): left = lax.ppermute(left, 'zl', [(i, i - 1) for i in range(1, ZL - step)])]
    unnamed x77 -> x84, local copies, waits for them, and re-layouts: 13.4 us -> 4.72 us
    convert_element_type x6 -> x12, other arithmetic: 11.1 us -> 3.28 us  [line_scatter(): to_left.astype(jnp.bfloat16)]
  transfers between devices with their start and end apart: 38 -> 67, of which waited for: 17 -> 18; matrix products, arithmetic and copies ran while one was open for 14% -> 6% of each run, Pallas kernels for 0% -> 0%
where the time goes in v4:
time: 439 us; the launch traced here: 437 us
  starting transfers between devices  310 us (71%)
  waiting for transfers between devices  70.4 us (16%)
  local copies, waits for them, and re-layouts  22.6 us (5%)
  other arithmetic  17.1 us (4%)
  matrix products  13.9 us (3%)
    ppermute x14, starting transfers between devices, line_scatter(): lax.ppermute(to_left, 'zl', [(i, i - 1) for i in range(ZL - 1 - step, ZL)])  91.2 us
    ppermute x14, starting transfers between devices, line_scatter(): lax.ppermute(to_right, 'zl', [(i, i + 1) for i in range(step + 1)])  81.7 us
    ppermute x18, starting transfers between devices, step_round(): lax.ppermute(values, axis_name, [(i, (i + by) % 4) for i in range(4)])  59.1 us
    ppermute x7, waiting for transfers between devices, line_gather(): left = lax.ppermute(left, 'zl', [(i, i - 1) for i in range(1, ZL - step)])  33.9 us
    ppermute x7, starting transfers between devices, swap(): return lax.ppermute(values, axis_name, [(0, 1), (1, 0)])  32.4 us
    ppermute x7, starting transfers between devices, line_gather(): left = lax.ppermute(left, 'zl', [(i, i - 1) for i in range(1, ZL - step)])  26.1 us
    ppermute x18, waiting for transfers between devices, step_round(): lax.ppermute(values, axis_name, [(i, (i + by) % 4) for i in range(4)])  23.4 us
    ppermute x7, starting transfers between devices, line_gather(): right = lax.ppermute(right, 'zl', [(i, i + 1) for i in range(step, ZL - 1)])  19.6 us
  transfers between devices with their start and end apart: 67, of which 18 were waited for; matrix products, arithmetic and copies ran while one was open for 6% of the time, Pallas kernels for 0%

profile of v4, /device:TPU:6, one launch (start us, length us, event | category | flops | bytes accessed | tf_op | source)
XLA Modules:
  0.0 436.5 jit_solution(16087446523625695640)
XLA Ops:
  1.8 3.8 collective-permute-start
  9.0 5.2 %collective-permute-start.2 = (bf16[84,640]{1,0:T(8,128)(2,1)S(1)}, bf16[84,640]{1,0:T(8,128)(2,1)S(1)}, u32[]{:S(2)}, u32[]{:S(2)}) collective-permute-start(bf16[84,640]{1,0:T(8,128)(2,1)S(1)} %constant_dynamic-update-slice_fusion), channel_id=1, source_target_pairs={{0,1},{1,2},{2,3},{3,0},{4,5},{5,6},{6,7},{7,4},{8,9},{9,10},{10,1... | collective-permute-start | bytes 322568 | tf_op jit(solution)/shard_map/ppermute | solution.py:46
  16.2 13.5 %collective-permute-start.7 = (bf16[84,640]{1,0:T(8,128)(2,1)S(1)}, bf16[84,640]{1,0:T(8,128)(2,1)S(1)}, u32[]{:S(2)}, u32[]{:S(2)}) collective-permute-start(bf16[84,640]{1,0:T(8,128)(2,1)S(1)} %constant_dynamic-update-slice_fusion), channel_id=1, source_target_pairs={{0,4},{4,0},{1,5},{5,1},{2,6},{6,2},{3,7},{7,3},{8,12},{12,8},{9,1... | collective-permute-start | bytes 322568 | tf_op jit(solution)/shard_map/ppermute | solution.py:42
  29.8 11.6 %collective-permute-start.4 = (bf16[168,1008]{1,0:T(8,128)(2,1)S(1)}, bf16[168,1008]{1,0:T(8,128)(2,1)S(1)}, u32[]{:S(2)}, u32[]{:S(2)}) collective-permute-start(bf16[168,1008]{1,0:T(8,128)(2,1)S(1)} %collective-permute-done), channel_id=1, source_target_pairs={{64,128},{128,192},{192,256},{256,320},{320,384},{384,448},{65,129... | collective-permute-start | bytes 1016072 | tf_op jit(solution)/shard_map/ppermute | solution.py:135
  41.4 18.4 %collective-permute-start.5 = (bf16[168,1008]{1,0:T(8,128)(2,1)S(1)}, bf16[168,1008]{1,0:T(8,128)(2,1)S(1)}, u32[]{:S(2)}, u32[]{:S(2)}) collective-permute-start(bf16[168,1008]{1,0:T(8,128)(2,1)S(1)} %collective-permute-done.1), channel_id=1, source_target_pairs={{64,0},{128,64},{192,128},{256,192},{320,256},{384,320},{65,1},{12... | collective-permute-start | bytes 1016072 | tf_op jit(solution)/shard_map/ppermute | solution.py:136
  59.8 6.1 %collective-permute-start.6 = (bf16[84,640]{1,0:T(8,128)(2,1)S(1)}, bf16[84,640]{1,0:T(8,128)(2,1)S(1)}, u32[]{:S(2)}, u32[]{:S(2)}) collective-permute-start(bf16[84,640]{1,0:T(8,128)(2,1)S(1)} %collective-permute-done.2), channel_id=1, source_target_pairs={{0,1},{1,2},{2,3},{3,0},{4,5},{5,6},{6,7},{7,4},{8,9},{9,10},{10,1... | collective-permute-start | bytes 322568 | tf_op jit(solution)/shard_map/ppermute | solution.py:46
  70.6 3.4 collective-permute-start.10
  74.0 3.6 collective-permute-start.11
  97.1 4.3 collective-permute-start.17
  104.1 5.3 %collective-permute-done.14 = bf16[168,1008]{1,0:T(8,128)(2,1)S(1)} collective-permute-done((bf16[168,1008]{1,0:T(8,128)(2,1)}, bf16[168,1008]{1,0:T(8,128)(2,1)S(1)}, u32[]{:S(2)}, u32[]{:S(2)}) %collective-permute-start.14) | collective-permute-done | bytes 338720 | tf_op jit(solution)/shard_map/ppermute | solution.py:136
  115.8 3.6 collective-permute-start.21
  121.5 10.5 %collective-permute-done.19 = bf16[168,1008]{1,0:T(8,128)(2,1)S(1)} collective-permute-done((bf16[168,1008]{1,0:T(8,128)(2,1)S(1)}, bf16[168,1008]{1,0:T(8,128)(2,1)S(1)}, u32[]{:S(2)}, u32[]{:S(2)}) %collective-permute-start.19) | collective-permute-done | bytes 338720 | tf_op jit(solution)/shard_map/ppermute | solution.py:136
  138.0 10.6 %collective-permute-done.24 = bf16[168,1008]{1,0:T(8,128)(2,1)S(1)} collective-permute-done((bf16[168,1008]{1,0:T(8,128)(2,1)}, bf16[168,1008]{1,0:T(8,128)(2,1)S(1)}, u32[]{:S(2)}, u32[]{:S(2)}) %collective-permute-start.24) | collective-permute-done | bytes 338720 | tf_op jit(solution)/shard_map/ppermute | solution.py:136
  168.7 3.6 copy.38
  172.3 7.5 %fusion.97 = f32[2,5,128,1008]{2,3,1,0:T(8,128)S(1)} fusion(bf16[2,5,128,1344]{3,2,1,0:T(8,128)(2,1)} %bitcast.304, bf16[1344,1008,1,1]{1,0,3,2:T(8,128)(2,1)} %bitcast.308), kind=kOutput, calls=%fused_computation.236 | convolution fusion | flops 3468165120 | bytes 11311104 | tf_op jit(solution)/shard_map/dot_general | solution.py:22
  200.1 4.0 convolution_convert_fusion
  216.1 4.8 %collective-permute-start.34 = (bf16[4,2,84,128]{3,2,1,0:T(8,128)(2,1)S(1)}, bf16[4,2,84,128]{3,2,1,0:T(8,128)(2,1)S(1)}, u32[]{:S(2)}, u32[]{:S(2)}) collective-permute-start(bf16[4,2,84,128]{3,2,1,0:T(8,128)(2,1)S(1)} %get-tuple-element.171), channel_id=1, source_target_pairs={{0,24},{8,0},{16,8},{24,16},{1,25},{9,1},{17,9},{25,17},{2,26},{10... | collective-permute-start | bytes 516104 | tf_op jit(solution)/shard_map/ppermute | solution.py:46
  235.3 4.6 %collective-permute-done.40 = bf16[4,2,84,128]{3,2,1,0:T(8,128)(2,1)S(1)} collective-permute-done((bf16[4,2,84,128]{3,2,1,0:T(8,128)(2,1)S(1)}, bf16[4,2,84,128]{3,2,1,0:T(8,128)(2,1)S(1)}, u32[]{:S(2)}, u32[]{:S(2)}) %collective-permute-start.40) | collective-permute-done | bytes 172064 | tf_op jit(solution)/shard_map/ppermute | solution.py:46
  240.0 4.3 collective-permute-start.48
  248.4 5.1 %collective-permute-done.43 = bf16[2,84,128]{2,1,0:T(8,128)(2,1)S(1)} collective-permute-done((bf16[2,84,128]{2,1,0:T(8,128)(2,1)S(1)}, bf16[2,84,128]{2,1,0:T(8,128)(2,1)S(1)}, u32[]{:S(2)}, u32[]{:S(2)}) %collective-permute-start.43) | collective-permute-done | bytes 43040 | tf_op jit(solution)/shard_map/ppermute | solution.py:46
  261.6 8.4 %collective-permute-start.52 = (bf16[84,128]{1,0:T(8,128)(2,1)S(1)}, bf16[84,128]{1,0:T(8,128)(2,1)S(1)}, u32[]{:S(2)}, u32[]{:S(2)}) collective-permute-start(bf16[84,128]{1,0:T(8,128)(2,1)S(1)} %fusion.90), channel_id=1, source_target_pairs={{0,4},{4,0},{1,5},{5,1},{2,6},{6,2},{3,7},{7,3},{8,12},{12,8},{9,1... | collective-permute-start | bytes 64520 | tf_op jit(solution)/shard_map/ppermute | solution.py:42
  278.3 10.5 %collective-permute-start.54 = (bf16[80,1008]{1,0:T(8,128)(2,1)S(1)}, bf16[80,1008]{1,0:T(8,128)(2,1)S(1)}, u32[]{:S(2)}, u32[]{:S(2)}) collective-permute-start(bf16[80,1008]{1,0:T(8,128)(2,1)S(1)} %get-tuple-element.113), channel_id=1, source_target_pairs={{192,128},{256,192},{320,256},{384,320},{448,384},{193,129},{257,1... | collective-permute-start | bytes 483848 | tf_op jit(solution)/shard_map/ppermute | solution.py:165
  289.0 3.5 collective-permute-start.59
  292.5 17.6 %collective-permute-start.60 = (bf16[88,1008]{1,0:T(8,128)(2,1)S(1)}, bf16[88,1008]{1,0:T(8,128)(2,1)S(1)}, u32[]{:S(2)}, u32[]{:S(2)}) collective-permute-start(bf16[88,1008]{1,0:T(8,128)(2,1)S(1)} %get-tuple-element.119), channel_id=1, source_target_pairs={{192,128},{256,192},{320,256},{384,320},{448,384},{193,129},{257,1... | collective-permute-start | bytes 532232 | tf_op jit(solution)/shard_map/ppermute | solution.py:165
  310.2 19.0 %collective-permute-start.57 = (bf16[80,1008]{1,0:T(8,128)(2,1)S(1)}, bf16[80,1008]{1,0:T(8,128)(2,1)S(1)}, u32[]{:S(2)}, u32[]{:S(2)}) collective-permute-start(bf16[80,1008]{1,0:T(8,128)(2,1)S(1)} %get-tuple-element.116), channel_id=1, source_target_pairs={{0,64},{64,128},{128,192},{192,256},{256,320},{320,384},{1,65},{65... | collective-permute-start | bytes 483848 | tf_op jit(solution)/shard_map/ppermute | solution.py:164
  329.2 18.4 %collective-permute-start.58 = (bf16[80,1008]{1,0:T(8,128)(2,1)S(1)}, bf16[80,1008]{1,0:T(8,128)(2,1)S(1)}, u32[]{:S(2)}, u32[]{:S(2)}) collective-permute-start(bf16[80,1008]{1,0:T(8,128)(2,1)S(1)} %get-tuple-element.117), channel_id=1, source_target_pairs={{128,64},{192,128},{256,192},{320,256},{384,320},{448,384},{129,65... | collective-permute-start | bytes 483848 | tf_op jit(solution)/shard_map/ppermute | solution.py:165
  347.7 19.0 %collective-permute-start.62 = (bf16[88,1008]{1,0:T(8,128)(2,1)S(1)}, bf16[88,1008]{1,0:T(8,128)(2,1)S(1)}, u32[]{:S(2)}, u32[]{:S(2)}) collective-permute-start(bf16[88,1008]{1,0:T(8,128)(2,1)S(1)} %get-tuple-element.121), channel_id=1, source_target_pairs={{0,64},{64,128},{128,192},{192,256},{256,320},{320,384},{1,65},{65... | collective-permute-start | bytes 532232 | tf_op jit(solution)/shard_map/ppermute | solution.py:164
  366.8 18.4 %collective-permute-start.63 = (bf16[88,1008]{1,0:T(8,128)(2,1)S(1)}, bf16[88,1008]{1,0:T(8,128)(2,1)S(1)}, u32[]{:S(2)}, u32[]{:S(2)}) collective-permute-start(bf16[88,1008]{1,0:T(8,128)(2,1)S(1)} %get-tuple-element.122), channel_id=1, source_target_pairs={{128,64},{192,128},{256,192},{320,256},{384,320},{448,384},{129,65... | collective-permute-start | bytes 532232 | tf_op jit(solution)/shard_map/ppermute | solution.py:165
  385.3 3.5 collective-permute-start.61
  390.2 19.7 %collective-permute-start.64 = (bf16[88,1008]{1,0:T(8,128)(2,1)S(1)}, bf16[88,1008]{1,0:T(8,128)(2,1)S(1)}, u32[]{:S(2)}, u32[]{:S(2)}) collective-permute-start(bf16[88,1008]{1,0:T(8,128)(2,1)S(1)} %get-tuple-element.123), channel_id=1, source_target_pairs={{0,64},{64,128},{128,192},{192,256},{256,320},{320,384},{384,448},... | collective-permute-start | bytes 532232 | tf_op jit(solution)/shard_map/ppermute | solution.py:164
  409.9 18.4 %collective-permute-start.66 = (bf16[88,1008]{1,0:T(8,128)(2,1)S(1)}, bf16[88,1008]{1,0:T(8,128)(2,1)S(1)}, u32[]{:S(2)}, u32[]{:S(2)}) collective-permute-start(bf16[88,1008]{1,0:T(8,128)(2,1)S(1)} %get-tuple-element.125), channel_id=1, source_target_pairs={{64,0},{128,64},{192,128},{256,192},{320,256},{384,320},{448,384},... | collective-permute-start | bytes 532232 | tf_op jit(solution)/shard_map/ppermute | solution.py:165
  428.9 6.5 %collective-permute-done.66 = bf16[88,1008]{1,0:T(8,128)(2,1)S(1)} collective-permute-done((bf16[88,1008]{1,0:T(8,128)(2,1)S(1)}, bf16[88,1008]{1,0:T(8,128)(2,1)S(1)}, u32[]{:S(2)}, u32[]{:S(2)}) %collective-permute-start.66) | collective-permute-done | bytes 177440 | tf_op jit(solution)/shard_map/ppermute | solution.py:165
  (261 shorter events, 137.2 us)
Async XLA Ops:
  1.8 27.9 %collective-permute-start = (bf16[168,1008]{1,0:T(8,128)(2,1)S(1)}, bf16[168,1008]{1,0:T(8,128)(2,1)S(1)}, u32[]{:S(2)}, u32[]{:S(2)}) collective-permute-start(bf16[168,1008]{1,0:T(8,128)(2,1)S(1)} %pad_maximum_fusion.4), channel_id=1, source_target_pairs={{0,64},{64,128},{128,192},{192,256},{256,320},{320,384},{384,448},... | collective-permute-start | bytes 1016072 | tf_op jit(solution)/shard_map/ppermute | solution.py:135
  5.7 24.1 %collective-permute-start.1 = (bf16[168,1008]{1,0:T(8,128)(2,1)S(1)}, bf16[168,1008]{1,0:T(8,128)(2,1)S(1)}, u32[]{:S(2)}, u32[]{:S(2)}) collective-permute-start(bf16[168,1008]{1,0:T(8,128)(2,1)S(1)} %pad_maximum_fusion.4), channel_id=1, source_target_pairs={{64,0},{128,64},{192,128},{256,192},{320,256},{384,320},{448,384},... | collective-permute-start | bytes 1016072 | tf_op jit(solution)/shard_map/ppermute | solution.py:136
  9.0 20.7 %collective-permute-start.2 = (bf16[84,640]{1,0:T(8,128)(2,1)S(1)}, bf16[84,640]{1,0:T(8,128)(2,1)S(1)}, u32[]{:S(2)}, u32[]{:S(2)}) collective-permute-start(bf16[84,640]{1,0:T(8,128)(2,1)S(1)} %constant_dynamic-update-slice_fusion), channel_id=1, source_target_pairs={{0,1},{1,2},{2,3},{3,0},{4,5},{5,6},{6,7},{7,4},{8,9},{9,10},{10,1... | collective-permute-start | bytes 322568 | tf_op jit(solution)/shard_map/ppermute | solution.py:46
  14.3 15.5 %collective-permute-start.3 = (bf16[84,640]{1,0:T(8,128)(2,1)S(1)}, bf16[84,640]{1,0:T(8,128)(2,1)S(1)}, u32[]{:S(2)}, u32[]{:S(2)}) collective-permute-start(bf16[84,640]{1,0:T(8,128)(2,1)S(1)} %constant_dynamic-update-slice_fusion), channel_id=1, source_target_pairs={{0,3},{1,0},{2,1},{3,2},{4,7},{5,4},{6,5},{7,6},{8,11},{9,8},{10,9... | collective-permute-start | bytes 322568 | tf_op jit(solution)/shard_map/ppermute | solution.py:46
  16.2 49.7 %collective-permute-start.7 = (bf16[84,640]{1,0:T(8,128)(2,1)S(1)}, bf16[84,640]{1,0:T(8,128)(2,1)S(1)}, u32[]{:S(2)}, u32[]{:S(2)}) collective-permute-start(bf16[84,640]{1,0:T(8,128)(2,1)S(1)} %constant_dynamic-update-slice_fusion), channel_id=1, source_target_pairs={{0,4},{4,0},{1,5},{5,1},{2,6},{6,2},{3,7},{7,3},{8,12},{12,8},{9,1... | collective-permute-start | bytes 322568 | tf_op jit(solution)/shard_map/ppermute | solution.py:42
  29.8 38.5 %collective-permute-start.4 = (bf16[168,1008]{1,0:T(8,128)(2,1)S(1)}, bf16[168,1008]{1,0:T(8,128)(2,1)S(1)}, u32[]{:S(2)}, u32[]{:S(2)}) collective-permute-start(bf16[168,1008]{1,0:T(8,128)(2,1)S(1)} %collective-permute-done), channel_id=1, source_target_pairs={{64,128},{128,192},{192,256},{256,320},{320,384},{384,448},{65,129... | collective-permute-start | bytes 1016072 | tf_op jit(solution)/shard_map/ppermute | solution.py:135
  41.4 29.0 %collective-permute-start.5 = (bf16[168,1008]{1,0:T(8,128)(2,1)S(1)}, bf16[168,1008]{1,0:T(8,128)(2,1)S(1)}, u32[]{:S(2)}, u32[]{:S(2)}) collective-permute-start(bf16[168,1008]{1,0:T(8,128)(2,1)S(1)} %collective-permute-done.1), channel_id=1, source_target_pairs={{64,0},{128,64},{192,128},{256,192},{320,256},{384,320},{65,1},{12... | collective-permute-start | bytes 1016072 | tf_op jit(solution)/shard_map/ppermute | solution.py:136
  70.6 19.5 %collective-permute-start.10 = (bf16[4,84,640]{2,1,0:T(8,128)(2,1)S(1)}, bf16[4,84,640]{2,1,0:T(8,128)(2,1)S(1)}, u32[]{:S(2)}, u32[]{:S(2)}) collective-permute-start(bf16[4,84,640]{2,1,0:T(8,128)(2,1)S(1)} %constant_dynamic-slice_fusion.6), channel_id=1, source_target_pairs={{0,8},{8,16},{16,24},{24,0},{1,9},{9,17},{17,25},{25,1},{2,10},{10... | collective-permute-start | bytes 1290248 | tf_op jit(solution)/shard_map/ppermute | solution.py:46
  74.0 16.1 %collective-permute-start.11 = (bf16[4,84,640]{2,1,0:T(8,128)(2,1)S(1)}, bf16[4,84,640]{2,1,0:T(8,128)(2,1)S(1)}, u32[]{:S(2)}, u32[]{:S(2)}) collective-permute-start(bf16[4,84,640]{2,1,0:T(8,128)(2,1)S(1)} %constant_dynamic-slice_fusion.6), channel_id=1, source_target_pairs={{0,24},{8,0},{16,8},{24,16},{1,25},{9,1},{17,9},{25,17},{2,26},{10... | collective-permute-start | bytes 1290248 | tf_op jit(solution)/shard_map/ppermute | solution.py:46
  90.1 19.3 %collective-permute-start.15 = (bf16[4,84,640]{2,1,0:T(8,128)(2,1)S(1)}, bf16[4,84,640]{2,1,0:T(8,128)(2,1)S(1)}, u32[]{:S(2)}, u32[]{:S(2)}) collective-permute-start(bf16[4,84,640]{2,1,0:T(8,128)(2,1)S(1)} %collective-permute-done.10), channel_id=1, source_target_pairs={{0,8},{8,16},{16,24},{24,0},{1,9},{9,17},{17,25},{25,1},{2,10},{10... | collective-permute-start | bytes 1290248 | tf_op jit(solution)/shard_map/ppermute | solution.py:46
  110.2 21.7 %collective-permute-start.22 = (bf16[4,2,84,640]{3,0,2,1:T(4,128)(2,1)S(1)}, bf16[4,2,84,640]{3,0,2,1:T(4,128)(2,1)S(1)}, u32[]{:S(2)}, u32[]{:S(2)}) collective-permute-start(bf16[4,2,84,640]{3,0,2,1:T(4,128)(2,1)S(1)} %copy.33), channel_id=1, source_target_pairs={{0,32},{32,0},{1,33},{33,1},{2,34},{34,2},{3,35},{35,3},{4,36},{36... | collective-permute-start | bytes 2580488 | tf_op jit(solution)/shard_map/ppermute | solution.py:42
  112.4 19.6 %collective-permute-start.20 = (bf16[4,84,640]{2,1,0:T(8,128)(2,1)S(1)}, bf16[4,84,640]{2,1,0:T(8,128)(2,1)S(1)}, u32[]{:S(2)}, u32[]{:S(2)}) collective-permute-start(bf16[4,84,640]{2,1,0:T(8,128)(2,1)S(1)} %constant_dynamic-slice_fusion.5), channel_id=1, source_target_pairs={{0,8},{8,16},{16,24},{24,0},{1,9},{9,17},{17,25},{25,1},{2,10},{10... | collective-permute-start | bytes 1290248 | tf_op jit(solution)/shard_map/ppermute | solution.py:46
  115.8 16.1 %collective-permute-start.21 = (bf16[4,84,640]{2,1,0:T(8,128)(2,1)S(1)}, bf16[4,84,640]{2,1,0:T(8,128)(2,1)S(1)}, u32[]{:S(2)}, u32[]{:S(2)}) collective-permute-start(bf16[4,84,640]{2,1,0:T(8,128)(2,1)S(1)} %constant_dynamic-slice_fusion.5), channel_id=1, source_target_pairs={{0,24},{8,0},{16,8},{24,16},{1,25},{9,1},{17,9},{25,17},{2,26},{10... | collective-permute-start | bytes 1290248 | tf_op jit(solution)/shard_map/ppermute | solution.py:46
  132.7 16.0 %collective-permute-start.25 = (bf16[4,84,640]{2,1,0:T(8,128)(2,1)S(1)}, bf16[4,84,640]{2,1,0:T(8,128)(2,1)}, u32[]{:S(2)}, u32[]{:S(2)}) collective-permute-start(bf16[4,84,640]{2,1,0:T(8,128)(2,1)S(1)} %collective-permute-done.20), channel_id=1, source_target_pairs={{0,8},{8,16},{16,24},{24,0},{1,9},{9,17},{17,25},{25,1},{2,10},{10... | collective-permute-start | bytes 1290248 | tf_op jit(solution)/shard_map/ppermute | solution.py:46
  193.5 17.0 %collective-permute-start.31 = (bf16[1344,128]{1,0:T(8,128)(2,1)S(1)}, bf16[1344,128]{1,0:T(8,128)(2,1)S(1)}, u32[]{:S(2)}, u32[]{:S(2)}) collective-permute-start(bf16[1344,128]{1,0:T(8,128)(2,1)S(1)} %slice.122), channel_id=1, source_target_pairs={{0,32},{32,0},{1,33},{33,1},{2,34},{34,2},{3,35},{35,3},{4,36},{36... | collective-permute-start | bytes 1032200 | tf_op jit(solution)/shard_map/ppermute | solution.py:42
  205.0 16.0 %collective-permute-start.32 = (bf16[80,1008]{1,0:T(8,128)(2,1)}, bf16[80,1008]{1,0:T(8,128)(2,1)}, u32[]{:S(2)}, u32[]{:S(2)}) collective-permute-start(bf16[80,1008]{1,0:T(8,128)(2,1)} %get-tuple-element.163), channel_id=1, source_target_pairs={{0,64},{1,65},{2,66},{3,67},{4,68},{5,69},{6,70},{7,71},{8,72},{9,... | collective-permute-start | bytes 483848 | tf_op jit(solution)/shard_map/ppermute | solution.py:164
  210.5 16.3 %collective-permute-start.37 = (bf16[88,1008]{1,0:T(8,128)(2,1)}, bf16[88,1008]{1,0:T(8,128)(2,1)}, u32[]{:S(2)}, u32[]{:S(2)}) collective-permute-start(bf16[88,1008]{1,0:T(8,128)(2,1)} %get-tuple-element.96), channel_id=1, source_target_pairs={{0,64},{1,65},{2,66},{3,67},{4,68},{5,69},{6,70},{7,71},{8,72},{9,... | collective-permute-start | bytes 532232 | tf_op jit(solution)/shard_map/ppermute | solution.py:164
  240.0 15.6 %collective-permute-start.48 = (bf16[2,84,128]{2,1,0:T(8,128)(2,1)S(1)}, bf16[2,84,128]{2,1,0:T(8,128)(2,1)S(1)}, u32[]{:S(2)}, u32[]{:S(2)}) collective-permute-start(bf16[2,84,128]{2,1,0:T(8,128)(2,1)S(1)} %get-tuple-element.175), channel_id=1, source_target_pairs={{0,1},{1,2},{2,3},{3,0},{4,5},{5,6},{6,7},{7,4},{8,9},{9,10},{10,1... | collective-permute-start | bytes 129032 | tf_op jit(solution)/shard_map/ppermute | solution.py:46
  270.0 18.8 %collective-permute-start.55 = (bf16[88,1008]{1,0:T(8,128)(2,1)S(1)}, bf16[88,1008]{1,0:T(8,128)(2,1)S(1)}, u32[]{:S(2)}, u32[]{:S(2)}) collective-permute-start(bf16[88,1008]{1,0:T(8,128)(2,1)S(1)} %get-tuple-element.114), channel_id=1, source_target_pairs={{0,64},{64,128},{128,192},{192,256},{1,65},{65,129},{129,193},{193... | collective-permute-start | bytes 532232 | tf_op jit(solution)/shard_map/ppermute | solution.py:164
  272.2 16.6 %collective-permute-start.56 = (bf16[88,1008]{1,0:T(8,128)(2,1)S(1)}, bf16[88,1008]{1,0:T(8,128)(2,1)S(1)}, u32[]{:S(2)}, u32[]{:S(2)}) collective-permute-start(bf16[88,1008]{1,0:T(8,128)(2,1)S(1)} %get-tuple-element.115), channel_id=1, source_target_pairs={{256,192},{320,256},{384,320},{448,384},{257,193},{321,257},{385,3... | collective-permute-start | bytes 532232 | tf_op jit(solution)/shard_map/ppermute | solution.py:165
  276.1 34.0 %collective-permute-start.53 = (bf16[80,1008]{1,0:T(8,128)(2,1)S(1)}, bf16[80,1008]{1,0:T(8,128)(2,1)S(1)}, u32[]{:S(2)}, u32[]{:S(2)}) collective-permute-start(bf16[80,1008]{1,0:T(8,128)(2,1)S(1)} %get-tuple-element.112), channel_id=1, source_target_pairs={{0,64},{64,128},{128,192},{192,256},{256,320},{1,65},{65,129},{129... | collective-permute-start | bytes 483848 | tf_op jit(solution)/shard_map/ppermute | solution.py:164
  278.3 31.8 %collective-permute-start.54 = (bf16[80,1008]{1,0:T(8,128)(2,1)S(1)}, bf16[80,1008]{1,0:T(8,128)(2,1)S(1)}, u32[]{:S(2)}, u32[]{:S(2)}) collective-permute-start(bf16[80,1008]{1,0:T(8,128)(2,1)S(1)} %get-tuple-element.113), channel_id=1, source_target_pairs={{192,128},{256,192},{320,256},{384,320},{448,384},{193,129},{257,1... | collective-permute-start | bytes 483848 | tf_op jit(solution)/shard_map/ppermute | solution.py:165
  289.0 58.7 %collective-permute-start.59 = (bf16[88,1008]{1,0:T(8,128)(2,1)S(1)}, bf16[88,1008]{1,0:T(8,128)(2,1)S(1)}, u32[]{:S(2)}, u32[]{:S(2)}) collective-permute-start(bf16[88,1008]{1,0:T(8,128)(2,1)S(1)} %get-tuple-element.118), channel_id=1, source_target_pairs={{0,64},{64,128},{128,192},{192,256},{256,320},{1,65},{65,129},{129... | collective-permute-start | bytes 532232 | tf_op jit(solution)/shard_map/ppermute | solution.py:164
  292.5 55.1 %collective-permute-start.60 = (bf16[88,1008]{1,0:T(8,128)(2,1)S(1)}, bf16[88,1008]{1,0:T(8,128)(2,1)S(1)}, u32[]{:S(2)}, u32[]{:S(2)}) collective-permute-start(bf16[88,1008]{1,0:T(8,128)(2,1)S(1)} %get-tuple-element.119), channel_id=1, source_target_pairs={{192,128},{256,192},{320,256},{384,320},{448,384},{193,129},{257,1... | collective-permute-start | bytes 532232 | tf_op jit(solution)/shard_map/ppermute | solution.py:165
  310.2 74.9 %collective-permute-start.57 = (bf16[80,1008]{1,0:T(8,128)(2,1)S(1)}, bf16[80,1008]{1,0:T(8,128)(2,1)S(1)}, u32[]{:S(2)}, u32[]{:S(2)}) collective-permute-start(bf16[80,1008]{1,0:T(8,128)(2,1)S(1)} %get-tuple-element.116), channel_id=1, source_target_pairs={{0,64},{64,128},{128,192},{192,256},{256,320},{320,384},{1,65},{65... | collective-permute-start | bytes 483848 | tf_op jit(solution)/shard_map/ppermute | solution.py:164
  329.2 55.9 %collective-permute-start.58 = (bf16[80,1008]{1,0:T(8,128)(2,1)S(1)}, bf16[80,1008]{1,0:T(8,128)(2,1)S(1)}, u32[]{:S(2)}, u32[]{:S(2)}) collective-permute-start(bf16[80,1008]{1,0:T(8,128)(2,1)S(1)} %get-tuple-element.117), channel_id=1, source_target_pairs={{128,64},{192,128},{256,192},{320,256},{384,320},{448,384},{129,65... | collective-permute-start | bytes 483848 | tf_op jit(solution)/shard_map/ppermute | solution.py:165
  347.7 42.3 %collective-permute-start.62 = (bf16[88,1008]{1,0:T(8,128)(2,1)S(1)}, bf16[88,1008]{1,0:T(8,128)(2,1)S(1)}, u32[]{:S(2)}, u32[]{:S(2)}) collective-permute-start(bf16[88,1008]{1,0:T(8,128)(2,1)S(1)} %get-tuple-element.121), channel_id=1, source_target_pairs={{0,64},{64,128},{128,192},{192,256},{256,320},{320,384},{1,65},{65... | collective-permute-start | bytes 532232 | tf_op jit(solution)/shard_map/ppermute | solution.py:164
  366.8 23.3 %collective-permute-start.63 = (bf16[88,1008]{1,0:T(8,128)(2,1)S(1)}, bf16[88,1008]{1,0:T(8,128)(2,1)S(1)}, u32[]{:S(2)}, u32[]{:S(2)}) collective-permute-start(bf16[88,1008]{1,0:T(8,128)(2,1)S(1)} %get-tuple-element.122), channel_id=1, source_target_pairs={{128,64},{192,128},{256,192},{320,256},{384,320},{448,384},{129,65... | collective-permute-start | bytes 532232 | tf_op jit(solution)/shard_map/ppermute | solution.py:165
  385.3 43.7 %collective-permute-start.61 = (bf16[80,1008]{1,0:T(8,128)(2,1)S(1)}, bf16[80,1008]{1,0:T(8,128)(2,1)S(1)}, u32[]{:S(2)}, u32[]{:S(2)}) collective-permute-start(bf16[80,1008]{1,0:T(8,128)(2,1)S(1)} %get-tuple-element.120), channel_id=1, source_target_pairs={{0,64},{64,128},{128,192},{192,256},{256,320},{320,384},{384,448},... | collective-permute-start | bytes 483848 | tf_op jit(solution)/shard_map/ppermute | solution.py:164
  388.8 40.1 %collective-permute-start.65 = (bf16[80,1008]{1,0:T(8,128)(2,1)S(1)}, bf16[80,1008]{1,0:T(8,128)(2,1)S(1)}, u32[]{:S(2)}, u32[]{:S(2)}) collective-permute-start(bf16[80,1008]{1,0:T(8,128)(2,1)S(1)} %get-tuple-element.124), channel_id=1, source_target_pairs={{64,0},{128,64},{192,128},{256,192},{320,256},{384,320},{448,384},... | collective-permute-start | bytes 483848 | tf_op jit(solution)/shard_map/ppermute | solution.py:165
  390.2 38.7 %collective-permute-start.64 = (bf16[88,1008]{1,0:T(8,128)(2,1)S(1)}, bf16[88,1008]{1,0:T(8,128)(2,1)S(1)}, u32[]{:S(2)}, u32[]{:S(2)}) collective-permute-start(bf16[88,1008]{1,0:T(8,128)(2,1)S(1)} %get-tuple-element.123), channel_id=1, source_target_pairs={{0,64},{64,128},{128,192},{192,256},{256,320},{320,384},{384,448},... | collective-permute-start | bytes 532232 | tf_op jit(solution)/shard_map/ppermute | solution.py:164
  409.9 25.5 %collective-permute-start.66 = (bf16[88,1008]{1,0:T(8,128)(2,1)S(1)}, bf16[88,1008]{1,0:T(8,128)(2,1)S(1)}, u32[]{:S(2)}, u32[]{:S(2)}) collective-permute-start(bf16[88,1008]{1,0:T(8,128)(2,1)S(1)} %get-tuple-element.125), channel_id=1, source_target_pairs={{64,0},{128,64},{192,128},{256,192},{320,256},{384,320},{448,384},... | collective-permute-start | bytes 532232 | tf_op jit(solution)/shard_map/ppermute | solution.py:165
  (64 other events, 619.6 us)

commit v5 on v4

--- a/solution.py
+++ b/solution.py
@@ -40,6 +40,10 @@
 
 def swap(values, axis_name):
     return lax.ppermute(values, axis_name, [(0, 1), (1, 0)])
+
+
+def line_step(values, by):
+    return lax.ppermute(values, "zl", [(i, i + by) for i in range(ZL) if 0 <= i + by < ZL])
 
 
 def step_round(values, axis_name, by):
@@ -132,8 +136,8 @@
         if step:
             right, left, tied = lax.optimization_barrier((right, left, beside.waiting))
             beside.resume(tied)
-        right = lax.ppermute(right, "zl", [(i, i + 1) for i in range(step, ZL - 1)])
-        left = lax.ppermute(left, "zl", [(i, i - 1) for i in range(1, ZL - step)])
+        right = line_step(right, 1)
+        left = line_step(left, -1)
         from_left.append(right)
         from_right.append(left)
     slots = jnp.stack(from_left[::-1] + [shard] + from_right)
@@ -161,8 +165,8 @@
             beside.resume(tied)
         sent.append(
             (
-                lax.ppermute(to_right, "zl", [(i, i + 1) for i in range(step + 1)]),
-                lax.ppermute(to_left, "zl", [(i, i - 1) for i in range(ZL - 1 - step, ZL)]),
+                line_step(to_right, 1),
+                line_step(to_left, -1),
             )
         )
     total = parts[place].astype(jnp.float32)

time: 439 us -> 336 us (0.77)
  the two profiles are of different devices: /device:TPU:6 before, /device:TPU:116 now
where the time goes in v5:
time: 336 us; the launch traced here: 333 us
  starting transfers between devices  227 us (68%)
  waiting for transfers between devices  49.7 us (15%)
  local copies, waits for them, and re-layouts  22.7 us (7%)
  other arithmetic  17.1 us (5%)
  matrix products  13.8 us (4%)
    ppermute x42, starting transfers between devices, line_step(): lax.ppermute(values, 'zl', [(i, i + by) for i in range(ZL) if 0 <= i + by...  139 us
    ppermute x18, starting transfers between devices, step_round(): lax.ppermute(values, axis_name, [(i, (i + by) % 4) for i in range(4)])  57.8 us
    ppermute x42, waiting for transfers between devices, line_step(): lax.ppermute(values, 'zl', [(i, i + by) for i in range(ZL) if 0 <= i + by...  31.2 us
    ppermute x7, starting transfers between devices, swap(): return lax.ppermute(values, axis_name, [(0, 1), (1, 0)])  30.2 us
    ppermute x18, waiting for transfers between devices, step_round(): lax.ppermute(values, axis_name, [(i, (i + by) % 4) for i in range(4)])  15.1 us
    dot_general x3, matrix products, dot(): lax.dot_general(left, right, (((left_dim,), (right_dim,)), ((), ())), pre...  13.8 us
  transfers between devices with their start and end apart: 67, of which 16 were waited for; matrix products, arithmetic and copies ran while one was open for 8% of the time, Pallas kernels for 0%

profile of v5, /device:TPU:116, one launch (start us, length us, event | category | flops | bytes accessed | tf_op | source)
XLA Modules:
  0.0 333.5 jit_solution(15629142122886492103)
XLA Ops:
  1.8 5.0 %collective-permute-start = (bf16[168,1008]{1,0:T(8,128)(2,1)S(1)}, bf16[168,1008]{1,0:T(8,128)(2,1)S(1)}, u32[]{:S(2)}, u32[]{:S(2)}) collective-permute-start(bf16[168,1008]{1,0:T(8,128)(2,1)S(1)} %pad_maximum_fusion.4), channel_id=1, source_target_pairs={{0,64},{64,128},{128,192},{192,256},{256,320},{320,384},{384,448},... | collective-permute-start | bytes 1016072 | tf_op jit(solution)/shard_map/ppermute | solution.py:46
  16.7 11.9 %collective-permute-start.7 = (bf16[84,640]{1,0:T(8,128)(2,1)S(1)}, bf16[84,640]{1,0:T(8,128)(2,1)S(1)}, u32[]{:S(2)}, u32[]{:S(2)}) collective-permute-start(bf16[84,640]{1,0:T(8,128)(2,1)S(1)} %constant_dynamic-update-slice_fusion), channel_id=1, source_target_pairs={{0,4},{4,0},{1,5},{5,1},{2,6},{6,2},{3,7},{7,3},{8,12},{12,8},{9,1... | collective-permute-start | bytes 322568 | tf_op jit(solution)/shard_map/ppermute | solution.py:42
  28.7 4.1 %collective-permute-start.4 = (bf16[168,1008]{1,0:T(8,128)(2,1)S(1)}, bf16[168,1008]{1,0:T(8,128)(2,1)S(1)}, u32[]{:S(2)}, u32[]{:S(2)}) collective-permute-start(bf16[168,1008]{1,0:T(8,128)(2,1)S(1)} %collective-permute-done), channel_id=1, source_target_pairs={{0,64},{64,128},{128,192},{192,256},{256,320},{320,384},{384,448},... | collective-permute-start | bytes 1016072 | tf_op jit(solution)/shard_map/ppermute | solution.py:46
  41.5 4.0 %collective-permute-done.4 = bf16[168,1008]{1,0:T(8,128)(2,1)S(1)} collective-permute-done((bf16[168,1008]{1,0:T(8,128)(2,1)S(1)}, bf16[168,1008]{1,0:T(8,128)(2,1)S(1)}, u32[]{:S(2)}, u32[]{:S(2)}) %collective-permute-start.4) | collective-permute-done | bytes 338720 | tf_op jit(solution)/shard_map/ppermute | solution.py:46
  51.6 4.6 %collective-permute-start.8 = (bf16[168,1008]{1,0:T(8,128)(2,1)S(1)}, bf16[168,1008]{1,0:T(8,128)(2,1)}, u32[]{:S(2)}, u32[]{:S(2)}) collective-permute-start(bf16[168,1008]{1,0:T(8,128)(2,1)S(1)} %collective-permute-done.4), channel_id=1, source_target_pairs={{0,64},{64,128},{128,192},{192,256},{256,320},{320,384},{384,448},... | collective-permute-start | bytes 1016072 | tf_op jit(solution)/shard_map/ppermute | solution.py:46
  75.7 3.9 %collective-permute-start.14 = (bf16[168,1008]{1,0:T(8,128)(2,1)}, bf16[168,1008]{1,0:T(8,128)(2,1)S(1)}, u32[]{:S(2)}, u32[]{:S(2)}) collective-permute-start(bf16[168,1008]{1,0:T(8,128)(2,1)} %collective-permute-done.9), channel_id=1, source_target_pairs={{64,0},{128,64},{192,128},{256,192},{320,256},{384,320},{448,384},... | collective-permute-start | bytes 1016072 | tf_op jit(solution)/shard_map/ppermute | solution.py:46
  95.4 4.0 %collective-permute-start.18 = (bf16[168,1008]{1,0:T(8,128)(2,1)S(1)}, bf16[168,1008]{1,0:T(8,128)(2,1)S(1)}, u32[]{:S(2)}, u32[]{:S(2)}) collective-permute-start(bf16[168,1008]{1,0:T(8,128)(2,1)S(1)} %collective-permute-done.13), channel_id=1, source_target_pairs={{0,64},{64,128},{128,192},{192,256},{256,320},{320,384},{384,448},... | collective-permute-start | bytes 1016072 | tf_op jit(solution)/shard_map/ppermute | solution.py:46
  101.3 5.9 %collective-permute-done.18 = bf16[168,1008]{1,0:T(8,128)(2,1)S(1)} collective-permute-done((bf16[168,1008]{1,0:T(8,128)(2,1)S(1)}, bf16[168,1008]{1,0:T(8,128)(2,1)S(1)}, u32[]{:S(2)}, u32[]{:S(2)}) %collective-permute-start.18) | collective-permute-done | bytes 338720 | tf_op jit(solution)/shard_map/ppermute | solution.py:46
  107.2 4.9 %collective-permute-done.19 = bf16[168,1008]{1,0:T(8,128)(2,1)S(1)} collective-permute-done((bf16[168,1008]{1,0:T(8,128)(2,1)S(1)}, bf16[168,1008]{1,0:T(8,128)(2,1)S(1)}, u32[]{:S(2)}, u32[]{:S(2)}) %collective-permute-start.19) | collective-permute-done | bytes 338720 | tf_op jit(solution)/shard_map/ppermute | solution.py:46
  118.4 3.9 %collective-permute-start.24 = (bf16[168,1008]{1,0:T(8,128)(2,1)}, bf16[168,1008]{1,0:T(8,128)(2,1)S(1)}, u32[]{:S(2)}, u32[]{:S(2)}) collective-permute-start(bf16[168,1008]{1,0:T(8,128)(2,1)} %copy-done.18), channel_id=1, source_target_pairs={{64,0},{128,64},{192,128},{256,192},{320,256},{384,320},{448,384},... | collective-permute-start | bytes 1016072 | tf_op jit(solution)/shard_map/ppermute | solution.py:46
  123.3 3.7 %collective-permute-done.23 = bf16[168,1008]{1,0:T(8,128)(2,1)S(1)} collective-permute-done((bf16[168,1008]{1,0:T(8,128)(2,1)}, bf16[168,1008]{1,0:T(8,128)(2,1)S(1)}, u32[]{:S(2)}, u32[]{:S(2)}) %collective-permute-start.23) | collective-permute-done | bytes 338720 | tf_op jit(solution)/shard_map/ppermute | solution.py:46
  132.2 3.9 %collective-permute-start.27 = (bf16[168,1008]{1,0:T(8,128)(2,1)S(1)}, bf16[168,1008]{1,0:T(8,128)(2,1)S(1)}, u32[]{:S(2)}, u32[]{:S(2)}) collective-permute-start(bf16[168,1008]{1,0:T(8,128)(2,1)S(1)} %collective-permute-done.24), channel_id=1, source_target_pairs={{64,0},{128,64},{192,128},{256,192},{320,256},{384,320},{448,384},... | collective-permute-start | bytes 1016072 | tf_op jit(solution)/shard_map/ppermute | solution.py:46
  155.5 7.5 %fusion.97 = f32[2,5,128,1008]{2,3,1,0:T(8,128)S(1)} fusion(bf16[2,5,128,1344]{3,2,1,0:T(8,128)(2,1)} %bitcast.304, bf16[1344,1008,1,1]{1,0,3,2:T(8,128)(2,1)} %bitcast.308), kind=kOutput, calls=%fused_computation.236 | convolution fusion | flops 3468165120 | bytes 11311104 | tf_op jit(solution)/shard_map/dot_general | solution.py:22
  183.6 4.0 %convolution_convert_fusion = bf16[1344,1008]{1,0:T(8,128)(2,1)S(1)} fusion(bf16[1344,1280]{1,0:T(8,128)(2,1)S(1)} %reshape.99, bf16[512,1008]{0,1:T(8,128)(2,1)S(1)} %get-tuple-element.200, bf16[128,1008]{0,1:T(8,128)(2,1)S(1)} %broadcast_select_fusion.2, bf16[512,1008]{0,1:T(8,128)(2,1)S(1)} %get-tuple-element.199, bf16[128,1008]{0,1:T(8,128)(2,1)S(1)} %copy-done.24), kind=kOutput, calls=%fused_computation | convolution fusion | flops 3479841792 | bytes 8730624 | tf_op jit(solution)/shard_map/dot_general | solution.py:22
  195.1 4.5 %collective-permute-start.37 = (bf16[88,1008]{1,0:T(8,128)(2,1)}, bf16[88,1008]{1,0:T(8,128)(2,1)}, u32[]{:S(2)}, u32[]{:S(2)}) collective-permute-start(bf16[88,1008]{1,0:T(8,128)(2,1)} %get-tuple-element.96), channel_id=1, source_target_pairs={{0,64},{64,128},{128,192},{192,256},{256,320},{320,384},{384,448},... | collective-permute-start | bytes 532232 | tf_op jit(solution)/shard_map/ppermute | solution.py:46
  211.3 4.9 %collective-permute-start.35 = (bf16[80,1008]{1,0:T(8,128)(2,1)S(1)}, bf16[80,1008]{1,0:T(8,128)(2,1)S(1)}, u32[]{:S(2)}, u32[]{:S(2)}) collective-permute-start(bf16[80,1008]{1,0:T(8,128)(2,1)S(1)} %get-tuple-element.94), channel_id=1, source_target_pairs={{0,64},{64,128},{128,192},{192,256},{256,320},{320,384},{384,448},... | collective-permute-start | bytes 483848 | tf_op jit(solution)/shard_map/ppermute | solution.py:46
  219.4 4.7 %collective-permute-start.40 = (bf16[4,2,84,128]{3,2,1,0:T(8,128)(2,1)S(1)}, bf16[4,2,84,128]{3,2,1,0:T(8,128)(2,1)S(1)}, u32[]{:S(2)}, u32[]{:S(2)}) collective-permute-start(bf16[4,2,84,128]{3,2,1,0:T(8,128)(2,1)S(1)} %fusion.44), channel_id=1, source_target_pairs={{0,8},{8,16},{16,24},{24,0},{1,9},{9,17},{17,25},{25,1},{2,10},{10... | collective-permute-start | bytes 516104 | tf_op jit(solution)/shard_map/ppermute | solution.py:50
  224.1 5.1 %collective-permute-start.41 = (bf16[88,1008]{1,0:T(8,128)(2,1)S(1)}, bf16[88,1008]{1,0:T(8,128)(2,1)S(1)}, u32[]{:S(2)}, u32[]{:S(2)}) collective-permute-start(bf16[88,1008]{1,0:T(8,128)(2,1)S(1)} %get-tuple-element.100), channel_id=1, source_target_pairs={{0,64},{64,128},{128,192},{192,256},{256,320},{320,384},{384,448},... | collective-permute-start | bytes 532232 | tf_op jit(solution)/shard_map/ppermute | solution.py:46
  233.9 5.1 %collective-permute-start.46 = (bf16[80,1008]{1,0:T(8,128)(2,1)S(1)}, bf16[80,1008]{1,0:T(8,128)(2,1)S(1)}, u32[]{:S(2)}, u32[]{:S(2)}) collective-permute-start(bf16[80,1008]{1,0:T(8,128)(2,1)S(1)} %get-tuple-element.105), channel_id=1, source_target_pairs={{0,64},{64,128},{128,192},{192,256},{256,320},{320,384},{384,448},... | collective-permute-start | bytes 483848 | tf_op jit(solution)/shard_map/ppermute | solution.py:46
  244.5 4.0 %collective-permute-done.43 = bf16[2,84,128]{2,1,0:T(8,128)(2,1)S(1)} collective-permute-done((bf16[2,84,128]{2,1,0:T(8,128)(2,1)S(1)}, bf16[2,84,128]{2,1,0:T(8,128)(2,1)S(1)}, u32[]{:S(2)}, u32[]{:S(2)}) %collective-permute-start.43) | collective-permute-done | bytes 43040 | tf_op jit(solution)/shard_map/ppermute | solution.py:50
  248.5 5.1 %collective-permute-start.44 = (bf16[88,1008]{1,0:T(8,128)(2,1)S(1)}, bf16[88,1008]{1,0:T(8,128)(2,1)S(1)}, u32[]{:S(2)}, u32[]{:S(2)}) collective-permute-start(bf16[88,1008]{1,0:T(8,128)(2,1)S(1)} %get-tuple-element.103), channel_id=1, source_target_pairs={{0,64},{64,128},{128,192},{192,256},{256,320},{320,384},{384,448},... | collective-permute-start | bytes 532232 | tf_op jit(solution)/shard_map/ppermute | solution.py:46
  255.7 5.1 %collective-permute-start.49 = (bf16[2,84,128]{2,1,0:T(8,128)(2,1)S(1)}, bf16[2,84,128]{2,1,0:T(8,128)(2,1)S(1)}, u32[]{:S(2)}, u32[]{:S(2)}) collective-permute-start(bf16[2,84,128]{2,1,0:T(8,128)(2,1)S(1)} %fusion.80), channel_id=1, source_target_pairs={{0,1},{1,2},{2,3},{3,0},{4,5},{5,6},{6,7},{7,4},{8,9},{9,10},{10,1... | collective-permute-start | bytes 129032 | tf_op jit(solution)/shard_map/ppermute | solution.py:50
  260.8 5.1 %collective-permute-start.50 = (bf16[80,1008]{1,0:T(8,128)(2,1)S(1)}, bf16[80,1008]{1,0:T(8,128)(2,1)S(1)}, u32[]{:S(2)}, u32[]{:S(2)}) collective-permute-start(bf16[80,1008]{1,0:T(8,128)(2,1)S(1)} %get-tuple-element.109), channel_id=1, source_target_pairs={{0,64},{64,128},{128,192},{192,256},{256,320},{320,384},{384,448},... | collective-permute-start | bytes 483848 | tf_op jit(solution)/shard_map/ppermute | solution.py:46
  268.1 6.9 %collective-permute-start.52 = (bf16[84,128]{1,0:T(8,128)(2,1)S(1)}, bf16[84,128]{1,0:T(8,128)(2,1)S(1)}, u32[]{:S(2)}, u32[]{:S(2)}) collective-permute-start(bf16[84,128]{1,0:T(8,128)(2,1)S(1)} %fusion.90), channel_id=1, source_target_pairs={{0,4},{4,0},{1,5},{5,1},{2,6},{6,2},{3,7},{7,3},{8,12},{12,8},{9,1... | collective-permute-start | bytes 64520 | tf_op jit(solution)/shard_map/ppermute | solution.py:42
  275.0 5.1 %collective-permute-start.55 = (bf16[88,1008]{1,0:T(8,128)(2,1)S(1)}, bf16[88,1008]{1,0:T(8,128)(2,1)S(1)}, u32[]{:S(2)}, u32[]{:S(2)}) collective-permute-start(bf16[88,1008]{1,0:T(8,128)(2,1)S(1)} %get-tuple-element.114), channel_id=1, source_target_pairs={{0,64},{64,128},{128,192},{192,256},{256,320},{320,384},{384,448},... | collective-permute-start | bytes 532232 | tf_op jit(solution)/shard_map/ppermute | solution.py:46
  282.8 5.0 %collective-permute-start.53 = (bf16[80,1008]{1,0:T(8,128)(2,1)S(1)}, bf16[80,1008]{1,0:T(8,128)(2,1)S(1)}, u32[]{:S(2)}, u32[]{:S(2)}) collective-permute-start(bf16[80,1008]{1,0:T(8,128)(2,1)S(1)} %get-tuple-element.112), channel_id=1, source_target_pairs={{0,64},{64,128},{128,192},{192,256},{256,320},{320,384},{384,448},... | collective-permute-start | bytes 483848 | tf_op jit(solution)/shard_map/ppermute | solution.py:46
  289.9 5.1 %collective-permute-start.59 = (bf16[88,1008]{1,0:T(8,128)(2,1)S(1)}, bf16[88,1008]{1,0:T(8,128)(2,1)S(1)}, u32[]{:S(2)}, u32[]{:S(2)}) collective-permute-start(bf16[88,1008]{1,0:T(8,128)(2,1)S(1)} %get-tuple-element.118), channel_id=1, source_target_pairs={{0,64},{64,128},{128,192},{192,256},{256,320},{320,384},{384,448},... | collective-permute-start | bytes 532232 | tf_op jit(solution)/shard_map/ppermute | solution.py:46
  297.1 5.1 %collective-permute-start.57 = (bf16[80,1008]{1,0:T(8,128)(2,1)S(1)}, bf16[80,1008]{1,0:T(8,128)(2,1)S(1)}, u32[]{:S(2)}, u32[]{:S(2)}) collective-permute-start(bf16[80,1008]{1,0:T(8,128)(2,1)S(1)} %get-tuple-element.116), channel_id=1, source_target_pairs={{0,64},{64,128},{128,192},{192,256},{256,320},{320,384},{384,448},... | collective-permute-start | bytes 483848 | tf_op jit(solution)/shard_map/ppermute | solution.py:46
  304.3 5.1 %collective-permute-start.62 = (bf16[88,1008]{1,0:T(8,128)(2,1)S(1)}, bf16[88,1008]{1,0:T(8,128)(2,1)S(1)}, u32[]{:S(2)}, u32[]{:S(2)}) collective-permute-start(bf16[88,1008]{1,0:T(8,128)(2,1)S(1)} %get-tuple-element.121), channel_id=1, source_target_pairs={{0,64},{64,128},{128,192},{192,256},{256,320},{320,384},{384,448},... | collective-permute-start | bytes 532232 | tf_op jit(solution)/shard_map/ppermute | solution.py:46
  311.4 5.1 %collective-permute-start.61 = (bf16[80,1008]{1,0:T(8,128)(2,1)S(1)}, bf16[80,1008]{1,0:T(8,128)(2,1)S(1)}, u32[]{:S(2)}, u32[]{:S(2)}) collective-permute-start(bf16[80,1008]{1,0:T(8,128)(2,1)S(1)} %get-tuple-element.120), channel_id=1, source_target_pairs={{0,64},{64,128},{128,192},{192,256},{256,320},{320,384},{384,448},... | collective-permute-start | bytes 483848 | tf_op jit(solution)/shard_map/ppermute | solution.py:46
  318.7 5.1 %collective-permute-start.64 = (bf16[88,1008]{1,0:T(8,128)(2,1)S(1)}, bf16[88,1008]{1,0:T(8,128)(2,1)S(1)}, u32[]{:S(2)}, u32[]{:S(2)}) collective-permute-start(bf16[88,1008]{1,0:T(8,128)(2,1)S(1)} %get-tuple-element.123), channel_id=1, source_target_pairs={{0,64},{64,128},{128,192},{192,256},{256,320},{320,384},{384,448},... | collective-permute-start | bytes 532232 | tf_op jit(solution)/shard_map/ppermute | solution.py:46
  326.8 5.6 %collective-permute-done.66 = bf16[88,1008]{1,0:T(8,128)(2,1)S(1)} collective-permute-done((bf16[88,1008]{1,0:T(8,128)(2,1)S(1)}, bf16[88,1008]{1,0:T(8,128)(2,1)S(1)}, u32[]{:S(2)}, u32[]{:S(2)}) %collective-permute-start.66) | collective-permute-done | bytes 177440 | tf_op jit(solution)/shard_map/ppermute | solution.py:46
  (261 shorter events, 167.3 us)
Async XLA Ops:
  1.8 26.9 %collective-permute-start = (bf16[168,1008]{1,0:T(8,128)(2,1)S(1)}, bf16[168,1008]{1,0:T(8,128)(2,1)S(1)}, u32[]{:S(2)}, u32[]{:S(2)}) collective-permute-start(bf16[168,1008]{1,0:T(8,128)(2,1)S(1)} %pad_maximum_fusion.4), channel_id=1, source_target_pairs={{0,64},{64,128},{128,192},{192,256},{256,320},{320,384},{384,448},... | collective-permute-start | bytes 1016072 | tf_op jit(solution)/shard_map/ppermute | solution.py:46
  6.9 21.8 %collective-permute-start.1 = (bf16[168,1008]{1,0:T(8,128)(2,1)S(1)}, bf16[168,1008]{1,0:T(8,128)(2,1)S(1)}, u32[]{:S(2)}, u32[]{:S(2)}) collective-permute-start(bf16[168,1008]{1,0:T(8,128)(2,1)S(1)} %pad_maximum_fusion.4), channel_id=1, source_target_pairs={{64,0},{128,64},{192,128},{256,192},{320,256},{384,320},{448,384},... | collective-permute-start | bytes 1016072 | tf_op jit(solution)/shard_map/ppermute | solution.py:46
  10.9 17.8 %collective-permute-start.2 = (bf16[84,640]{1,0:T(8,128)(2,1)S(1)}, bf16[84,640]{1,0:T(8,128)(2,1)S(1)}, u32[]{:S(2)}, u32[]{:S(2)}) collective-permute-start(bf16[84,640]{1,0:T(8,128)(2,1)S(1)} %constant_dynamic-update-slice_fusion), channel_id=1, source_target_pairs={{0,1},{1,2},{2,3},{3,0},{4,5},{5,6},{6,7},{7,4},{8,9},{9,10},{10,1... | collective-permute-start | bytes 322568 | tf_op jit(solution)/shard_map/ppermute | solution.py:50
  14.0 14.7 %collective-permute-start.3 = (bf16[84,640]{1,0:T(8,128)(2,1)S(1)}, bf16[84,640]{1,0:T(8,128)(2,1)S(1)}, u32[]{:S(2)}, u32[]{:S(2)}) collective-permute-start(bf16[84,640]{1,0:T(8,128)(2,1)S(1)} %constant_dynamic-update-slice_fusion), channel_id=1, source_target_pairs={{0,3},{1,0},{2,1},{3,2},{4,7},{5,4},{6,5},{7,6},{8,11},{9,8},{10,9... | collective-permute-start | bytes 322568 | tf_op jit(solution)/shard_map/ppermute | solution.py:50
  16.7 21.2 %collective-permute-start.7 = (bf16[84,640]{1,0:T(8,128)(2,1)S(1)}, bf16[84,640]{1,0:T(8,128)(2,1)S(1)}, u32[]{:S(2)}, u32[]{:S(2)}) collective-permute-start(bf16[84,640]{1,0:T(8,128)(2,1)S(1)} %constant_dynamic-update-slice_fusion), channel_id=1, source_target_pairs={{0,4},{4,0},{1,5},{5,1},{2,6},{6,2},{3,7},{7,3},{8,12},{12,8},{9,1... | collective-permute-start | bytes 322568 | tf_op jit(solution)/shard_map/ppermute | solution.py:42
  28.7 16.8 %collective-permute-start.4 = (bf16[168,1008]{1,0:T(8,128)(2,1)S(1)}, bf16[168,1008]{1,0:T(8,128)(2,1)S(1)}, u32[]{:S(2)}, u32[]{:S(2)}) collective-permute-start(bf16[168,1008]{1,0:T(8,128)(2,1)S(1)} %collective-permute-done), channel_id=1, source_target_pairs={{0,64},{64,128},{128,192},{192,256},{256,320},{320,384},{384,448},... | collective-permute-start | bytes 1016072 | tf_op jit(solution)/shard_map/ppermute | solution.py:46
  45.7 22.4 %collective-permute-start.10 = (bf16[4,84,640]{2,1,0:T(8,128)(2,1)S(1)}, bf16[4,84,640]{2,1,0:T(8,128)(2,1)S(1)}, u32[]{:S(2)}, u32[]{:S(2)}) collective-permute-start(bf16[4,84,640]{2,1,0:T(8,128)(2,1)S(1)} %constant_dynamic-slice_fusion.6), channel_id=1, source_target_pairs={{0,8},{8,16},{16,24},{24,0},{1,9},{9,17},{17,25},{25,1},{2,10},{10... | collective-permute-start | bytes 1290248 | tf_op jit(solution)/shard_map/ppermute | solution.py:50
  48.9 19.2 %collective-permute-start.11 = (bf16[4,84,640]{2,1,0:T(8,128)(2,1)S(1)}, bf16[4,84,640]{2,1,0:T(8,128)(2,1)S(1)}, u32[]{:S(2)}, u32[]{:S(2)}) collective-permute-start(bf16[4,84,640]{2,1,0:T(8,128)(2,1)S(1)} %constant_dynamic-slice_fusion.6), channel_id=1, source_target_pairs={{0,24},{8,0},{16,8},{24,16},{1,25},{9,1},{17,9},{25,17},{2,26},{10... | collective-permute-start | bytes 1290248 | tf_op jit(solution)/shard_map/ppermute | solution.py:50
  68.1 18.4 %collective-permute-start.15 = (bf16[4,84,640]{2,1,0:T(8,128)(2,1)S(1)}, bf16[4,84,640]{2,1,0:T(8,128)(2,1)S(1)}, u32[]{:S(2)}, u32[]{:S(2)}) collective-permute-start(bf16[4,84,640]{2,1,0:T(8,128)(2,1)S(1)} %collective-permute-done.10), channel_id=1, source_target_pairs={{0,8},{8,16},{16,24},{24,0},{1,9},{9,17},{17,25},{25,1},{2,10},{10... | collective-permute-start | bytes 1290248 | tf_op jit(solution)/shard_map/ppermute | solution.py:50
  87.4 24.7 %collective-permute-start.22 = (bf16[4,2,84,640]{3,0,2,1:T(4,128)(2,1)S(1)}, bf16[4,2,84,640]{3,0,2,1:T(4,128)(2,1)S(1)}, u32[]{:S(2)}, u32[]{:S(2)}) collective-permute-start(bf16[4,2,84,640]{3,0,2,1:T(4,128)(2,1)S(1)} %copy.33), channel_id=1, source_target_pairs={{0,32},{32,0},{1,33},{33,1},{2,34},{34,2},{3,35},{35,3},{4,36},{36... | collective-permute-start | bytes 2580488 | tf_op jit(solution)/shard_map/ppermute | solution.py:42
  89.6 22.6 %collective-permute-start.20 = (bf16[4,84,640]{2,1,0:T(8,128)(2,1)S(1)}, bf16[4,84,640]{2,1,0:T(8,128)(2,1)S(1)}, u32[]{:S(2)}, u32[]{:S(2)}) collective-permute-start(bf16[4,84,640]{2,1,0:T(8,128)(2,1)S(1)} %constant_dynamic-slice_fusion.5), channel_id=1, source_target_pairs={{0,8},{8,16},{16,24},{24,0},{1,9},{9,17},{17,25},{25,1},{2,10},{10... | collective-permute-start | bytes 1290248 | tf_op jit(solution)/shard_map/ppermute | solution.py:50
  93.0 19.2 %collective-permute-start.21 = (bf16[4,84,640]{2,1,0:T(8,128)(2,1)S(1)}, bf16[4,84,640]{2,1,0:T(8,128)(2,1)S(1)}, u32[]{:S(2)}, u32[]{:S(2)}) collective-permute-start(bf16[4,84,640]{2,1,0:T(8,128)(2,1)S(1)} %constant_dynamic-slice_fusion.5), channel_id=1, source_target_pairs={{0,24},{8,0},{16,8},{24,16},{1,25},{9,1},{17,9},{25,17},{2,26},{10... | collective-permute-start | bytes 1290248 | tf_op jit(solution)/shard_map/ppermute | solution.py:50
  112.9 17.3 %collective-permute-start.25 = (bf16[4,84,640]{2,1,0:T(8,128)(2,1)S(1)}, bf16[4,84,640]{2,1,0:T(8,128)(2,1)}, u32[]{:S(2)}, u32[]{:S(2)}) collective-permute-start(bf16[4,84,640]{2,1,0:T(8,128)(2,1)S(1)} %collective-permute-done.20), channel_id=1, source_target_pairs={{0,8},{8,16},{16,24},{24,0},{1,9},{9,17},{17,25},{25,1},{2,10},{10... | collective-permute-start | bytes 1290248 | tf_op jit(solution)/shard_map/ppermute | solution.py:50
  176.8 18.4 %collective-permute-start.31 = (bf16[1344,128]{1,0:T(8,128)(2,1)S(1)}, bf16[1344,128]{1,0:T(8,128)(2,1)S(1)}, u32[]{:S(2)}, u32[]{:S(2)}) collective-permute-start(bf16[1344,128]{1,0:T(8,128)(2,1)S(1)} %slice.122), channel_id=1, source_target_pairs={{0,32},{32,0},{1,33},{33,1},{2,34},{34,2},{3,35},{35,3},{4,36},{36... | collective-permute-start | bytes 1032200 | tf_op jit(solution)/shard_map/ppermute | solution.py:42
  188.5 17.7 %collective-permute-start.32 = (bf16[80,1008]{1,0:T(8,128)(2,1)}, bf16[80,1008]{1,0:T(8,128)(2,1)}, u32[]{:S(2)}, u32[]{:S(2)}) collective-permute-start(bf16[80,1008]{1,0:T(8,128)(2,1)} %get-tuple-element.163), channel_id=1, source_target_pairs={{0,64},{64,128},{128,192},{192,256},{256,320},{320,384},{384,448},... | collective-permute-start | bytes 483848 | tf_op jit(solution)/shard_map/ppermute | solution.py:46
  191.6 14.6 %collective-permute-start.33 = (bf16[80,1008]{1,0:T(8,128)(2,1)}, bf16[80,1008]{1,0:T(8,128)(2,1)}, u32[]{:S(2)}, u32[]{:S(2)}) collective-permute-start(bf16[80,1008]{1,0:T(8,128)(2,1)} %get-tuple-element.162), channel_id=1, source_target_pairs={{64,0},{128,64},{192,128},{256,192},{320,256},{384,320},{448,384},... | collective-permute-start | bytes 483848 | tf_op jit(solution)/shard_map/ppermute | solution.py:46
  195.1 23.0 %collective-permute-start.37 = (bf16[88,1008]{1,0:T(8,128)(2,1)}, bf16[88,1008]{1,0:T(8,128)(2,1)}, u32[]{:S(2)}, u32[]{:S(2)}) collective-permute-start(bf16[88,1008]{1,0:T(8,128)(2,1)} %get-tuple-element.96), channel_id=1, source_target_pairs={{0,64},{64,128},{128,192},{192,256},{256,320},{320,384},{384,448},... | collective-permute-start | bytes 532232 | tf_op jit(solution)/shard_map/ppermute | solution.py:46
  199.7 18.5 %collective-permute-start.38 = (bf16[88,1008]{1,0:T(8,128)(2,1)}, bf16[88,1008]{1,0:T(8,128)(2,1)}, u32[]{:S(2)}, u32[]{:S(2)}) collective-permute-start(bf16[88,1008]{1,0:T(8,128)(2,1)} %get-tuple-element.97), channel_id=1, source_target_pairs={{64,0},{128,64},{192,128},{256,192},{320,256},{384,320},{448,384},... | collective-permute-start | bytes 532232 | tf_op jit(solution)/shard_map/ppermute | solution.py:46
  211.3 19.9 %collective-permute-start.35 = (bf16[80,1008]{1,0:T(8,128)(2,1)S(1)}, bf16[80,1008]{1,0:T(8,128)(2,1)S(1)}, u32[]{:S(2)}, u32[]{:S(2)}) collective-permute-start(bf16[80,1008]{1,0:T(8,128)(2,1)S(1)} %get-tuple-element.94), channel_id=1, source_target_pairs={{0,64},{64,128},{128,192},{192,256},{256,320},{320,384},{384,448},... | collective-permute-start | bytes 483848 | tf_op jit(solution)/shard_map/ppermute | solution.py:46
  216.2 15.0 %collective-permute-start.36 = (bf16[80,1008]{1,0:T(8,128)(2,1)S(1)}, bf16[80,1008]{1,0:T(8,128)(2,1)S(1)}, u32[]{:S(2)}, u32[]{:S(2)}) collective-permute-start(bf16[80,1008]{1,0:T(8,128)(2,1)S(1)} %get-tuple-element.95), channel_id=1, source_target_pairs={{64,0},{128,64},{192,128},{256,192},{320,256},{384,320},{448,384},... | collective-permute-start | bytes 483848 | tf_op jit(solution)/shard_map/ppermute | solution.py:46
  224.1 16.9 %collective-permute-start.41 = (bf16[88,1008]{1,0:T(8,128)(2,1)S(1)}, bf16[88,1008]{1,0:T(8,128)(2,1)S(1)}, u32[]{:S(2)}, u32[]{:S(2)}) collective-permute-start(bf16[88,1008]{1,0:T(8,128)(2,1)S(1)} %get-tuple-element.100), channel_id=1, source_target_pairs={{0,64},{64,128},{128,192},{192,256},{256,320},{320,384},{384,448},... | collective-permute-start | bytes 532232 | tf_op jit(solution)/shard_map/ppermute | solution.py:46
  229.3 15.1 %collective-permute-start.42 = (bf16[88,1008]{1,0:T(8,128)(2,1)S(1)}, bf16[88,1008]{1,0:T(8,128)(2,1)S(1)}, u32[]{:S(2)}, u32[]{:S(2)}) collective-permute-start(bf16[88,1008]{1,0:T(8,128)(2,1)S(1)} %get-tuple-element.101), channel_id=1, source_target_pairs={{64,0},{128,64},{192,128},{256,192},{320,256},{384,320},{448,384},... | collective-permute-start | bytes 532232 | tf_op jit(solution)/shard_map/ppermute | solution.py:46
  231.4 24.2 %collective-permute-start.48 = (bf16[2,84,128]{2,1,0:T(8,128)(2,1)S(1)}, bf16[2,84,128]{2,1,0:T(8,128)(2,1)S(1)}, u32[]{:S(2)}, u32[]{:S(2)}) collective-permute-start(bf16[2,84,128]{2,1,0:T(8,128)(2,1)S(1)} %get-tuple-element.175), channel_id=1, source_target_pairs={{0,1},{1,2},{2,3},{3,0},{4,5},{5,6},{6,7},{7,4},{8,9},{9,10},{10,1... | collective-permute-start | bytes 129032 | tf_op jit(solution)/shard_map/ppermute | solution.py:50
  233.9 21.6 %collective-permute-start.46 = (bf16[80,1008]{1,0:T(8,128)(2,1)S(1)}, bf16[80,1008]{1,0:T(8,128)(2,1)S(1)}, u32[]{:S(2)}, u32[]{:S(2)}) collective-permute-start(bf16[80,1008]{1,0:T(8,128)(2,1)S(1)} %get-tuple-element.105), channel_id=1, source_target_pairs={{0,64},{64,128},{128,192},{192,256},{256,320},{320,384},{384,448},... | collective-permute-start | bytes 483848 | tf_op jit(solution)/shard_map/ppermute | solution.py:46
  239.1 16.5 %collective-permute-start.47 = (bf16[80,1008]{1,0:T(8,128)(2,1)S(1)}, bf16[80,1008]{1,0:T(8,128)(2,1)S(1)}, u32[]{:S(2)}, u32[]{:S(2)}) collective-permute-start(bf16[80,1008]{1,0:T(8,128)(2,1)S(1)} %get-tuple-element.106), channel_id=1, source_target_pairs={{64,0},{128,64},{192,128},{256,192},{320,256},{384,320},{448,384},... | collective-permute-start | bytes 483848 | tf_op jit(solution)/shard_map/ppermute | solution.py:46
  248.5 19.4 %collective-permute-start.44 = (bf16[88,1008]{1,0:T(8,128)(2,1)S(1)}, bf16[88,1008]{1,0:T(8,128)(2,1)S(1)}, u32[]{:S(2)}, u32[]{:S(2)}) collective-permute-start(bf16[88,1008]{1,0:T(8,128)(2,1)S(1)} %get-tuple-element.103), channel_id=1, source_target_pairs={{0,64},{64,128},{128,192},{192,256},{256,320},{320,384},{384,448},... | collective-permute-start | bytes 532232 | tf_op jit(solution)/shard_map/ppermute | solution.py:46
  253.6 14.3 %collective-permute-start.45 = (bf16[88,1008]{1,0:T(8,128)(2,1)S(1)}, bf16[88,1008]{1,0:T(8,128)(2,1)S(1)}, u32[]{:S(2)}, u32[]{:S(2)}) collective-permute-start(bf16[88,1008]{1,0:T(8,128)(2,1)S(1)} %get-tuple-element.104), channel_id=1, source_target_pairs={{64,0},{128,64},{192,128},{256,192},{320,256},{384,320},{448,384},... | collective-permute-start | bytes 532232 | tf_op jit(solution)/shard_map/ppermute | solution.py:46
  260.8 21.2 %collective-permute-start.50 = (bf16[80,1008]{1,0:T(8,128)(2,1)S(1)}, bf16[80,1008]{1,0:T(8,128)(2,1)S(1)}, u32[]{:S(2)}, u32[]{:S(2)}) collective-permute-start(bf16[80,1008]{1,0:T(8,128)(2,1)S(1)} %get-tuple-element.109), channel_id=1, source_target_pairs={{0,64},{64,128},{128,192},{192,256},{256,320},{320,384},{384,448},... | collective-permute-start | bytes 483848 | tf_op jit(solution)/shard_map/ppermute | solution.py:46
  266.0 16.1 %collective-permute-start.51 = (bf16[80,1008]{1,0:T(8,128)(2,1)S(1)}, bf16[80,1008]{1,0:T(8,128)(2,1)S(1)}, u32[]{:S(2)}, u32[]{:S(2)}) collective-permute-start(bf16[80,1008]{1,0:T(8,128)(2,1)S(1)} %get-tuple-element.110), channel_id=1, source_target_pairs={{64,0},{128,64},{192,128},{256,192},{320,256},{384,320},{448,384},... | collective-permute-start | bytes 483848 | tf_op jit(solution)/shard_map/ppermute | solution.py:46
  268.1 14.6 %collective-permute-start.52 = (bf16[84,128]{1,0:T(8,128)(2,1)S(1)}, bf16[84,128]{1,0:T(8,128)(2,1)S(1)}, u32[]{:S(2)}, u32[]{:S(2)}) collective-permute-start(bf16[84,128]{1,0:T(8,128)(2,1)S(1)} %fusion.90), channel_id=1, source_target_pairs={{0,4},{4,0},{1,5},{5,1},{2,6},{6,2},{3,7},{7,3},{8,12},{12,8},{9,1... | collective-permute-start | bytes 64520 | tf_op jit(solution)/shard_map/ppermute | solution.py:42
  275.0 14.7 %collective-permute-start.55 = (bf16[88,1008]{1,0:T(8,128)(2,1)S(1)}, bf16[88,1008]{1,0:T(8,128)(2,1)S(1)}, u32[]{:S(2)}, u32[]{:S(2)}) collective-permute-start(bf16[88,1008]{1,0:T(8,128)(2,1)S(1)} %get-tuple-element.114), channel_id=1, source_target_pairs={{0,64},{64,128},{128,192},{192,256},{256,320},{320,384},{384,448},... | collective-permute-start | bytes 532232 | tf_op jit(solution)/shard_map/ppermute | solution.py:46
  311.4 14.9 %collective-permute-start.61 = (bf16[80,1008]{1,0:T(8,128)(2,1)S(1)}, bf16[80,1008]{1,0:T(8,128)(2,1)S(1)}, u32[]{:S(2)}, u32[]{:S(2)}) collective-permute-start(bf16[80,1008]{1,0:T(8,128)(2,1)S(1)} %get-tuple-element.120), channel_id=1, source_target_pairs={{0,64},{64,128},{128,192},{192,256},{256,320},{320,384},{384,448},... | collective-permute-start | bytes 483848 | tf_op jit(solution)/shard_map/ppermute | solution.py:46
  (64 other events, 605.9 us)

commit v6 on v2

--- a/solution.py
+++ b/solution.py
@@ -42,17 +42,20 @@
     return lax.ppermute(values, axis_name, [(0, 1), (1, 0)])
 
 
-def line_gather(shard, place, ties):
+def line_gather(shard, place, stages):
     from_left, from_right = [], []
     right = left = shard
+    waiting = next(stages)
     for step in range(ZL - 1):
-        right, left, _ = lax.optimization_barrier((right, left, ties.get(step, ())))
+        right, left, waiting = lax.optimization_barrier((right, left, waiting))
+        if step < ZL - 2:
+            waiting = stages.send(waiting)
         right = lax.ppermute(right, "zl", [(i, i + 1) for i in range(step, ZL - 1)])
         left = lax.ppermute(left, "zl", [(i, i - 1) for i in range(1, ZL - step)])
         from_left.append(right)
         from_right.append(left)
     slots = jnp.stack(from_left[::-1] + [shard] + from_right)
-    return lax.dynamic_slice_in_dim(slots, ZL - 1 - place, ZL, 0)
+    return lax.dynamic_slice_in_dim(slots, ZL - 1 - place, ZL, 0), waiting
 
 
 def line_scatter(parts, place, ties):
@@ -64,12 +67,14 @@
             to_right = to_right.astype(jnp.float32) + right.astype(jnp.float32)
             to_left = to_left.astype(jnp.float32) + left.astype(jnp.float32)
         to_right, to_left = to_right.astype(jnp.bfloat16), to_left.astype(jnp.bfloat16)
-        to_right, to_left, _ = lax.optimization_barrier((to_right, to_left, ties.get(step, ())))
+        if step in (4, ZL - 2):
+            to_right, to_left, ties = lax.optimization_barrier((to_right, to_left, ties))
+        else:
+            to_right, to_left = lax.optimization_barrier((to_right, to_left))
         right = lax.ppermute(to_right, "zl", [(i, i + 1) for i in range(step + 1)])
         left = lax.ppermute(to_left, "zl", [(i, i - 1) for i in range(ZL - 1 - step, ZL)])
-    return (
-        parts[place].astype(jnp.float32) + right.astype(jnp.float32) + left.astype(jnp.float32)
-    )
+    total = parts[place].astype(jnp.float32)
+    return total + right.astype(jnp.float32) + left.astype(jnp.float32), ties
 
 
 def per_device(acts, cotangents, w_gate, w_up, w_down, unit_rank):
@@ -81,8 +86,6 @@
     rows = w_gate.shape[0]
 
     local = jnp.concatenate([acts.T] + [part.T for part in suffix_sums(cotangents)], 1)
-    far_local = swap(local, "zh")
-
     def spread(values):
         copies = jnp.broadcast_to(values[None], (16,) + values.shape)
         got = lax.all_to_all(copies, ("y", "x"), 0, 0)
@@ -93,17 +96,24 @@
         given = lax.dynamic_index_in_dim(values, 1 - core, 1, False)
         return kept, swap(given, "co")
 
-    near = spread(local)
-    near_parts = both_tokens(near)
-    far = spread(far_local)
-    far_parts = both_tokens(far)
-    ties = {1: (far_local,), 3: (near,), 4: near_parts, 5: (far,), 6: far_parts}
+    def gathers():
+        far = swap(local, "zh")
+        near = spread(local)
+        (far,) = yield (far,)
+        far, near = yield far, near
+        far = spread(far)
+        near = both_tokens(near)
+        (near,) = yield (near,)
+        (near,) = yield (near,)
+        far, near = yield far, near
+        far, near = yield both_tokens(far), near
+        parts = in_order(jnp.concatenate(near, -1), jnp.concatenate(far, -1), half, 1)
+        yield parts.reshape(ZL * rows, 10 * tokens)
 
-    weights = line_gather(jnp.concatenate([w_gate, w_up, w_down.T], 1), place, ties)
+    weights, inputs = line_gather(
+        jnp.concatenate([w_gate, w_up, w_down.T], 1), place, gathers()
+    )
     weights = weights.reshape(ZL * rows, 3 * units)
-    inputs = in_order(
-        jnp.concatenate(near_parts, -1), jnp.concatenate(far_parts, -1), half, 1
-    ).reshape(ZL * rows, 10 * tokens)
 
     band = (
         (unit_rank >= FF // 8).astype(jnp.int32)
@@ -146,10 +156,10 @@
     partial_acts = partial_acts.transpose(1, 0, 3, 2, 4, 5).reshape(16, 2, features, tokens)
     shares = lax.all_to_all(partial_acts, ("y", "x"), 0, 0)
     shares = jnp.sum(shares.astype(jnp.float32), 0)
+    grads, (shares,) = line_scatter(parts, place, (shares,))
+    grads = grads.astype(jnp.bfloat16)
     away = swap(shares[1 - half].astype(jnp.bfloat16), "zh")
     grad_acts = (shares[half] + away.astype(jnp.float32)).astype(jnp.bfloat16).T
-
-    grads = line_scatter(parts, place, {3: (shares,), 5: (away,)}).astype(jnp.bfloat16)
     return (
         grad_acts,
         grads[:, :units],

time: 278 us -> 287 us (1.032)
  waiting for transfers between devices: 81.5 us -> 94.2 us
  starting transfers between devices: 124 us -> 121 us
    ppermute x7, waiting for transfers between devices: 42.7 us -> 58.2 us  [line_gather(): left = lax.ppermute(left, 'zl', [(i, i - 1) for i in range(1, ZL - step)])]
    ppermute x7, waiting for transfers between devices: 12.1 us -> 17.8 us  [swap(): return lax.ppermute(values, axis_name, [(0, 1), (1, 0)])]
    ppermute x7, waiting for transfers between devices: 4.43 us -> 0.02 us  [line_scatter(): lax.ppermute(to_left, 'zl', [(i, i - 1) for i in range(ZL - 1 - step, ZL)])]
    ppermute x7, starting transfers between devices: 35 us -> 31.2 us  [swap(): return lax.ppermute(values, axis_name, [(0, 1), (1, 0)])]
    unnamed x77 -> x81, local copies, waits for them, and re-layouts: 13.4 us -> 10.5 us
  transfers between devices with their start and end apart: 38 -> 38, of which waited for: 17 -> 16; matrix products, arithmetic and copies ran while one was open for 14% -> 12% of each run, Pallas kernels for 0% -> 0%
where the time goes in v6:
time: 287 us; the launch traced here: 284 us
  starting transfers between devices  121 us (42%)
  waiting for transfers between devices  94.2 us (33%)
  local copies, waits for them, and re-layouts  36.2 us (13%)
  other arithmetic  22 us (8%)
  matrix products  9.36 us (3%)
    ppermute x7, waiting for transfers between devices, line_gather(): left = lax.ppermute(left, 'zl', [(i, i - 1) for i in range(1, ZL - step)])  58.2 us
    ppermute x7, starting transfers between devices, line_scatter(): right = lax.ppermute(to_right, 'zl', [(i, i + 1) for i in range(step + 1)])  36.3 us
    ppermute x7, starting transfers between devices, swap(): return lax.ppermute(values, axis_name, [(0, 1), (1, 0)])  31.2 us
    ppermute x7, waiting for transfers between devices, swap(): return lax.ppermute(values, axis_name, [(0, 1), (1, 0)])  17.8 us
    all_to_all x2, starting transfers between devices, spread(): got = lax.all_to_all(copies, ('y', 'x'), 0, 0)  16.6 us
    convert_element_type x6, other arithmetic, line_scatter(): to_left.astype(jnp.bfloat16)  11.9 us
    ppermute x7, waiting for transfers between devices, line_scatter(): right = lax.ppermute(to_right, 'zl', [(i, i + 1) for i in range(step + 1)])  11.6 us
    ppermute x7, starting transfers between devices, line_gather(): right = lax.ppermute(right, 'zl', [(i, i + 1) for i in range(step, ZL - 1)])  11.1 us
  transfers between devices with their start and end apart: 38, of which 16 were waited for; matrix products, arithmetic and copies ran while one was open for 12% of the time, Pallas kernels for 0%

profile of v6, /device:TPU:6, one launch (start us, length us, event | category | flops | bytes accessed | tf_op | source)
XLA Modules:
  0.0 284.0 jit_solution(18106803982866957483)
XLA Ops:
  4.1 9.4 %all-to-all-start = ((bf16[16,84,640]{2,1,0:T(8,128)(2,1)}), bf16[16,84,640]{2,1,0:T(8,128)(2,1)S(1)}, u32[]{:S(2)}, u32[]{:S(2)}) async-start(bf16[16,84,640]{2,1,0:T(8,128)(2,1)} %broadcast_in_dim.86), calls=%async_computation | async-start | bytes 3604480 | tf_op jit(solution)/shard_map/all_to_all | solution.py:91
  13.5 13.8 %collective-permute-start = (bf16[84,640]{1,0:T(8,128)(2,1)S(1)}, bf16[84,640]{1,0:T(8,128)(2,1)S(1)}, u32[]{:S(2)}, u32[]{:S(2)}) collective-permute-start(bf16[84,640]{1,0:T(8,128)(2,1)S(1)} %constant_dynamic-update-slice_fusion), channel_id=1, source_target_pairs={{0,4},{4,0},{1,5},{5,1},{2,6},{6,2},{3,7},{7,3},{8,12},{12,8},{9,1... | collective-permute-start | bytes 322568 | tf_op jit(solution)/shard_map/ppermute | solution.py:42
  27.4 7.4 %collective-permute-done = bf16[84,640]{1,0:T(8,128)(2,1)S(1)} collective-permute-done((bf16[84,640]{1,0:T(8,128)(2,1)S(1)}, bf16[84,640]{1,0:T(8,128)(2,1)S(1)}, u32[]{:S(2)}, u32[]{:S(2)}) %collective-permute-start) | collective-permute-done | bytes 107552 | tf_op jit(solution)/shard_map/ppermute | solution.py:42
  34.8 4.1 %collective-permute-start.1 = (bf16[168,1008]{1,0:T(8,128)(2,1)S(1)}, bf16[168,1008]{1,0:T(8,128)(2,1)S(1)}, u32[]{:S(2)}, u32[]{:S(2)}) collective-permute-start(bf16[168,1008]{1,0:T(8,128)(2,1)S(1)} %pad_maximum_fusion.4), channel_id=1, source_target_pairs={{0,64},{64,128},{128,192},{192,256},{256,320},{320,384},{384,448},... | collective-permute-start | bytes 1016072 | tf_op jit(solution)/shard_map/ppermute | solution.py:53
  40.2 3.4 %collective-permute-done.1 = bf16[168,1008]{1,0:T(8,128)(2,1)S(1)} collective-permute-done((bf16[168,1008]{1,0:T(8,128)(2,1)S(1)}, bf16[168,1008]{1,0:T(8,128)(2,1)S(1)}, u32[]{:S(2)}, u32[]{:S(2)}) %collective-permute-start.1) | collective-permute-done | bytes 338720 | tf_op jit(solution)/shard_map/ppermute | solution.py:53
  43.7 4.4 %collective-permute-done.2 = bf16[168,1008]{1,0:T(8,128)(2,1)S(1)} collective-permute-done((bf16[168,1008]{1,0:T(8,128)(2,1)S(1)}, bf16[168,1008]{1,0:T(8,128)(2,1)S(1)}, u32[]{:S(2)}, u32[]{:S(2)}) %collective-permute-start.2) | collective-permute-done | bytes 338720 | tf_op jit(solution)/shard_map/ppermute | solution.py:54
  49.9 7.2 %all-to-all-start.1 = ((bf16[16,84,640]{2,1,0:T(8,128)(2,1)}), bf16[16,84,640]{2,1,0:T(8,128)(2,1)S(1)}, u32[]{:S(2)}, u32[]{:S(2)}) async-start(bf16[16,84,640]{2,1,0:T(8,128)(2,1)} %broadcast_in_dim.87), calls=%async_computation.1 | async-start | bytes 3604480 | tf_op jit(solution)/shard_map/all_to_all | solution.py:91
  63.0 13.3 %collective-permute-done.4 = bf16[168,1008]{1,0:T(8,128)(2,1)S(1)} collective-permute-done((bf16[168,1008]{1,0:T(8,128)(2,1)S(1)}, bf16[168,1008]{1,0:T(8,128)(2,1)S(1)}, u32[]{:S(2)}, u32[]{:S(2)}) %collective-permute-start.4) | collective-permute-done | bytes 338720 | tf_op jit(solution)/shard_map/ppermute | solution.py:54
  78.4 11.4 %collective-permute-done.7 = bf16[168,1008]{1,0:T(8,128)(2,1)S(1)} collective-permute-done((bf16[168,1008]{1,0:T(8,128)(2,1)S(1)}, bf16[168,1008]{1,0:T(8,128)(2,1)S(1)}, u32[]{:S(2)}, u32[]{:S(2)}) %collective-permute-start.7) | collective-permute-done | bytes 338720 | tf_op jit(solution)/shard_map/ppermute | solution.py:54
  92.6 14.1 %collective-permute-done.9 = bf16[168,1008]{1,0:T(8,128)(2,1)} collective-permute-done((bf16[168,1008]{1,0:T(8,128)(2,1)S(1)}, bf16[168,1008]{1,0:T(8,128)(2,1)}, u32[]{:S(2)}, u32[]{:S(2)}) %collective-permute-start.9) | collective-permute-done | bytes 338720 | tf_op jit(solution)/shard_map/ppermute | solution.py:54
  112.8 11.4 %collective-permute-done.11 = bf16[168,1008]{1,0:T(8,128)(2,1)} collective-permute-done((bf16[168,1008]{1,0:T(8,128)(2,1)}, bf16[168,1008]{1,0:T(8,128)(2,1)}, u32[]{:S(2)}, u32[]{:S(2)}) %collective-permute-start.11) | collective-permute-done | bytes 338720 | tf_op jit(solution)/shard_map/ppermute | solution.py:54
  131.3 3.0 %reshape.188 = bf16[1344,1280]{1,0:T(8,128)(2,1)S(1)} reshape(bf16[4,2,2,84,1280]{4,3,2,1,0:T(8,128)(2,1)} %copy.83) | data formatting | bytes 6881280 | tf_op jit(solution)/shard_map/reshape | solution.py:111
  134.4 3.6 %collective-permute-done.14 = bf16[168,1008]{1,0:T(8,128)(2,1)} collective-permute-done((bf16[168,1008]{1,0:T(8,128)(2,1)}, bf16[168,1008]{1,0:T(8,128)(2,1)}, u32[]{:S(2)}, u32[]{:S(2)}) %collective-permute-start.14) | collective-permute-done | bytes 338720 | tf_op jit(solution)/shard_map/ppermute | solution.py:54
  140.9 3.6 %copy.84 = bf16[1280,1344]{1,0:T(8,128)(2,1)} copy(bf16[1280,1344]{0,1:T(8,128)(2,1)S(1)} %bitcast.207) | data formatting | bytes 6881280 | tf_op jit(solution)/shard_map/dot_general | solution.py:22
  154.6 4.6 %fusion.71 = f32[2,5,128,1008]{2,3,1,0:T(8,128)S(1)} fusion(bf16[2,5,128,1344]{3,2,1,0:T(8,128)(2,1)S(1)} %bitcast.218, bf16[1344,1008,1,1]{1,0,3,2:T(8,128)(2,1)S(1)} %bitcast.221), kind=kOutput, calls=%fused_computation.170 | convolution fusion | flops 3468165120 | bytes 11311104 | tf_op jit(solution)/shard_map/dot_general | solution.py:22
  173.0 4.0 %convolution_convert_fusion = bf16[1344,1008]{1,0:T(8,128)(2,1)S(1)} fusion(bf16[1344,1280]{1,0:T(8,128)(2,1)S(1)} %reshape.188, bf16[512,1008]{0,1:T(8,128)(2,1)S(1)} %fusion.21, bf16[128,1008]{0,1:T(8,128)(2,1)S(1)} %broadcast_select_fusion.4, bf16[512,1008]{0,1:T(8,128)(2,1)S(1)} %fusion.18, bf16[128,1008]{0,1:T(8,128)(2,1)S(1)} %copy-done.30), kind=kOutput, calls=%fused_computation | convolution fusion | flops 3479841792 | bytes 8730624 | tf_op jit(solution)/shard_map/dot_general | solution.py:22
  178.1 5.1 %collective-permute-start.19 = (bf16[168,1008]{1,0:T(8,128)(2,1)}, bf16[168,1008]{1,0:T(8,128)(2,1)S(1)}, u32[]{:S(2)}, u32[]{:S(2)}) collective-permute-start(bf16[168,1008]{1,0:T(8,128)(2,1)} %get-tuple-element.78), channel_id=1, source_target_pairs={{0,64},{1,65},{2,66},{3,67},{4,68},{5,69},{6,70},{7,71},{8,72},{9,... | collective-permute-start | bytes 1016072 | tf_op jit(solution)/shard_map/ppermute | solution.py:74
  188.7 2.4 collective-permute-done.19
  191.0 2.2 fusion.29
  193.3 5.0 %collective-permute-start.21 = (bf16[168,1008]{1,0:T(8,128)(2,1)}, bf16[168,1008]{1,0:T(8,128)(2,1)}, u32[]{:S(2)}, u32[]{:S(2)}) collective-permute-start(bf16[168,1008]{1,0:T(8,128)(2,1)} %get-tuple-element.80), channel_id=1, source_target_pairs={{0,64},{64,128},{1,65},{65,129},{2,66},{66,130},{3,67},{67,131},{4... | collective-permute-start | bytes 1016072 | tf_op jit(solution)/shard_map/ppermute | solution.py:74
  206.8 5.1 %collective-permute-start.23 = (bf16[168,1008]{1,0:T(8,128)(2,1)}, bf16[168,1008]{1,0:T(8,128)(2,1)}, u32[]{:S(2)}, u32[]{:S(2)}) collective-permute-start(bf16[168,1008]{1,0:T(8,128)(2,1)} %get-tuple-element.82), channel_id=1, source_target_pairs={{0,64},{64,128},{128,192},{1,65},{65,129},{129,193},{2,66},{66,130... | collective-permute-start | bytes 1016072 | tf_op jit(solution)/shard_map/ppermute | solution.py:74
  215.5 7.2 %all-to-all-start.2 = ((bf16[16,2,84,128]{3,1,2,0:T(2,128)(2,1)}), bf16[16,2,84,128]{3,1,2,0:T(2,128)(2,1)S(1)}, u32[]{:S(2)}, u32[]{:S(2)}) async-start(bf16[16,2,84,128]{3,1,2,0:T(2,128)(2,1)} %copy.87), calls=%async_computation.2 | async-start | bytes 1376256 | tf_op jit(solution)/shard_map/all_to_all | solution.py:157
  222.8 2.2 fusion.27
  225.0 2.2 collective-permute-start.25
  228.6 3.1 %all-to-all-done.2 = bf16[16,2,84,128]{3,1,2,0:T(2,128)(2,1)S(1)} async-done(((bf16[16,2,84,128]{3,1,2,0:T(2,128)(2,1)}), bf16[16,2,84,128]{3,1,2,0:T(2,128)(2,1)S(1)}, u32[]{:S(2)}, u32[]{:S(2)}) %all-to-all-start.2) | async-done | bytes 688160 | tf_op jit(solution)/shard_map/all_to_all | solution.py:157
  234.4 4.2 %collective-permute-start.28 = (bf16[168,1008]{1,0:T(8,128)(2,1)}, bf16[168,1008]{1,0:T(8,128)(2,1)S(1)}, u32[]{:S(2)}, u32[]{:S(2)}) collective-permute-start(bf16[168,1008]{1,0:T(8,128)(2,1)} %get-tuple-element.86), channel_id=1, source_target_pairs={{0,64},{64,128},{128,192},{192,256},{256,320},{1,65},{65,129},{129... | collective-permute-start | bytes 1016072 | tf_op jit(solution)/shard_map/ppermute | solution.py:74
  239.9 3.6 %collective-permute-done.28 = bf16[168,1008]{1,0:T(8,128)(2,1)S(1)} collective-permute-done((bf16[168,1008]{1,0:T(8,128)(2,1)}, bf16[168,1008]{1,0:T(8,128)(2,1)S(1)}, u32[]{:S(2)}, u32[]{:S(2)}) %collective-permute-start.28) | collective-permute-done | bytes 338720 | tf_op jit(solution)/shard_map/ppermute | solution.py:74
  245.6 4.3 %collective-permute-start.30 = (bf16[168,1008]{1,0:T(8,128)(2,1)}, bf16[168,1008]{1,0:T(8,128)(2,1)S(1)}, u32[]{:S(2)}, u32[]{:S(2)}) collective-permute-start(bf16[168,1008]{1,0:T(8,128)(2,1)} %get-tuple-element.88), channel_id=1, source_target_pairs={{0,64},{64,128},{128,192},{192,256},{256,320},{320,384},{1,65},{65... | collective-permute-start | bytes 1016072 | tf_op jit(solution)/shard_map/ppermute | solution.py:74
  251.3 3.6 %collective-permute-done.30 = bf16[168,1008]{1,0:T(8,128)(2,1)S(1)} collective-permute-done((bf16[168,1008]{1,0:T(8,128)(2,1)}, bf16[168,1008]{1,0:T(8,128)(2,1)S(1)}, u32[]{:S(2)}, u32[]{:S(2)}) %collective-permute-start.30) | collective-permute-done | bytes 338720 | tf_op jit(solution)/shard_map/ppermute | solution.py:74
  256.1 10.4 %collective-permute-start.33 = (bf16[168,1008]{1,0:T(8,128)(2,1)S(1)}, bf16[168,1008]{1,0:T(8,128)(2,1)S(1)}, u32[]{:S(2)}, u32[]{:S(2)}) collective-permute-start(bf16[168,1008]{1,0:T(8,128)(2,1)S(1)} %get-tuple-element.92), channel_id=1, source_target_pairs={{0,64},{64,128},{128,192},{192,256},{256,320},{320,384},{384,448},... | collective-permute-start | bytes 1016072 | tf_op jit(solution)/shard_map/ppermute | solution.py:74
  267.9 7.5 %collective-permute-start.32 = (bf16[84,128]{1,0:T(8,128)(2,1)S(1)}, bf16[84,128]{1,0:T(8,128)(2,1)S(1)}, u32[]{:S(2)}, u32[]{:S(2)}) collective-permute-start(bf16[84,128]{1,0:T(8,128)(2,1)S(1)} %bitcast.226), channel_id=1, source_target_pairs={{0,4},{4,0},{1,5},{5,1},{2,6},{6,2},{3,7},{7,3},{8,12},{12,8},{9,1... | collective-permute-start | bytes 64520 | tf_op jit(solution)/shard_map/ppermute | solution.py:42
  275.5 6.8 %collective-permute-done.32 = bf16[84,128]{1,0:T(8,128)(2,1)S(1)} collective-permute-done((bf16[84,128]{1,0:T(8,128)(2,1)S(1)}, bf16[84,128]{1,0:T(8,128)(2,1)S(1)}, u32[]{:S(2)}, u32[]{:S(2)}) %collective-permute-start.32) | collective-permute-done | bytes 21536 | tf_op jit(solution)/shard_map/ppermute | solution.py:42
  (182 shorter events, 88.7 us)
Async XLA Ops:
  4.1 44.0 %all-to-all-start = ((bf16[16,84,640]{2,1,0:T(8,128)(2,1)}), bf16[16,84,640]{2,1,0:T(8,128)(2,1)S(1)}, u32[]{:S(2)}, u32[]{:S(2)}) async-start(bf16[16,84,640]{2,1,0:T(8,128)(2,1)} %broadcast_in_dim.86), calls=%async_computation | async-start | bytes 3604480 | tf_op jit(solution)/shard_map/all_to_all | solution.py:91
  13.5 21.4 %collective-permute-start = (bf16[84,640]{1,0:T(8,128)(2,1)S(1)}, bf16[84,640]{1,0:T(8,128)(2,1)S(1)}, u32[]{:S(2)}, u32[]{:S(2)}) collective-permute-start(bf16[84,640]{1,0:T(8,128)(2,1)S(1)} %constant_dynamic-update-slice_fusion), channel_id=1, source_target_pairs={{0,4},{4,0},{1,5},{5,1},{2,6},{6,2},{3,7},{7,3},{8,12},{12,8},{9,1... | collective-permute-start | bytes 322568 | tf_op jit(solution)/shard_map/ppermute | solution.py:42
  34.8 8.8 %collective-permute-start.1 = (bf16[168,1008]{1,0:T(8,128)(2,1)S(1)}, bf16[168,1008]{1,0:T(8,128)(2,1)S(1)}, u32[]{:S(2)}, u32[]{:S(2)}) collective-permute-start(bf16[168,1008]{1,0:T(8,128)(2,1)S(1)} %pad_maximum_fusion.4), channel_id=1, source_target_pairs={{0,64},{64,128},{128,192},{192,256},{256,320},{320,384},{384,448},... | collective-permute-start | bytes 1016072 | tf_op jit(solution)/shard_map/ppermute | solution.py:53
  38.9 9.1 %collective-permute-start.2 = (bf16[168,1008]{1,0:T(8,128)(2,1)S(1)}, bf16[168,1008]{1,0:T(8,128)(2,1)S(1)}, u32[]{:S(2)}, u32[]{:S(2)}) collective-permute-start(bf16[168,1008]{1,0:T(8,128)(2,1)S(1)} %pad_maximum_fusion.4), channel_id=1, source_target_pairs={{64,0},{128,64},{192,128},{256,192},{320,256},{384,320},{448,384},... | collective-permute-start | bytes 1016072 | tf_op jit(solution)/shard_map/ppermute | solution.py:54
  49.9 56.8 %all-to-all-start.1 = ((bf16[16,84,640]{2,1,0:T(8,128)(2,1)}), bf16[16,84,640]{2,1,0:T(8,128)(2,1)S(1)}, u32[]{:S(2)}, u32[]{:S(2)}) async-start(bf16[16,84,640]{2,1,0:T(8,128)(2,1)} %broadcast_in_dim.87), calls=%async_computation.1 | async-start | bytes 3604480 | tf_op jit(solution)/shard_map/all_to_all | solution.py:91
  59.1 17.3 %collective-permute-start.5 = (bf16[4,2,84,640]{3,0,2,1:T(4,128)(2,1)S(1)}, bf16[4,2,84,640]{3,0,2,1:T(4,128)(2,1)S(1)}, u32[]{:S(2)}, u32[]{:S(2)}) collective-permute-start(bf16[4,2,84,640]{3,0,2,1:T(4,128)(2,1)S(1)} %copy.79), channel_id=1, source_target_pairs={{0,32},{32,0},{1,33},{33,1},{2,34},{34,2},{3,35},{35,3},{4,36},{36... | collective-permute-start | bytes 2580488 | tf_op jit(solution)/shard_map/ppermute | solution.py:42
  61.7 14.7 %collective-permute-start.4 = (bf16[168,1008]{1,0:T(8,128)(2,1)S(1)}, bf16[168,1008]{1,0:T(8,128)(2,1)S(1)}, u32[]{:S(2)}, u32[]{:S(2)}) collective-permute-start(bf16[168,1008]{1,0:T(8,128)(2,1)S(1)} %collective-permute-done.2), channel_id=1, source_target_pairs={{64,0},{128,64},{192,128},{256,192},{320,256},{384,320},{65,1},{12... | collective-permute-start | bytes 1016072 | tf_op jit(solution)/shard_map/ppermute | solution.py:54
  77.0 12.8 %collective-permute-start.7 = (bf16[168,1008]{1,0:T(8,128)(2,1)S(1)}, bf16[168,1008]{1,0:T(8,128)(2,1)S(1)}, u32[]{:S(2)}, u32[]{:S(2)}) collective-permute-start(bf16[168,1008]{1,0:T(8,128)(2,1)S(1)} %collective-permute-done.4), channel_id=1, source_target_pairs={{64,0},{128,64},{192,128},{256,192},{320,256},{65,1},{129,65},{193... | collective-permute-start | bytes 1016072 | tf_op jit(solution)/shard_map/ppermute | solution.py:54
  91.3 15.4 %collective-permute-start.9 = (bf16[168,1008]{1,0:T(8,128)(2,1)S(1)}, bf16[168,1008]{1,0:T(8,128)(2,1)}, u32[]{:S(2)}, u32[]{:S(2)}) collective-permute-start(bf16[168,1008]{1,0:T(8,128)(2,1)S(1)} %collective-permute-done.7), channel_id=1, source_target_pairs={{64,0},{128,64},{192,128},{256,192},{65,1},{129,65},{193,129},{257... | collective-permute-start | bytes 1016072 | tf_op jit(solution)/shard_map/ppermute | solution.py:54
  108.1 16.0 %collective-permute-start.12 = (bf16[4,2,84,640]{3,0,2,1:T(4,128)(2,1)S(1)}, bf16[4,2,84,640]{3,0,2,1:T(4,128)(2,1)S(1)}, u32[]{:S(2)}, u32[]{:S(2)}) collective-permute-start(bf16[4,2,84,640]{3,0,2,1:T(4,128)(2,1)S(1)} %copy.80), channel_id=1, source_target_pairs={{0,32},{32,0},{1,33},{33,1},{2,34},{34,2},{3,35},{35,3},{4,36},{36... | collective-permute-start | bytes 2580488 | tf_op jit(solution)/shard_map/ppermute | solution.py:42
  111.5 12.7 %collective-permute-start.11 = (bf16[168,1008]{1,0:T(8,128)(2,1)}, bf16[168,1008]{1,0:T(8,128)(2,1)}, u32[]{:S(2)}, u32[]{:S(2)}) collective-permute-start(bf16[168,1008]{1,0:T(8,128)(2,1)} %collective-permute-done.9), channel_id=1, source_target_pairs={{64,0},{128,64},{192,128},{65,1},{129,65},{193,129},{66,2},{130,66... | collective-permute-start | bytes 1016072 | tf_op jit(solution)/shard_map/ppermute | solution.py:54
  124.2 10.2 %collective-permute-start.13 = (bf16[168,1008]{1,0:T(8,128)(2,1)}, bf16[168,1008]{1,0:T(8,128)(2,1)}, u32[]{:S(2)}, u32[]{:S(2)}) collective-permute-start(bf16[168,1008]{1,0:T(8,128)(2,1)} %collective-permute-done.10), channel_id=1, source_target_pairs={{320,384},{384,448},{321,385},{385,449},{322,386},{386,450},{323,3... | collective-permute-start | bytes 1016072 | tf_op jit(solution)/shard_map/ppermute | solution.py:53
  125.6 12.4 %collective-permute-start.14 = (bf16[168,1008]{1,0:T(8,128)(2,1)}, bf16[168,1008]{1,0:T(8,128)(2,1)}, u32[]{:S(2)}, u32[]{:S(2)}) collective-permute-start(bf16[168,1008]{1,0:T(8,128)(2,1)} %collective-permute-done.11), channel_id=1, source_target_pairs={{64,0},{128,64},{65,1},{129,65},{66,2},{130,66},{67,3},{131,67},{6... | collective-permute-start | bytes 1016072 | tf_op jit(solution)/shard_map/ppermute | solution.py:54
  138.0 6.5 %collective-permute-start.15 = (bf16[168,1008]{1,0:T(8,128)(2,1)}, bf16[168,1008]{1,0:T(8,128)(2,1)}, u32[]{:S(2)}, u32[]{:S(2)}) collective-permute-start(bf16[168,1008]{1,0:T(8,128)(2,1)} %collective-permute-done.13), channel_id=1, source_target_pairs={{384,448},{385,449},{386,450},{387,451},{388,452},{389,453},{390,4... | collective-permute-start | bytes 1016072 | tf_op jit(solution)/shard_map/ppermute | solution.py:53
  139.4 13.8 %collective-permute-start.16 = (bf16[168,1008]{1,0:T(8,128)(2,1)}, bf16[168,1008]{1,0:T(8,128)(2,1)}, u32[]{:S(2)}, u32[]{:S(2)}) collective-permute-start(bf16[168,1008]{1,0:T(8,128)(2,1)} %collective-permute-done.14), channel_id=1, source_target_pairs={{64,0},{65,1},{66,2},{67,3},{68,4},{69,5},{70,6},{71,7},{72,8},{73... | collective-permute-start | bytes 1016072 | tf_op jit(solution)/shard_map/ppermute | solution.py:54
  178.1 13.0 %collective-permute-start.19 = (bf16[168,1008]{1,0:T(8,128)(2,1)}, bf16[168,1008]{1,0:T(8,128)(2,1)S(1)}, u32[]{:S(2)}, u32[]{:S(2)}) collective-permute-start(bf16[168,1008]{1,0:T(8,128)(2,1)} %get-tuple-element.78), channel_id=1, source_target_pairs={{0,64},{1,65},{2,66},{3,67},{4,68},{5,69},{6,70},{7,71},{8,72},{9,... | collective-permute-start | bytes 1016072 | tf_op jit(solution)/shard_map/ppermute | solution.py:74
  183.1 7.9 %collective-permute-start.20 = (bf16[168,1008]{1,0:T(8,128)(2,1)}, bf16[168,1008]{1,0:T(8,128)(2,1)S(1)}, u32[]{:S(2)}, u32[]{:S(2)}) collective-permute-start(bf16[168,1008]{1,0:T(8,128)(2,1)} %get-tuple-element.79), channel_id=1, source_target_pairs={{448,384},{449,385},{450,386},{451,387},{452,388},{453,389},{454,3... | collective-permute-start | bytes 1016072 | tf_op jit(solution)/shard_map/ppermute | solution.py:75
  186.5 13.2 %collective-permute-start.27 = (bf16[1344,128]{1,0:T(8,128)(2,1)}, bf16[1344,128]{1,0:T(8,128)(2,1)}, u32[]{:S(2)}, u32[]{:S(2)}) collective-permute-start(bf16[1344,128]{1,0:T(8,128)(2,1)} %slice.110), channel_id=1, source_target_pairs={{0,32},{32,0},{1,33},{33,1},{2,34},{34,2},{3,35},{35,3},{4,36},{36... | collective-permute-start | bytes 1032200 | tf_op jit(solution)/shard_map/ppermute | solution.py:42
  193.3 11.4 %collective-permute-start.21 = (bf16[168,1008]{1,0:T(8,128)(2,1)}, bf16[168,1008]{1,0:T(8,128)(2,1)}, u32[]{:S(2)}, u32[]{:S(2)}) collective-permute-start(bf16[168,1008]{1,0:T(8,128)(2,1)} %get-tuple-element.80), channel_id=1, source_target_pairs={{0,64},{64,128},{1,65},{65,129},{2,66},{66,130},{3,67},{67,131},{4... | collective-permute-start | bytes 1016072 | tf_op jit(solution)/shard_map/ppermute | solution.py:74
  198.3 6.4 %collective-permute-start.22 = (bf16[168,1008]{1,0:T(8,128)(2,1)}, bf16[168,1008]{1,0:T(8,128)(2,1)}, u32[]{:S(2)}, u32[]{:S(2)}) collective-permute-start(bf16[168,1008]{1,0:T(8,128)(2,1)} %get-tuple-element.81), channel_id=1, source_target_pairs={{384,320},{448,384},{385,321},{449,385},{386,322},{450,386},{387,3... | collective-permute-start | bytes 1016072 | tf_op jit(solution)/shard_map/ppermute | solution.py:75
  206.8 15.9 %collective-permute-start.23 = (bf16[168,1008]{1,0:T(8,128)(2,1)}, bf16[168,1008]{1,0:T(8,128)(2,1)}, u32[]{:S(2)}, u32[]{:S(2)}) collective-permute-start(bf16[168,1008]{1,0:T(8,128)(2,1)} %get-tuple-element.82), channel_id=1, source_target_pairs={{0,64},{64,128},{128,192},{1,65},{65,129},{129,193},{2,66},{66,130... | collective-permute-start | bytes 1016072 | tf_op jit(solution)/shard_map/ppermute | solution.py:74
  212.0 10.8 %collective-permute-start.24 = (bf16[168,1008]{1,0:T(8,128)(2,1)}, bf16[168,1008]{1,0:T(8,128)(2,1)}, u32[]{:S(2)}, u32[]{:S(2)}) collective-permute-start(bf16[168,1008]{1,0:T(8,128)(2,1)} %get-tuple-element.83), channel_id=1, source_target_pairs={{320,256},{384,320},{448,384},{321,257},{385,321},{449,385},{322,2... | collective-permute-start | bytes 1016072 | tf_op jit(solution)/shard_map/ppermute | solution.py:75
  215.5 16.1 %all-to-all-start.2 = ((bf16[16,2,84,128]{3,1,2,0:T(2,128)(2,1)}), bf16[16,2,84,128]{3,1,2,0:T(2,128)(2,1)S(1)}, u32[]{:S(2)}, u32[]{:S(2)}) async-start(bf16[16,2,84,128]{3,1,2,0:T(2,128)(2,1)} %copy.87), calls=%async_computation.2 | async-start | bytes 1376256 | tf_op jit(solution)/shard_map/all_to_all | solution.py:157
  225.0 7.3 %collective-permute-start.25 = (bf16[168,1008]{1,0:T(8,128)(2,1)}, bf16[168,1008]{1,0:T(8,128)(2,1)}, u32[]{:S(2)}, u32[]{:S(2)}) collective-permute-start(bf16[168,1008]{1,0:T(8,128)(2,1)} %get-tuple-element.84), channel_id=1, source_target_pairs={{0,64},{64,128},{128,192},{192,256},{1,65},{65,129},{129,193},{193... | collective-permute-start | bytes 1016072 | tf_op jit(solution)/shard_map/ppermute | solution.py:74
  227.2 5.1 %collective-permute-start.26 = (bf16[168,1008]{1,0:T(8,128)(2,1)}, bf16[168,1008]{1,0:T(8,128)(2,1)}, u32[]{:S(2)}, u32[]{:S(2)}) collective-permute-start(bf16[168,1008]{1,0:T(8,128)(2,1)} %get-tuple-element.85), channel_id=1, source_target_pairs={{256,192},{320,256},{384,320},{448,384},{257,193},{321,257},{385,3... | collective-permute-start | bytes 1016072 | tf_op jit(solution)/shard_map/ppermute | solution.py:75
  234.4 9.2 %collective-permute-start.28 = (bf16[168,1008]{1,0:T(8,128)(2,1)}, bf16[168,1008]{1,0:T(8,128)(2,1)S(1)}, u32[]{:S(2)}, u32[]{:S(2)}) collective-permute-start(bf16[168,1008]{1,0:T(8,128)(2,1)} %get-tuple-element.86), channel_id=1, source_target_pairs={{0,64},{64,128},{128,192},{192,256},{256,320},{1,65},{65,129},{129... | collective-permute-start | bytes 1016072 | tf_op jit(solution)/shard_map/ppermute | solution.py:74
  238.5 5.0 %collective-permute-start.29 = (bf16[168,1008]{1,0:T(8,128)(2,1)S(1)}, bf16[168,1008]{1,0:T(8,128)(2,1)}, u32[]{:S(2)}, u32[]{:S(2)}) collective-permute-start(bf16[168,1008]{1,0:T(8,128)(2,1)S(1)} %get-tuple-element.87), channel_id=1, source_target_pairs={{192,128},{256,192},{320,256},{384,320},{448,384},{193,129},{257,1... | collective-permute-start | bytes 1016072 | tf_op jit(solution)/shard_map/ppermute | solution.py:75
  245.6 9.3 %collective-permute-start.30 = (bf16[168,1008]{1,0:T(8,128)(2,1)}, bf16[168,1008]{1,0:T(8,128)(2,1)S(1)}, u32[]{:S(2)}, u32[]{:S(2)}) collective-permute-start(bf16[168,1008]{1,0:T(8,128)(2,1)} %get-tuple-element.88), channel_id=1, source_target_pairs={{0,64},{64,128},{128,192},{192,256},{256,320},{320,384},{1,65},{65... | collective-permute-start | bytes 1016072 | tf_op jit(solution)/shard_map/ppermute | solution.py:74
  249.9 5.0 %collective-permute-start.31 = (bf16[168,1008]{1,0:T(8,128)(2,1)S(1)}, bf16[168,1008]{1,0:T(8,128)(2,1)}, u32[]{:S(2)}, u32[]{:S(2)}) collective-permute-start(bf16[168,1008]{1,0:T(8,128)(2,1)S(1)} %get-tuple-element.89), channel_id=1, source_target_pairs={{128,64},{192,128},{256,192},{320,256},{384,320},{448,384},{129,65... | collective-permute-start | bytes 1016072 | tf_op jit(solution)/shard_map/ppermute | solution.py:75
  256.1 26.8 %collective-permute-start.33 = (bf16[168,1008]{1,0:T(8,128)(2,1)S(1)}, bf16[168,1008]{1,0:T(8,128)(2,1)S(1)}, u32[]{:S(2)}, u32[]{:S(2)}) collective-permute-start(bf16[168,1008]{1,0:T(8,128)(2,1)S(1)} %get-tuple-element.92), channel_id=1, source_target_pairs={{0,64},{64,128},{128,192},{192,256},{256,320},{320,384},{384,448},... | collective-permute-start | bytes 1016072 | tf_op jit(solution)/shard_map/ppermute | solution.py:74
  266.6 16.4 %collective-permute-start.34 = (bf16[168,1008]{1,0:T(8,128)(2,1)S(1)}, bf16[168,1008]{1,0:T(8,128)(2,1)S(1)}, u32[]{:S(2)}, u32[]{:S(2)}) collective-permute-start(bf16[168,1008]{1,0:T(8,128)(2,1)S(1)} %get-tuple-element.93), channel_id=1, source_target_pairs={{64,0},{128,64},{192,128},{256,192},{320,256},{384,320},{448,384},... | collective-permute-start | bytes 1016072 | tf_op jit(solution)/shard_map/ppermute | solution.py:75
  267.9 14.4 %collective-permute-start.32 = (bf16[84,128]{1,0:T(8,128)(2,1)S(1)}, bf16[84,128]{1,0:T(8,128)(2,1)S(1)}, u32[]{:S(2)}, u32[]{:S(2)}) collective-permute-start(bf16[84,128]{1,0:T(8,128)(2,1)S(1)} %bitcast.226), channel_id=1, source_target_pairs={{0,4},{4,0},{1,5},{5,1},{2,6},{6,2},{3,7},{7,3},{8,12},{12,8},{9,1... | collective-permute-start | bytes 64520 | tf_op jit(solution)/shard_map/ppermute | solution.py:42
  (39 other events, 462.6 us)

commit v7 on v2

--- a/solution.py
+++ b/solution.py
@@ -59,14 +59,18 @@
     right = left = None
     for step in range(ZL - 1):
         to_right = parts[jnp.clip(place + ZL - 1 - step, 0, ZL - 1)]
+        if step:
+            to_right = to_right.astype(jnp.float32) + right.astype(jnp.float32)
+        to_right, left, _ = lax.optimization_barrier(
+            (to_right.astype(jnp.bfloat16), left, ties.get(step, ()))
+        )
+        right = lax.ppermute(to_right, "zl", [(i, i + 1) for i in range(step + 1)])
         to_left = parts[jnp.clip(place - ZL + 1 + step, 0, ZL - 1)]
         if step:
-            to_right = to_right.astype(jnp.float32) + right.astype(jnp.float32)
             to_left = to_left.astype(jnp.float32) + left.astype(jnp.float32)
-        to_right, to_left = to_right.astype(jnp.bfloat16), to_left.astype(jnp.bfloat16)
-        to_right, to_left, _ = lax.optimization_barrier((to_right, to_left, ties.get(step, ())))
-        right = lax.ppermute(to_right, "zl", [(i, i + 1) for i in range(step + 1)])
-        left = lax.ppermute(to_left, "zl", [(i, i - 1) for i in range(ZL - 1 - step, ZL)])
+        left = lax.ppermute(
+            to_left.astype(jnp.bfloat16), "zl", [(i, i - 1) for i in range(ZL - 1 - step, ZL)]
+        )
     return (
         parts[place].astype(jnp.float32) + right.astype(jnp.float32) + left.astype(jnp.float32)
     )
@@ -97,14 +101,13 @@
     near_parts = both_tokens(near)
     far = spread(far_local)
     far_parts = both_tokens(far)
-    ties = {1: (far_local,), 3: (near,), 4: near_parts, 5: (far,), 6: far_parts}
+    inputs = in_order(
+        jnp.concatenate(near_parts, -1), jnp.concatenate(far_parts, -1), half, 1
+    ).reshape(ZL * rows, 10 * tokens)
+    ties = {1: (far_local,), 3: (near,), 4: near_parts + (far,), 5: far_parts, 6: (inputs,)}
 
     weights = line_gather(jnp.concatenate([w_gate, w_up, w_down.T], 1), place, ties)
     weights = weights.reshape(ZL * rows, 3 * units)
-    inputs = in_order(
-        jnp.concatenate(near_parts, -1), jnp.concatenate(far_parts, -1), half, 1
-    ).reshape(ZL * rows, 10 * tokens)
-
     band = (
         (unit_rank >= FF // 8).astype(jnp.int32)
         + (unit_rank >= FF // 4).astype(jnp.int32)

time: 278 us -> 317 us (1.14)
  the two profiles are of different devices: /device:TPU:6 before, /device:TPU:128 now
where the time goes in v7:
time: 317 us; the launch traced here: 315 us
  waiting for transfers between devices  132 us (42%)
  starting transfers between devices  109 us (34%)
  local copies, waits for them, and re-layouts  39.3 us (12%)
  other arithmetic  23.2 us (7%)
  matrix products  11.1 us (4%)
    ppermute x7, waiting for transfers between devices, line_scatter(): lax.ppermute(to_left.astype(jnp.bfloat16), 'zl', [(i, i - 1) for i in ran...  39.8 us
    ppermute x7, starting transfers between devices, swap(): return lax.ppermute(values, axis_name, [(0, 1), (1, 0)])  30.4 us
    ppermute x7, waiting for transfers between devices, line_scatter(): right = lax.ppermute(to_right, 'zl', [(i, i + 1) for i in range(step + 1)])  30.2 us
    ppermute x7, starting transfers between devices, line_gather(): left = lax.ppermute(left, 'zl', [(i, i - 1) for i in range(1, ZL - step)])  19.9 us
    ppermute x7, starting transfers between devices, line_gather(): right = lax.ppermute(right, 'zl', [(i, i + 1) for i in range(step, ZL - 1)])  18.3 us
    ppermute x7, waiting for transfers between devices, swap(): return lax.ppermute(values, axis_name, [(0, 1), (1, 0)])  17.9 us
    ppermute x7, waiting for transfers between devices, line_gather(): right = lax.ppermute(right, 'zl', [(i, i + 1) for i in range(step, ZL - 1)])  17.7 us
    unnamed x49, local copies, waits for them, and re-layouts  17.5 us
  transfers between devices with their start and end apart: 38, of which 22 were waited for; matrix products, arithmetic and copies ran while one was open for 14% of the time, Pallas kernels for 0%

profile of v7, /device:TPU:128, one launch (start us, length us, event | category | flops | bytes accessed | tf_op | source)
XLA Modules:
  0.0 315.3 jit_solution(15002939322314091092)
XLA Ops:
  4.1 7.0 %all-to-all-start = ((bf16[16,84,640]{2,1,0:T(8,128)(2,1)}), bf16[16,84,640]{2,1,0:T(8,128)(2,1)S(1)}, u32[]{:S(2)}, u32[]{:S(2)}) async-start(bf16[16,84,640]{2,1,0:T(8,128)(2,1)} %broadcast_in_dim.86), calls=%async_computation | async-start | bytes 3604480 | tf_op jit(solution)/shard_map/all_to_all | solution.py:92
  11.2 11.0 %collective-permute-start.2 = (bf16[84,640]{1,0:T(8,128)(2,1)S(1)}, bf16[84,640]{1,0:T(8,128)(2,1)S(1)}, u32[]{:S(2)}, u32[]{:S(2)}) collective-permute-start(bf16[84,640]{1,0:T(8,128)(2,1)S(1)} %constant_dynamic-update-slice_fusion), channel_id=1, source_target_pairs={{0,4},{4,0},{1,5},{5,1},{2,6},{6,2},{3,7},{7,3},{8,12},{12,8},{9,1... | collective-permute-start | bytes 322568 | tf_op jit(solution)/shard_map/ppermute | solution.py:42
  22.2 9.3 %collective-permute-done.2 = bf16[84,640]{1,0:T(8,128)(2,1)S(1)} collective-permute-done((bf16[84,640]{1,0:T(8,128)(2,1)S(1)}, bf16[84,640]{1,0:T(8,128)(2,1)S(1)}, u32[]{:S(2)}, u32[]{:S(2)}) %collective-permute-start.2) | collective-permute-done | bytes 107552 | tf_op jit(solution)/shard_map/ppermute | solution.py:42
  31.5 7.0 %all-to-all-done = bf16[16,84,640]{2,1,0:T(8,128)(2,1)S(1)} async-done(((bf16[16,84,640]{2,1,0:T(8,128)(2,1)}), bf16[16,84,640]{2,1,0:T(8,128)(2,1)S(1)}, u32[]{:S(2)}, u32[]{:S(2)}) %all-to-all-start) | async-done | bytes 1720352 | tf_op jit(solution)/shard_map/all_to_all | solution.py:92
  39.9 4.4 %all-to-all-start.1 = ((bf16[16,84,640]{2,1,0:T(8,128)(2,1)}), bf16[16,84,640]{2,1,0:T(8,128)(2,1)}, u32[]{:S(2)}, u32[]{:S(2)}) async-start(bf16[16,84,640]{2,1,0:T(8,128)(2,1)} %broadcast_in_dim.87), calls=%async_computation.1 | async-start | bytes 3604480 | tf_op jit(solution)/shard_map/all_to_all | solution.py:92
  44.5 3.8 %collective-permute-start = (bf16[168,1008]{1,0:T(8,128)(2,1)S(1)}, bf16[168,1008]{1,0:T(8,128)(2,1)}, u32[]{:S(2)}, u32[]{:S(2)}) collective-permute-start(bf16[168,1008]{1,0:T(8,128)(2,1)S(1)} %pad_maximum_fusion.4), channel_id=1, source_target_pairs={{0,64},{64,128},{128,192},{192,256},{256,320},{320,384},{384,448},... | collective-permute-start | bytes 1016072 | tf_op jit(solution)/shard_map/ppermute | solution.py:50
  48.4 3.2 %collective-permute-start.1 = (bf16[168,1008]{1,0:T(8,128)(2,1)S(1)}, bf16[168,1008]{1,0:T(8,128)(2,1)}, u32[]{:S(2)}, u32[]{:S(2)}) collective-permute-start(bf16[168,1008]{1,0:T(8,128)(2,1)S(1)} %pad_maximum_fusion.4), channel_id=1, source_target_pairs={{64,0},{128,64},{192,128},{256,192},{320,256},{384,320},{448,384},... | collective-permute-start | bytes 1016072 | tf_op jit(solution)/shard_map/ppermute | solution.py:51
  51.6 4.6 %collective-permute-done = bf16[168,1008]{1,0:T(8,128)(2,1)} collective-permute-done((bf16[168,1008]{1,0:T(8,128)(2,1)S(1)}, bf16[168,1008]{1,0:T(8,128)(2,1)}, u32[]{:S(2)}, u32[]{:S(2)}) %collective-permute-start) | collective-permute-done | bytes 338720 | tf_op jit(solution)/shard_map/ppermute | solution.py:50
  58.8 3.8 %collective-permute-start.3 = (bf16[168,1008]{1,0:T(8,128)(2,1)}, bf16[168,1008]{1,0:T(8,128)(2,1)}, u32[]{:S(2)}, u32[]{:S(2)}) collective-permute-start(bf16[168,1008]{1,0:T(8,128)(2,1)} %collective-permute-done), channel_id=1, source_target_pairs={{64,128},{128,192},{192,256},{256,320},{320,384},{384,448},{65,129... | collective-permute-start | bytes 1016072 | tf_op jit(solution)/shard_map/ppermute | solution.py:50
  62.6 3.2 %collective-permute-start.4 = (bf16[168,1008]{1,0:T(8,128)(2,1)}, bf16[168,1008]{1,0:T(8,128)(2,1)}, u32[]{:S(2)}, u32[]{:S(2)}) collective-permute-start(bf16[168,1008]{1,0:T(8,128)(2,1)} %collective-permute-done.1), channel_id=1, source_target_pairs={{64,0},{128,64},{192,128},{256,192},{320,256},{384,320},{65,1},{12... | collective-permute-start | bytes 1016072 | tf_op jit(solution)/shard_map/ppermute | solution.py:51
  75.0 3.8 %collective-permute-start.5 = (bf16[168,1008]{1,0:T(8,128)(2,1)}, bf16[168,1008]{1,0:T(8,128)(2,1)}, u32[]{:S(2)}, u32[]{:S(2)}) collective-permute-start(bf16[168,1008]{1,0:T(8,128)(2,1)} %collective-permute-done.3), channel_id=1, source_target_pairs={{128,192},{192,256},{256,320},{320,384},{384,448},{129,193},{193,2... | collective-permute-start | bytes 1016072 | tf_op jit(solution)/shard_map/ppermute | solution.py:50
  78.8 3.2 %collective-permute-start.6 = (bf16[168,1008]{1,0:T(8,128)(2,1)}, bf16[168,1008]{1,0:T(8,128)(2,1)}, u32[]{:S(2)}, u32[]{:S(2)}) collective-permute-start(bf16[168,1008]{1,0:T(8,128)(2,1)} %collective-permute-done.4), channel_id=1, source_target_pairs={{64,0},{128,64},{192,128},{256,192},{320,256},{65,1},{129,65},{193... | collective-permute-start | bytes 1016072 | tf_op jit(solution)/shard_map/ppermute | solution.py:51
  82.0 6.8 %collective-permute-done.5 = bf16[168,1008]{1,0:T(8,128)(2,1)} collective-permute-done((bf16[168,1008]{1,0:T(8,128)(2,1)}, bf16[168,1008]{1,0:T(8,128)(2,1)}, u32[]{:S(2)}, u32[]{:S(2)}) %collective-permute-start.5) | collective-permute-done | bytes 338720 | tf_op jit(solution)/shard_map/ppermute | solution.py:50
  93.1 6.6 %collective-permute-start.8 = (bf16[168,1008]{1,0:T(8,128)(2,1)}, bf16[168,1008]{1,0:T(8,128)(2,1)}, u32[]{:S(2)}, u32[]{:S(2)}) collective-permute-start(bf16[168,1008]{1,0:T(8,128)(2,1)} %collective-permute-done.6), channel_id=1, source_target_pairs={{64,0},{128,64},{192,128},{256,192},{65,1},{129,65},{193,129},{257... | collective-permute-start | bytes 1016072 | tf_op jit(solution)/shard_map/ppermute | solution.py:51
  99.7 4.2 %collective-permute-done.7 = bf16[168,1008]{1,0:T(8,128)(2,1)} collective-permute-done((bf16[168,1008]{1,0:T(8,128)(2,1)}, bf16[168,1008]{1,0:T(8,128)(2,1)}, u32[]{:S(2)}, u32[]{:S(2)}) %collective-permute-start.7) | collective-permute-done | bytes 338720 | tf_op jit(solution)/shard_map/ppermute | solution.py:50
  118.3 3.0 reshape.180
  122.8 3.6 %copy.83 = bf16[1280,1344]{1,0:T(8,128)(2,1)} copy(bf16[1280,1344]{0,1:T(8,128)(2,1)S(1)} %bitcast.203) | data formatting | bytes 6881280 | tf_op jit(solution)/shard_map/dot_general | solution.py:22
  141.6 4.6 %fusion.71 = f32[2,5,128,1008]{2,3,1,0:T(8,128)S(1)} fusion(bf16[2,5,128,1344]{3,2,1,0:T(8,128)(2,1)S(1)} %bitcast.214, bf16[1344,1008,1,1]{1,0,3,2:T(8,128)(2,1)S(1)} %bitcast.217), kind=kOutput, calls=%fused_computation.170 | convolution fusion | flops 3468165120 | bytes 11311104 | tf_op jit(solution)/shard_map/dot_general | solution.py:22
  160.9 4.0 %convolution_convert_fusion = bf16[1344,1008]{1,0:T(8,128)(2,1)S(1)} fusion(bf16[1344,1280]{1,0:T(8,128)(2,1)S(1)} %reshape.180, bf16[512,1008]{0,1:T(8,128)(2,1)S(1)} %get-tuple-element.110, bf16[128,1008]{0,1:T(8,128)(2,1)S(1)} %broadcast_select_fusion.4, bf16[512,1008]{0,1:T(8,128)(2,1)S(1)} %get-tuple-element.109, bf16[128,1008]{0,1:T(8,128)(2,1)S(1)} %copy-done.14), kind=kOutput, calls=%fused_computation | convolution fusion | flops 3479841792 | bytes 8730624 | tf_op jit(solution)/shard_map/dot_general | solution.py:22
  186.6 3.6 %all-to-all-start.2 = ((bf16[16,2,84,128]{3,1,2,0:T(2,128)(2,1)}), bf16[16,2,84,128]{3,1,2,0:T(2,128)(2,1)S(1)}, u32[]{:S(2)}, u32[]{:S(2)}) async-start(bf16[16,2,84,128]{3,1,2,0:T(2,128)(2,1)} %copy.86), calls=%async_computation.2 | async-start | bytes 1376256 | tf_op jit(solution)/shard_map/all_to_all | solution.py:150
  193.7 10.5 %all-to-all-done.2 = bf16[16,2,84,128]{3,1,2,0:T(2,128)(2,1)S(1)} async-done(((bf16[16,2,84,128]{3,1,2,0:T(2,128)(2,1)}), bf16[16,2,84,128]{3,1,2,0:T(2,128)(2,1)S(1)}, u32[]{:S(2)}, u32[]{:S(2)}) %all-to-all-start.2) | async-done | bytes 688160 | tf_op jit(solution)/shard_map/all_to_all | solution.py:150
  204.8 19.1 %collective-permute-done.26 = bf16[168,1008]{1,0:T(8,128)(2,1)} collective-permute-done((bf16[168,1008]{1,0:T(8,128)(2,1)}, bf16[168,1008]{1,0:T(8,128)(2,1)}, u32[]{:S(2)}, u32[]{:S(2)}) %collective-permute-start.26) | collective-permute-done | bytes 338720 | tf_op jit(solution)/shard_map/ppermute | solution.py:71
  225.2 11.3 %collective-permute-done.27 = bf16[168,1008]{1,0:T(8,128)(2,1)S(1)} collective-permute-done((bf16[168,1008]{1,0:T(8,128)(2,1)}, bf16[168,1008]{1,0:T(8,128)(2,1)S(1)}, u32[]{:S(2)}, u32[]{:S(2)}) %collective-permute-start.27) | collective-permute-done | bytes 338720 | tf_op jit(solution)/shard_map/ppermute | solution.py:67
  240.0 8.1 %collective-permute-done.28 = bf16[168,1008]{1,0:T(8,128)(2,1)S(1)} collective-permute-done((bf16[168,1008]{1,0:T(8,128)(2,1)S(1)}, bf16[168,1008]{1,0:T(8,128)(2,1)S(1)}, u32[]{:S(2)}, u32[]{:S(2)}) %collective-permute-start.28) | collective-permute-done | bytes 338720 | tf_op jit(solution)/shard_map/ppermute | solution.py:71
  250.1 8.8 %collective-permute-done.29 = bf16[168,1008]{1,0:T(8,128)(2,1)} collective-permute-done((bf16[168,1008]{1,0:T(8,128)(2,1)S(1)}, bf16[168,1008]{1,0:T(8,128)(2,1)}, u32[]{:S(2)}, u32[]{:S(2)}) %collective-permute-start.29) | collective-permute-done | bytes 338720 | tf_op jit(solution)/shard_map/ppermute | solution.py:67
  263.1 9.4 %collective-permute-start.20 = (bf16[84,128]{1,0:T(8,128)(2,1)S(1)}, bf16[84,128]{1,0:T(8,128)(2,1)S(1)}, u32[]{:S(2)}, u32[]{:S(2)}) collective-permute-start(bf16[84,128]{1,0:T(8,128)(2,1)S(1)} %bitcast.222), channel_id=1, source_target_pairs={{0,4},{4,0},{1,5},{5,1},{2,6},{6,2},{3,7},{7,3},{8,12},{12,8},{9,1... | collective-permute-start | bytes 64520 | tf_op jit(solution)/shard_map/ppermute | solution.py:42
  272.5 5.2 %collective-permute-done.20 = bf16[84,128]{1,0:T(8,128)(2,1)S(1)} collective-permute-done((bf16[84,128]{1,0:T(8,128)(2,1)S(1)}, bf16[84,128]{1,0:T(8,128)(2,1)S(1)}, u32[]{:S(2)}, u32[]{:S(2)}) %collective-permute-start.20) | collective-permute-done | bytes 21536 | tf_op jit(solution)/shard_map/ppermute | solution.py:42
  277.6 3.5 %collective-permute-start.31 = (bf16[168,1008]{1,0:T(8,128)(2,1)S(1)}, bf16[168,1008]{1,0:T(8,128)(2,1)}, u32[]{:S(2)}, u32[]{:S(2)}) collective-permute-start(bf16[168,1008]{1,0:T(8,128)(2,1)S(1)} %get-tuple-element.52), channel_id=1, source_target_pairs={{0,64},{64,128},{128,192},{192,256},{256,320},{320,384},{1,65},{65... | collective-permute-start | bytes 1016072 | tf_op jit(solution)/shard_map/ppermute | solution.py:67
  281.1 7.0 %collective-permute-done.31 = bf16[168,1008]{1,0:T(8,128)(2,1)} collective-permute-done((bf16[168,1008]{1,0:T(8,128)(2,1)S(1)}, bf16[168,1008]{1,0:T(8,128)(2,1)}, u32[]{:S(2)}, u32[]{:S(2)}) %collective-permute-start.31) | collective-permute-done | bytes 338720 | tf_op jit(solution)/shard_map/ppermute | solution.py:67
  292.0 9.9 %collective-permute-done.32 = bf16[168,1008]{1,0:T(8,128)(2,1)S(1)} collective-permute-done((bf16[168,1008]{1,0:T(8,128)(2,1)}, bf16[168,1008]{1,0:T(8,128)(2,1)S(1)}, u32[]{:S(2)}, u32[]{:S(2)}) %collective-permute-start.32) | collective-permute-done | bytes 338720 | tf_op jit(solution)/shard_map/ppermute | solution.py:71
  303.9 3.9 %collective-permute-start.33 = (bf16[168,1008]{1,0:T(8,128)(2,1)S(1)}, bf16[168,1008]{1,0:T(8,128)(2,1)S(1)}, u32[]{:S(2)}, u32[]{:S(2)}) collective-permute-start(bf16[168,1008]{1,0:T(8,128)(2,1)S(1)} %get-tuple-element.54), channel_id=1, source_target_pairs={{0,64},{64,128},{128,192},{192,256},{256,320},{320,384},{384,448},... | collective-permute-start | bytes 1016072 | tf_op jit(solution)/shard_map/ppermute | solution.py:67
  311.1 3.1 collective-permute-done.33
  (150 shorter events, 112.9 us)
Async XLA Ops:
  4.1 34.5 %all-to-all-start = ((bf16[16,84,640]{2,1,0:T(8,128)(2,1)}), bf16[16,84,640]{2,1,0:T(8,128)(2,1)S(1)}, u32[]{:S(2)}, u32[]{:S(2)}) async-start(bf16[16,84,640]{2,1,0:T(8,128)(2,1)} %broadcast_in_dim.86), calls=%async_computation | async-start | bytes 3604480 | tf_op jit(solution)/shard_map/all_to_all | solution.py:92
  11.2 20.4 %collective-permute-start.2 = (bf16[84,640]{1,0:T(8,128)(2,1)S(1)}, bf16[84,640]{1,0:T(8,128)(2,1)S(1)}, u32[]{:S(2)}, u32[]{:S(2)}) collective-permute-start(bf16[84,640]{1,0:T(8,128)(2,1)S(1)} %constant_dynamic-update-slice_fusion), channel_id=1, source_target_pairs={{0,4},{4,0},{1,5},{5,1},{2,6},{6,2},{3,7},{7,3},{8,12},{12,8},{9,1... | collective-permute-start | bytes 322568 | tf_op jit(solution)/shard_map/ppermute | solution.py:42
  39.9 30.2 %all-to-all-start.1 = ((bf16[16,84,640]{2,1,0:T(8,128)(2,1)}), bf16[16,84,640]{2,1,0:T(8,128)(2,1)}, u32[]{:S(2)}, u32[]{:S(2)}) async-start(bf16[16,84,640]{2,1,0:T(8,128)(2,1)} %broadcast_in_dim.87), calls=%async_computation.1 | async-start | bytes 3604480 | tf_op jit(solution)/shard_map/all_to_all | solution.py:92
  44.5 11.7 %collective-permute-start = (bf16[168,1008]{1,0:T(8,128)(2,1)S(1)}, bf16[168,1008]{1,0:T(8,128)(2,1)}, u32[]{:S(2)}, u32[]{:S(2)}) collective-permute-start(bf16[168,1008]{1,0:T(8,128)(2,1)S(1)} %pad_maximum_fusion.4), channel_id=1, source_target_pairs={{0,64},{64,128},{128,192},{192,256},{256,320},{320,384},{384,448},... | collective-permute-start | bytes 1016072 | tf_op jit(solution)/shard_map/ppermute | solution.py:50
  48.4 10.4 %collective-permute-start.1 = (bf16[168,1008]{1,0:T(8,128)(2,1)S(1)}, bf16[168,1008]{1,0:T(8,128)(2,1)}, u32[]{:S(2)}, u32[]{:S(2)}) collective-permute-start(bf16[168,1008]{1,0:T(8,128)(2,1)S(1)} %pad_maximum_fusion.4), channel_id=1, source_target_pairs={{64,0},{128,64},{192,128},{256,192},{320,256},{384,320},{448,384},... | collective-permute-start | bytes 1016072 | tf_op jit(solution)/shard_map/ppermute | solution.py:51
  58.8 16.2 %collective-permute-start.3 = (bf16[168,1008]{1,0:T(8,128)(2,1)}, bf16[168,1008]{1,0:T(8,128)(2,1)}, u32[]{:S(2)}, u32[]{:S(2)}) collective-permute-start(bf16[168,1008]{1,0:T(8,128)(2,1)} %collective-permute-done), channel_id=1, source_target_pairs={{64,128},{128,192},{192,256},{256,320},{320,384},{384,448},{65,129... | collective-permute-start | bytes 1016072 | tf_op jit(solution)/shard_map/ppermute | solution.py:50
  62.6 12.4 %collective-permute-start.4 = (bf16[168,1008]{1,0:T(8,128)(2,1)}, bf16[168,1008]{1,0:T(8,128)(2,1)}, u32[]{:S(2)}, u32[]{:S(2)}) collective-permute-start(bf16[168,1008]{1,0:T(8,128)(2,1)} %collective-permute-done.1), channel_id=1, source_target_pairs={{64,0},{128,64},{192,128},{256,192},{320,256},{384,320},{65,1},{12... | collective-permute-start | bytes 1016072 | tf_op jit(solution)/shard_map/ppermute | solution.py:51
  66.3 39.5 %collective-permute-start.9 = (bf16[4,2,84,640]{3,0,2,1:T(4,128)(2,1)S(1)}, bf16[4,2,84,640]{3,0,2,1:T(4,128)(2,1)S(1)}, u32[]{:S(2)}, u32[]{:S(2)}) collective-permute-start(bf16[4,2,84,640]{3,0,2,1:T(4,128)(2,1)S(1)} %copy.79), channel_id=1, source_target_pairs={{0,32},{32,0},{1,33},{33,1},{2,34},{34,2},{3,35},{35,3},{4,36},{36... | collective-permute-start | bytes 2580488 | tf_op jit(solution)/shard_map/ppermute | solution.py:42
  73.0 36.4 %collective-permute-start.12 = (bf16[4,2,84,640]{3,0,2,1:T(4,128)(2,1)}, bf16[4,2,84,640]{3,0,2,1:T(4,128)(2,1)}, u32[]{:S(2)}, u32[]{:S(2)}) collective-permute-start(bf16[4,2,84,640]{3,0,2,1:T(4,128)(2,1)} %copy.80), channel_id=1, source_target_pairs={{0,32},{32,0},{1,33},{33,1},{2,34},{34,2},{3,35},{35,3},{4,36},{36... | collective-permute-start | bytes 2580488 | tf_op jit(solution)/shard_map/ppermute | solution.py:42
  75.0 13.9 %collective-permute-start.5 = (bf16[168,1008]{1,0:T(8,128)(2,1)}, bf16[168,1008]{1,0:T(8,128)(2,1)}, u32[]{:S(2)}, u32[]{:S(2)}) collective-permute-start(bf16[168,1008]{1,0:T(8,128)(2,1)} %collective-permute-done.3), channel_id=1, source_target_pairs={{128,192},{192,256},{256,320},{320,384},{384,448},{129,193},{193,2... | collective-permute-start | bytes 1016072 | tf_op jit(solution)/shard_map/ppermute | solution.py:50
  78.8 12.4 %collective-permute-start.6 = (bf16[168,1008]{1,0:T(8,128)(2,1)}, bf16[168,1008]{1,0:T(8,128)(2,1)}, u32[]{:S(2)}, u32[]{:S(2)}) collective-permute-start(bf16[168,1008]{1,0:T(8,128)(2,1)} %collective-permute-done.4), channel_id=1, source_target_pairs={{64,0},{128,64},{192,128},{256,192},{320,256},{65,1},{129,65},{193... | collective-permute-start | bytes 1016072 | tf_op jit(solution)/shard_map/ppermute | solution.py:51
  91.2 12.8 %collective-permute-start.7 = (bf16[168,1008]{1,0:T(8,128)(2,1)}, bf16[168,1008]{1,0:T(8,128)(2,1)}, u32[]{:S(2)}, u32[]{:S(2)}) collective-permute-start(bf16[168,1008]{1,0:T(8,128)(2,1)} %collective-permute-done.5), channel_id=1, source_target_pairs={{192,256},{256,320},{320,384},{384,448},{193,257},{257,321},{321,3... | collective-permute-start | bytes 1016072 | tf_op jit(solution)/shard_map/ppermute | solution.py:50
  93.1 12.8 %collective-permute-start.8 = (bf16[168,1008]{1,0:T(8,128)(2,1)}, bf16[168,1008]{1,0:T(8,128)(2,1)}, u32[]{:S(2)}, u32[]{:S(2)}) collective-permute-start(bf16[168,1008]{1,0:T(8,128)(2,1)} %collective-permute-done.6), channel_id=1, source_target_pairs={{64,0},{128,64},{192,128},{256,192},{65,1},{129,65},{193,129},{257... | collective-permute-start | bytes 1016072 | tf_op jit(solution)/shard_map/ppermute | solution.py:51
  105.9 7.5 %collective-permute-start.10 = (bf16[168,1008]{1,0:T(8,128)(2,1)}, bf16[168,1008]{1,0:T(8,128)(2,1)}, u32[]{:S(2)}, u32[]{:S(2)}) collective-permute-start(bf16[168,1008]{1,0:T(8,128)(2,1)} %collective-permute-done.7), channel_id=1, source_target_pairs={{256,320},{320,384},{384,448},{257,321},{321,385},{385,449},{258,3... | collective-permute-start | bytes 1016072 | tf_op jit(solution)/shard_map/ppermute | solution.py:50
  107.9 5.5 %collective-permute-start.11 = (bf16[168,1008]{1,0:T(8,128)(2,1)}, bf16[168,1008]{1,0:T(8,128)(2,1)}, u32[]{:S(2)}, u32[]{:S(2)}) collective-permute-start(bf16[168,1008]{1,0:T(8,128)(2,1)} %collective-permute-done.8), channel_id=1, source_target_pairs={{64,0},{128,64},{192,128},{65,1},{129,65},{193,129},{66,2},{130,66... | collective-permute-start | bytes 1016072 | tf_op jit(solution)/shard_map/ppermute | solution.py:51
  113.4 7.9 %collective-permute-start.13 = (bf16[168,1008]{1,0:T(8,128)(2,1)}, bf16[168,1008]{1,0:T(8,128)(2,1)}, u32[]{:S(2)}, u32[]{:S(2)}) collective-permute-start(bf16[168,1008]{1,0:T(8,128)(2,1)} %collective-permute-done.10), channel_id=1, source_target_pairs={{320,384},{384,448},{321,385},{385,449},{322,386},{386,450},{323,3... | collective-permute-start | bytes 1016072 | tf_op jit(solution)/shard_map/ppermute | solution.py:50
  114.8 6.5 %collective-permute-start.14 = (bf16[168,1008]{1,0:T(8,128)(2,1)}, bf16[168,1008]{1,0:T(8,128)(2,1)}, u32[]{:S(2)}, u32[]{:S(2)}) collective-permute-start(bf16[168,1008]{1,0:T(8,128)(2,1)} %collective-permute-done.11), channel_id=1, source_target_pairs={{64,0},{128,64},{65,1},{129,65},{66,2},{130,66},{67,3},{131,67},{6... | collective-permute-start | bytes 1016072 | tf_op jit(solution)/shard_map/ppermute | solution.py:51
  121.4 5.9 %collective-permute-start.15 = (bf16[168,1008]{1,0:T(8,128)(2,1)}, bf16[168,1008]{1,0:T(8,128)(2,1)}, u32[]{:S(2)}, u32[]{:S(2)}) collective-permute-start(bf16[168,1008]{1,0:T(8,128)(2,1)} %collective-permute-done.13), channel_id=1, source_target_pairs={{384,448},{385,449},{386,450},{387,451},{388,452},{389,453},{390,4... | collective-permute-start | bytes 1016072 | tf_op jit(solution)/shard_map/ppermute | solution.py:50
  126.4 14.2 %collective-permute-start.16 = (bf16[168,1008]{1,0:T(8,128)(2,1)}, bf16[168,1008]{1,0:T(8,128)(2,1)S(1)}, u32[]{:S(2)}, u32[]{:S(2)}) collective-permute-start(bf16[168,1008]{1,0:T(8,128)(2,1)} %collective-permute-done.14), channel_id=1, source_target_pairs={{64,0},{65,1},{66,2},{67,3},{68,4},{69,5},{70,6},{71,7},{72,8},{73... | collective-permute-start | bytes 1016072 | tf_op jit(solution)/shard_map/ppermute | solution.py:51
  170.6 6.8 %collective-permute-start.23 = (bf16[168,1008]{1,0:T(8,128)(2,1)}, bf16[168,1008]{1,0:T(8,128)(2,1)S(1)}, u32[]{:S(2)}, u32[]{:S(2)}) collective-permute-start(bf16[168,1008]{1,0:T(8,128)(2,1)} %fusion.28), channel_id=1, source_target_pairs={{0,64},{64,128},{1,65},{65,129},{2,66},{66,130},{3,67},{67,131},{4... | collective-permute-start | bytes 1016072 | tf_op jit(solution)/shard_map/ppermute | solution.py:67
  183.0 7.2 %collective-permute-start.25 = (bf16[168,1008]{1,0:T(8,128)(2,1)}, bf16[168,1008]{1,0:T(8,128)(2,1)}, u32[]{:S(2)}, u32[]{:S(2)}) collective-permute-start(bf16[168,1008]{1,0:T(8,128)(2,1)} %get-tuple-element.46), channel_id=1, source_target_pairs={{0,64},{64,128},{128,192},{1,65},{65,129},{129,193},{2,66},{66,130... | collective-permute-start | bytes 1016072 | tf_op jit(solution)/shard_map/ppermute | solution.py:67
  186.6 17.7 %all-to-all-start.2 = ((bf16[16,2,84,128]{3,1,2,0:T(2,128)(2,1)}), bf16[16,2,84,128]{3,1,2,0:T(2,128)(2,1)S(1)}, u32[]{:S(2)}, u32[]{:S(2)}) async-start(bf16[16,2,84,128]{3,1,2,0:T(2,128)(2,1)} %copy.86), calls=%async_computation.2 | async-start | bytes 1376256 | tf_op jit(solution)/shard_map/all_to_all | solution.py:150
  192.4 31.5 %collective-permute-start.26 = (bf16[168,1008]{1,0:T(8,128)(2,1)}, bf16[168,1008]{1,0:T(8,128)(2,1)}, u32[]{:S(2)}, u32[]{:S(2)}) collective-permute-start(bf16[168,1008]{1,0:T(8,128)(2,1)} %get-tuple-element.72), channel_id=1, source_target_pairs={{320,256},{384,320},{448,384},{321,257},{385,321},{449,385},{322,2... | collective-permute-start | bytes 1016072 | tf_op jit(solution)/shard_map/ppermute | solution.py:71
  223.9 12.6 %collective-permute-start.27 = (bf16[168,1008]{1,0:T(8,128)(2,1)}, bf16[168,1008]{1,0:T(8,128)(2,1)S(1)}, u32[]{:S(2)}, u32[]{:S(2)}) collective-permute-start(bf16[168,1008]{1,0:T(8,128)(2,1)} %get-tuple-element.48), channel_id=1, source_target_pairs={{0,64},{64,128},{128,192},{192,256},{1,65},{65,129},{129,193},{193... | collective-permute-start | bytes 1016072 | tf_op jit(solution)/shard_map/ppermute | solution.py:67
  237.8 10.3 %collective-permute-start.28 = (bf16[168,1008]{1,0:T(8,128)(2,1)S(1)}, bf16[168,1008]{1,0:T(8,128)(2,1)S(1)}, u32[]{:S(2)}, u32[]{:S(2)}) collective-permute-start(bf16[168,1008]{1,0:T(8,128)(2,1)S(1)} %get-tuple-element.70), channel_id=1, source_target_pairs={{256,192},{320,256},{384,320},{448,384},{257,193},{321,257},{385,3... | collective-permute-start | bytes 1016072 | tf_op jit(solution)/shard_map/ppermute | solution.py:71
  248.1 10.7 %collective-permute-start.29 = (bf16[168,1008]{1,0:T(8,128)(2,1)S(1)}, bf16[168,1008]{1,0:T(8,128)(2,1)}, u32[]{:S(2)}, u32[]{:S(2)}) collective-permute-start(bf16[168,1008]{1,0:T(8,128)(2,1)S(1)} %get-tuple-element.50), channel_id=1, source_target_pairs={{0,64},{64,128},{128,192},{192,256},{256,320},{1,65},{65,129},{129... | collective-permute-start | bytes 1016072 | tf_op jit(solution)/shard_map/ppermute | solution.py:67
  260.8 16.9 %collective-permute-start.30 = (bf16[168,1008]{1,0:T(8,128)(2,1)}, bf16[168,1008]{1,0:T(8,128)(2,1)S(1)}, u32[]{:S(2)}, u32[]{:S(2)}) collective-permute-start(bf16[168,1008]{1,0:T(8,128)(2,1)} %get-tuple-element.68), channel_id=1, source_target_pairs={{192,128},{256,192},{320,256},{384,320},{448,384},{193,129},{257,1... | collective-permute-start | bytes 1016072 | tf_op jit(solution)/shard_map/ppermute | solution.py:71
  263.1 14.5 %collective-permute-start.20 = (bf16[84,128]{1,0:T(8,128)(2,1)S(1)}, bf16[84,128]{1,0:T(8,128)(2,1)S(1)}, u32[]{:S(2)}, u32[]{:S(2)}) collective-permute-start(bf16[84,128]{1,0:T(8,128)(2,1)S(1)} %bitcast.222), channel_id=1, source_target_pairs={{0,4},{4,0},{1,5},{5,1},{2,6},{6,2},{3,7},{7,3},{8,12},{12,8},{9,1... | collective-permute-start | bytes 64520 | tf_op jit(solution)/shard_map/ppermute | solution.py:42
  277.6 10.4 %collective-permute-start.31 = (bf16[168,1008]{1,0:T(8,128)(2,1)S(1)}, bf16[168,1008]{1,0:T(8,128)(2,1)}, u32[]{:S(2)}, u32[]{:S(2)}) collective-permute-start(bf16[168,1008]{1,0:T(8,128)(2,1)S(1)} %get-tuple-element.52), channel_id=1, source_target_pairs={{0,64},{64,128},{128,192},{192,256},{256,320},{320,384},{1,65},{65... | collective-permute-start | bytes 1016072 | tf_op jit(solution)/shard_map/ppermute | solution.py:67
  290.1 11.8 %collective-permute-start.32 = (bf16[168,1008]{1,0:T(8,128)(2,1)}, bf16[168,1008]{1,0:T(8,128)(2,1)S(1)}, u32[]{:S(2)}, u32[]{:S(2)}) collective-permute-start(bf16[168,1008]{1,0:T(8,128)(2,1)} %get-tuple-element.66), channel_id=1, source_target_pairs={{128,64},{192,128},{256,192},{320,256},{384,320},{448,384},{129,65... | collective-permute-start | bytes 1016072 | tf_op jit(solution)/shard_map/ppermute | solution.py:71
  302.0 9.1 %collective-permute-start.34 = (bf16[168,1008]{1,0:T(8,128)(2,1)S(1)}, bf16[168,1008]{1,0:T(8,128)(2,1)S(1)}, u32[]{:S(2)}, u32[]{:S(2)}) collective-permute-start(bf16[168,1008]{1,0:T(8,128)(2,1)S(1)} %fusion.22), channel_id=1, source_target_pairs={{64,0},{128,64},{192,128},{256,192},{320,256},{384,320},{448,384},... | collective-permute-start | bytes 1016072 | tf_op jit(solution)/shard_map/ppermute | solution.py:71
  303.9 10.4 %collective-permute-start.33 = (bf16[168,1008]{1,0:T(8,128)(2,1)S(1)}, bf16[168,1008]{1,0:T(8,128)(2,1)S(1)}, u32[]{:S(2)}, u32[]{:S(2)}) collective-permute-start(bf16[168,1008]{1,0:T(8,128)(2,1)S(1)} %get-tuple-element.54), channel_id=1, source_target_pairs={{0,64},{64,128},{128,192},{192,256},{256,320},{320,384},{384,448},... | collective-permute-start | bytes 1016072 | tf_op jit(solution)/shard_map/ppermute | solution.py:67
  (23 other events, 197.5 us)

commit v8 on v2

--- a/solution.py
+++ b/solution.py
@@ -46,7 +46,9 @@
     from_left, from_right = [], []
     right = left = shard
     for step in range(ZL - 1):
-        right, left, _ = lax.optimization_barrier((right, left, ties.get(step, ())))
+        other = (from_left[step - 2], from_right[step - 2]) if step > 1 else ((), ())
+        right, _ = lax.optimization_barrier((right, (other[1], ties.get(step, ()))))
+        left, _ = lax.optimization_barrier((left, other[0]))
         right = lax.ppermute(right, "zl", [(i, i + 1) for i in range(step, ZL - 1)])
         left = lax.ppermute(left, "zl", [(i, i - 1) for i in range(1, ZL - step)])
         from_left.append(right)

time: 278 us -> 277 us (level)
  waiting for transfers between devices: 81.5 us -> 68.2 us
  starting transfers between devices: 124 us -> 137 us
    ppermute x7, starting transfers between devices: 34 us -> 44 us  [line_scatter(): right = lax.ppermute(to_right, 'zl', [(i, i + 1) for i in range(step + 1)])]
    ppermute x7, waiting for transfers between devices: 42.7 us -> 34.9 us  [line_gather(): left = lax.ppermute(left, 'zl', [(i, i - 1) for i in range(1, ZL - step)])]
    ppermute x7, waiting for transfers between devices: 5.13 us -> 0.02 us  [line_gather(): right = lax.ppermute(right, 'zl', [(i, i + 1) for i in range(step, ZL - 1)])]
    unnamed x77 -> x69, local copies, waits for them, and re-layouts: 13.4 us -> 13.4 us
  transfers between devices with their start and end apart: 38 -> 38, of which waited for: 17 -> 15; matrix products, arithmetic and copies ran while one was open for 14% -> 14% of each run, Pallas kernels for 0% -> 0%
where the time goes in v8:
time: 277 us; the launch traced here: 275 us
  starting transfers between devices  137 us (49%)
  waiting for transfers between devices  68.2 us (25%)
  local copies, waits for them, and re-layouts  36.6 us (13%)
  other arithmetic  22.8 us (8%)
  matrix products  9.36 us (3%)
    ppermute x7, starting transfers between devices, line_scatter(): right = lax.ppermute(to_right, 'zl', [(i, i + 1) for i in range(step + 1)])  44 us
    ppermute x7, starting transfers between devices, swap(): return lax.ppermute(values, axis_name, [(0, 1), (1, 0)])  36.6 us
    ppermute x7, waiting for transfers between devices, line_gather(): left = lax.ppermute(left, 'zl', [(i, i - 1) for i in range(1, ZL - step)])  34.9 us
    all_to_all x2, starting transfers between devices, spread(): got = lax.all_to_all(copies, ('y', 'x'), 0, 0)  16.6 us
    ppermute x7, starting transfers between devices, line_gather(): right = lax.ppermute(right, 'zl', [(i, i + 1) for i in range(step, ZL - 1)])  14.1 us
    ppermute x7, waiting for transfers between devices, line_scatter(): right = lax.ppermute(to_right, 'zl', [(i, i + 1) for i in range(step + 1)])  13.5 us
    unnamed x69, local copies, waits for them, and re-layouts  13.4 us
    convert_element_type x6, other arithmetic, line_scatter(): to_left.astype(jnp.bfloat16)  11.2 us
  transfers between devices with their start and end apart: 38, of which 15 were waited for; matrix products, arithmetic and copies ran while one was open for 14% of the time, Pallas kernels for 0%

profile of v8, /device:TPU:6, one launch (start us, length us, event | category | flops | bytes accessed | tf_op | source)
XLA Modules:
  0.0 275.1 jit_solution(16327721832960008083)
XLA Ops:
  4.1 9.4 %all-to-all-start = ((bf16[16,84,640]{2,1,0:T(8,128)(2,1)}), bf16[16,84,640]{2,1,0:T(8,128)(2,1)S(1)}, u32[]{:S(2)}, u32[]{:S(2)}) async-start(bf16[16,84,640]{2,1,0:T(8,128)(2,1)} %broadcast_in_dim.86), calls=%async_computation | async-start | bytes 3604480 | tf_op jit(solution)/shard_map/all_to_all | solution.py:90
  13.5 13.9 %collective-permute-start.1 = (bf16[84,640]{1,0:T(8,128)(2,1)S(1)}, bf16[84,640]{1,0:T(8,128)(2,1)S(1)}, u32[]{:S(2)}, u32[]{:S(2)}) collective-permute-start(bf16[84,640]{1,0:T(8,128)(2,1)S(1)} %constant_dynamic-update-slice_fusion), channel_id=1, source_target_pairs={{0,4},{4,0},{1,5},{5,1},{2,6},{6,2},{3,7},{7,3},{8,12},{12,8},{9,1... | collective-permute-start | bytes 322568 | tf_op jit(solution)/shard_map/ppermute | solution.py:42
  27.4 7.6 %collective-permute-done.1 = bf16[84,640]{1,0:T(8,128)(2,1)S(1)} collective-permute-done((bf16[84,640]{1,0:T(8,128)(2,1)S(1)}, bf16[84,640]{1,0:T(8,128)(2,1)S(1)}, u32[]{:S(2)}, u32[]{:S(2)}) %collective-permute-start.1) | collective-permute-done | bytes 107552 | tf_op jit(solution)/shard_map/ppermute | solution.py:42
  36.8 7.2 %all-to-all-start.1 = ((bf16[16,84,640]{2,1,0:T(8,128)(2,1)}), bf16[16,84,640]{2,1,0:T(8,128)(2,1)S(1)}, u32[]{:S(2)}, u32[]{:S(2)}) async-start(bf16[16,84,640]{2,1,0:T(8,128)(2,1)} %broadcast_in_dim.87), calls=%async_computation.1 | async-start | bytes 3604480 | tf_op jit(solution)/shard_map/all_to_all | solution.py:90
  45.5 5.5 %collective-permute-start = (bf16[168,1008]{1,0:T(8,128)(2,1)S(1)}, bf16[168,1008]{1,0:T(8,128)(2,1)}, u32[]{:S(2)}, u32[]{:S(2)}) collective-permute-start(bf16[168,1008]{1,0:T(8,128)(2,1)S(1)} %pad_maximum_fusion.4), channel_id=1, source_target_pairs={{0,64},{64,128},{128,192},{192,256},{256,320},{320,384},{384,448},... | collective-permute-start | bytes 1016072 | tf_op jit(solution)/shard_map/ppermute | solution.py:52
  51.0 4.5 %collective-permute-done.3 = bf16[168,1008]{1,0:T(8,128)(2,1)S(1)} collective-permute-done((bf16[168,1008]{1,0:T(8,128)(2,1)S(1)}, bf16[168,1008]{1,0:T(8,128)(2,1)S(1)}, u32[]{:S(2)}, u32[]{:S(2)}) %collective-permute-start.3) | collective-permute-done | bytes 338720 | tf_op jit(solution)/shard_map/ppermute | solution.py:53
  63.0 2.9 %collective-permute-done.5 = bf16[168,1008]{1,0:T(8,128)(2,1)S(1)} collective-permute-done((bf16[168,1008]{1,0:T(8,128)(2,1)S(1)}, bf16[168,1008]{1,0:T(8,128)(2,1)S(1)}, u32[]{:S(2)}, u32[]{:S(2)}) %collective-permute-start.5) | collective-permute-done | bytes 338720 | tf_op jit(solution)/shard_map/ppermute | solution.py:53
  71.9 7.6 %collective-permute-done.7 = bf16[168,1008]{1,0:T(8,128)(2,1)} collective-permute-done((bf16[168,1008]{1,0:T(8,128)(2,1)S(1)}, bf16[168,1008]{1,0:T(8,128)(2,1)}, u32[]{:S(2)}, u32[]{:S(2)}) %collective-permute-start.7) | collective-permute-done | bytes 338720 | tf_op jit(solution)/shard_map/ppermute | solution.py:53
  82.3 9.8 %collective-permute-done.10 = bf16[168,1008]{1,0:T(8,128)(2,1)S(1)} collective-permute-done((bf16[168,1008]{1,0:T(8,128)(2,1)}, bf16[168,1008]{1,0:T(8,128)(2,1)S(1)}, u32[]{:S(2)}, u32[]{:S(2)}) %collective-permute-start.10) | collective-permute-done | bytes 338720 | tf_op jit(solution)/shard_map/ppermute | solution.py:53
  94.9 10.0 %collective-permute-done.12 = bf16[168,1008]{1,0:T(8,128)(2,1)} collective-permute-done((bf16[168,1008]{1,0:T(8,128)(2,1)S(1)}, bf16[168,1008]{1,0:T(8,128)(2,1)}, u32[]{:S(2)}, u32[]{:S(2)}) %collective-permute-start.12) | collective-permute-done | bytes 338720 | tf_op jit(solution)/shard_map/ppermute | solution.py:53
  112.4 2.1 pad_maximum_fusion
  114.5 3.0 %reshape.181 = bf16[1344,1280]{1,0:T(8,128)(2,1)S(1)} reshape(bf16[4,2,2,84,1280]{4,3,2,1,0:T(8,128)(2,1)} %pad_maximum_fusion) | data formatting | bytes 6881280 | tf_op jit(solution)/shard_map/reshape | solution.py:108
  117.5 3.6 %copy.83 = bf16[1280,1344]{1,0:T(8,128)(2,1)} copy(bf16[1280,1344]{0,1:T(8,128)(2,1)S(1)} %bitcast.203) | data formatting | bytes 6881280 | tf_op jit(solution)/shard_map/dot_general | solution.py:22
  134.1 4.6 %fusion.71 = f32[2,5,128,1008]{2,3,1,0:T(8,128)S(1)} fusion(bf16[2,5,128,1344]{3,2,1,0:T(8,128)(2,1)S(1)} %bitcast.214, bf16[1344,1008,1,1]{1,0,3,2:T(8,128)(2,1)S(1)} %bitcast.217), kind=kOutput, calls=%fused_computation.170 | convolution fusion | flops 3468165120 | bytes 11311104 | tf_op jit(solution)/shard_map/dot_general | solution.py:22
  139.1 2.1 collective-permute-start.17
  153.3 4.0 %convolution_convert_fusion = bf16[1344,1008]{1,0:T(8,128)(2,1)S(1)} fusion(bf16[1344,1280]{1,0:T(8,128)(2,1)S(1)} %reshape.181, bf16[512,1008]{0,1:T(8,128)(2,1)S(1)} %get-tuple-element.110, bf16[128,1008]{0,1:T(8,128)(2,1)S(1)} %broadcast_select_fusion.4, bf16[512,1008]{0,1:T(8,128)(2,1)S(1)} %get-tuple-element.109, bf16[128,1008]{0,1:T(8,128)(2,1)S(1)} %copy-done.24), kind=kOutput, calls=%fused_computation | convolution fusion | flops 3479841792 | bytes 8730624 | tf_op jit(solution)/shard_map/dot_general | solution.py:22
  157.4 5.1 %collective-permute-start.21 = (bf16[168,1008]{1,0:T(8,128)(2,1)S(1)}, bf16[168,1008]{1,0:T(8,128)(2,1)S(1)}, u32[]{:S(2)}, u32[]{:S(2)}) collective-permute-start(bf16[168,1008]{1,0:T(8,128)(2,1)S(1)} %get-tuple-element.40), channel_id=1, source_target_pairs={{0,64},{1,65},{2,66},{3,67},{4,68},{5,69},{6,70},{7,71},{8,72},{9,... | collective-permute-start | bytes 1016072 | tf_op jit(solution)/shard_map/ppermute | solution.py:70
  166.9 3.2 %collective-permute-done.21 = bf16[168,1008]{1,0:T(8,128)(2,1)S(1)} collective-permute-done((bf16[168,1008]{1,0:T(8,128)(2,1)S(1)}, bf16[168,1008]{1,0:T(8,128)(2,1)S(1)}, u32[]{:S(2)}, u32[]{:S(2)}) %collective-permute-start.21) | collective-permute-done | bytes 338720 | tf_op jit(solution)/shard_map/ppermute | solution.py:70
  170.1 2.2 fusion.27
  172.3 5.1 %collective-permute-start.23 = (bf16[168,1008]{1,0:T(8,128)(2,1)}, bf16[168,1008]{1,0:T(8,128)(2,1)}, u32[]{:S(2)}, u32[]{:S(2)}) collective-permute-start(bf16[168,1008]{1,0:T(8,128)(2,1)} %get-tuple-element.42), channel_id=1, source_target_pairs={{0,64},{64,128},{1,65},{65,129},{2,66},{66,130},{3,67},{67,131},{4... | collective-permute-start | bytes 1016072 | tf_op jit(solution)/shard_map/ppermute | solution.py:70
  183.1 7.2 %all-to-all-start.2 = ((bf16[16,2,84,128]{3,1,2,0:T(2,128)(2,1)}), bf16[16,2,84,128]{3,1,2,0:T(2,128)(2,1)S(1)}, u32[]{:S(2)}, u32[]{:S(2)}) async-start(bf16[16,2,84,128]{3,1,2,0:T(2,128)(2,1)} %copy.86), calls=%async_computation.2 | async-start | bytes 1376256 | tf_op jit(solution)/shard_map/all_to_all | solution.py:149
  190.4 2.2 fusion.26
  196.0 4.2 %all-to-all-done.2 = bf16[16,2,84,128]{3,1,2,0:T(2,128)(2,1)S(1)} async-done(((bf16[16,2,84,128]{3,1,2,0:T(2,128)(2,1)}), bf16[16,2,84,128]{3,1,2,0:T(2,128)(2,1)S(1)}, u32[]{:S(2)}, u32[]{:S(2)}) %all-to-all-start.2) | async-done | bytes 688160 | tf_op jit(solution)/shard_map/all_to_all | solution.py:149
  202.9 4.0 %collective-permute-start.27 = (bf16[168,1008]{1,0:T(8,128)(2,1)}, bf16[168,1008]{1,0:T(8,128)(2,1)S(1)}, u32[]{:S(2)}, u32[]{:S(2)}) collective-permute-start(bf16[168,1008]{1,0:T(8,128)(2,1)} %get-tuple-element.46), channel_id=1, source_target_pairs={{0,64},{64,128},{128,192},{192,256},{1,65},{65,129},{129,193},{193... | collective-permute-start | bytes 1016072 | tf_op jit(solution)/shard_map/ppermute | solution.py:70
  208.3 4.2 %collective-permute-done.27 = bf16[168,1008]{1,0:T(8,128)(2,1)S(1)} collective-permute-done((bf16[168,1008]{1,0:T(8,128)(2,1)}, bf16[168,1008]{1,0:T(8,128)(2,1)S(1)}, u32[]{:S(2)}, u32[]{:S(2)}) %collective-permute-start.27) | collective-permute-done | bytes 338720 | tf_op jit(solution)/shard_map/ppermute | solution.py:70
  214.4 4.3 %collective-permute-start.29 = (bf16[168,1008]{1,0:T(8,128)(2,1)}, bf16[168,1008]{1,0:T(8,128)(2,1)S(1)}, u32[]{:S(2)}, u32[]{:S(2)}) collective-permute-start(bf16[168,1008]{1,0:T(8,128)(2,1)} %get-tuple-element.48), channel_id=1, source_target_pairs={{0,64},{64,128},{128,192},{192,256},{256,320},{1,65},{65,129},{129... | collective-permute-start | bytes 1016072 | tf_op jit(solution)/shard_map/ppermute | solution.py:70
  220.2 12.8 %collective-permute-start.20 = (bf16[84,128]{1,0:T(8,128)(2,1)S(1)}, bf16[84,128]{1,0:T(8,128)(2,1)S(1)}, u32[]{:S(2)}, u32[]{:S(2)}) collective-permute-start(bf16[84,128]{1,0:T(8,128)(2,1)S(1)} %bitcast.222), channel_id=1, source_target_pairs={{0,4},{4,0},{1,5},{5,1},{2,6},{6,2},{3,7},{7,3},{8,12},{12,8},{9,1... | collective-permute-start | bytes 64520 | tf_op jit(solution)/shard_map/ppermute | solution.py:42
  235.3 3.0 %collective-permute-start.31 = (bf16[168,1008]{1,0:T(8,128)(2,1)S(1)}, bf16[168,1008]{1,0:T(8,128)(2,1)}, u32[]{:S(2)}, u32[]{:S(2)}) collective-permute-start(bf16[168,1008]{1,0:T(8,128)(2,1)S(1)} %get-tuple-element.50), channel_id=1, source_target_pairs={{0,64},{64,128},{128,192},{192,256},{256,320},{320,384},{1,65},{65... | collective-permute-start | bytes 1016072 | tf_op jit(solution)/shard_map/ppermute | solution.py:70
  239.7 3.3 %collective-permute-done.31 = bf16[168,1008]{1,0:T(8,128)(2,1)} collective-permute-done((bf16[168,1008]{1,0:T(8,128)(2,1)S(1)}, bf16[168,1008]{1,0:T(8,128)(2,1)}, u32[]{:S(2)}, u32[]{:S(2)}) %collective-permute-start.31) | collective-permute-done | bytes 338720 | tf_op jit(solution)/shard_map/ppermute | solution.py:70
  244.3 20.6 %collective-permute-start.33 = (bf16[168,1008]{1,0:T(8,128)(2,1)S(1)}, bf16[168,1008]{1,0:T(8,128)(2,1)S(1)}, u32[]{:S(2)}, u32[]{:S(2)}) collective-permute-start(bf16[168,1008]{1,0:T(8,128)(2,1)S(1)} %get-tuple-element.52), channel_id=1, source_target_pairs={{0,64},{64,128},{128,192},{192,256},{256,320},{320,384},{384,448},... | collective-permute-start | bytes 1016072 | tf_op jit(solution)/shard_map/ppermute | solution.py:70
  266.9 2.8 %collective-permute-done.33 = bf16[168,1008]{1,0:T(8,128)(2,1)S(1)} collective-permute-done((bf16[168,1008]{1,0:T(8,128)(2,1)S(1)}, bf16[168,1008]{1,0:T(8,128)(2,1)S(1)}, u32[]{:S(2)}, u32[]{:S(2)}) %collective-permute-start.33) | collective-permute-done | bytes 338720 | tf_op jit(solution)/shard_map/ppermute | solution.py:70
  269.6 4.4 %collective-permute-done.34 = bf16[168,1008]{1,0:T(8,128)(2,1)S(1)} collective-permute-done((bf16[168,1008]{1,0:T(8,128)(2,1)S(1)}, bf16[168,1008]{1,0:T(8,128)(2,1)S(1)}, u32[]{:S(2)}, u32[]{:S(2)}) %collective-permute-start.34) | collective-permute-done | bytes 338720 | tf_op jit(solution)/shard_map/ppermute | solution.py:71
  (169 shorter events, 87.0 us)
Async XLA Ops:
  4.1 30.9 %all-to-all-start = ((bf16[16,84,640]{2,1,0:T(8,128)(2,1)}), bf16[16,84,640]{2,1,0:T(8,128)(2,1)S(1)}, u32[]{:S(2)}, u32[]{:S(2)}) async-start(bf16[16,84,640]{2,1,0:T(8,128)(2,1)} %broadcast_in_dim.86), calls=%async_computation | async-start | bytes 3604480 | tf_op jit(solution)/shard_map/all_to_all | solution.py:90
  13.5 21.5 %collective-permute-start.1 = (bf16[84,640]{1,0:T(8,128)(2,1)S(1)}, bf16[84,640]{1,0:T(8,128)(2,1)S(1)}, u32[]{:S(2)}, u32[]{:S(2)}) collective-permute-start(bf16[84,640]{1,0:T(8,128)(2,1)S(1)} %constant_dynamic-update-slice_fusion), channel_id=1, source_target_pairs={{0,4},{4,0},{1,5},{5,1},{2,6},{6,2},{3,7},{7,3},{8,12},{12,8},{9,1... | collective-permute-start | bytes 322568 | tf_op jit(solution)/shard_map/ppermute | solution.py:42
  36.8 31.8 %all-to-all-start.1 = ((bf16[16,84,640]{2,1,0:T(8,128)(2,1)}), bf16[16,84,640]{2,1,0:T(8,128)(2,1)S(1)}, u32[]{:S(2)}, u32[]{:S(2)}) async-start(bf16[16,84,640]{2,1,0:T(8,128)(2,1)} %broadcast_in_dim.87), calls=%async_computation.1 | async-start | bytes 3604480 | tf_op jit(solution)/shard_map/all_to_all | solution.py:90
  44.2 11.3 %collective-permute-start.3 = (bf16[168,1008]{1,0:T(8,128)(2,1)S(1)}, bf16[168,1008]{1,0:T(8,128)(2,1)S(1)}, u32[]{:S(2)}, u32[]{:S(2)}) collective-permute-start(bf16[168,1008]{1,0:T(8,128)(2,1)S(1)} %pad_maximum_fusion.4), channel_id=1, source_target_pairs={{64,0},{128,64},{192,128},{256,192},{320,256},{384,320},{448,384},... | collective-permute-start | bytes 1016072 | tf_op jit(solution)/shard_map/ppermute | solution.py:53
  45.5 11.3 %collective-permute-start = (bf16[168,1008]{1,0:T(8,128)(2,1)S(1)}, bf16[168,1008]{1,0:T(8,128)(2,1)}, u32[]{:S(2)}, u32[]{:S(2)}) collective-permute-start(bf16[168,1008]{1,0:T(8,128)(2,1)S(1)} %pad_maximum_fusion.4), channel_id=1, source_target_pairs={{0,64},{64,128},{128,192},{192,256},{256,320},{320,384},{384,448},... | collective-permute-start | bytes 1016072 | tf_op jit(solution)/shard_map/ppermute | solution.py:52
  55.5 10.4 %collective-permute-start.5 = (bf16[168,1008]{1,0:T(8,128)(2,1)S(1)}, bf16[168,1008]{1,0:T(8,128)(2,1)S(1)}, u32[]{:S(2)}, u32[]{:S(2)}) collective-permute-start(bf16[168,1008]{1,0:T(8,128)(2,1)S(1)} %collective-permute-done.3), channel_id=1, source_target_pairs={{64,0},{128,64},{192,128},{256,192},{320,256},{384,320},{65,1},{12... | collective-permute-start | bytes 1016072 | tf_op jit(solution)/shard_map/ppermute | solution.py:53
  56.8 10.4 %collective-permute-start.2 = (bf16[168,1008]{1,0:T(8,128)(2,1)}, bf16[168,1008]{1,0:T(8,128)(2,1)}, u32[]{:S(2)}, u32[]{:S(2)}) collective-permute-start(bf16[168,1008]{1,0:T(8,128)(2,1)} %collective-permute-done), channel_id=1, source_target_pairs={{64,128},{128,192},{192,256},{256,320},{320,384},{384,448},{65,129... | collective-permute-start | bytes 1016072 | tf_op jit(solution)/shard_map/ppermute | solution.py:52
  61.1 32.3 %collective-permute-start.8 = (bf16[4,2,84,640]{3,0,2,1:T(4,128)(2,1)}, bf16[4,2,84,640]{3,0,2,1:T(4,128)(2,1)}, u32[]{:S(2)}, u32[]{:S(2)}) collective-permute-start(bf16[4,2,84,640]{3,0,2,1:T(4,128)(2,1)} %copy.79), channel_id=1, source_target_pairs={{0,32},{32,0},{1,33},{33,1},{2,34},{34,2},{3,35},{35,3},{4,36},{36... | collective-permute-start | bytes 2580488 | tf_op jit(solution)/shard_map/ppermute | solution.py:42
  65.9 13.7 %collective-permute-start.7 = (bf16[168,1008]{1,0:T(8,128)(2,1)S(1)}, bf16[168,1008]{1,0:T(8,128)(2,1)}, u32[]{:S(2)}, u32[]{:S(2)}) collective-permute-start(bf16[168,1008]{1,0:T(8,128)(2,1)S(1)} %collective-permute-done.5), channel_id=1, source_target_pairs={{64,0},{128,64},{192,128},{256,192},{320,256},{65,1},{129,65},{193... | collective-permute-start | bytes 1016072 | tf_op jit(solution)/shard_map/ppermute | solution.py:53
  67.2 13.7 %collective-permute-start.4 = (bf16[168,1008]{1,0:T(8,128)(2,1)}, bf16[168,1008]{1,0:T(8,128)(2,1)}, u32[]{:S(2)}, u32[]{:S(2)}) collective-permute-start(bf16[168,1008]{1,0:T(8,128)(2,1)} %collective-permute-done.2), channel_id=1, source_target_pairs={{128,192},{192,256},{256,320},{320,384},{384,448},{129,193},{193,2... | collective-permute-start | bytes 1016072 | tf_op jit(solution)/shard_map/ppermute | solution.py:52
  70.0 37.5 %collective-permute-start.13 = (bf16[4,2,84,640]{3,0,2,1:T(4,128)(2,1)S(1)}, bf16[4,2,84,640]{3,0,2,1:T(4,128)(2,1)}, u32[]{:S(2)}, u32[]{:S(2)}) collective-permute-start(bf16[4,2,84,640]{3,0,2,1:T(4,128)(2,1)S(1)} %copy.80), channel_id=1, source_target_pairs={{0,32},{32,0},{1,33},{33,1},{2,34},{34,2},{3,35},{35,3},{4,36},{36... | collective-permute-start | bytes 2580488 | tf_op jit(solution)/shard_map/ppermute | solution.py:42
  79.6 12.6 %collective-permute-start.10 = (bf16[168,1008]{1,0:T(8,128)(2,1)}, bf16[168,1008]{1,0:T(8,128)(2,1)S(1)}, u32[]{:S(2)}, u32[]{:S(2)}) collective-permute-start(bf16[168,1008]{1,0:T(8,128)(2,1)} %collective-permute-done.7), channel_id=1, source_target_pairs={{64,0},{128,64},{192,128},{256,192},{65,1},{129,65},{193,129},{257... | collective-permute-start | bytes 1016072 | tf_op jit(solution)/shard_map/ppermute | solution.py:53
  80.9 12.6 %collective-permute-start.6 = (bf16[168,1008]{1,0:T(8,128)(2,1)}, bf16[168,1008]{1,0:T(8,128)(2,1)}, u32[]{:S(2)}, u32[]{:S(2)}) collective-permute-start(bf16[168,1008]{1,0:T(8,128)(2,1)} %collective-permute-done.4), channel_id=1, source_target_pairs={{192,256},{256,320},{320,384},{384,448},{193,257},{257,321},{321,3... | collective-permute-start | bytes 1016072 | tf_op jit(solution)/shard_map/ppermute | solution.py:52
  92.1 12.8 %collective-permute-start.12 = (bf16[168,1008]{1,0:T(8,128)(2,1)S(1)}, bf16[168,1008]{1,0:T(8,128)(2,1)}, u32[]{:S(2)}, u32[]{:S(2)}) collective-permute-start(bf16[168,1008]{1,0:T(8,128)(2,1)S(1)} %collective-permute-done.10), channel_id=1, source_target_pairs={{64,0},{128,64},{192,128},{65,1},{129,65},{193,129},{66,2},{130,66... | collective-permute-start | bytes 1016072 | tf_op jit(solution)/shard_map/ppermute | solution.py:53
  93.4 15.4 %collective-permute-start.9 = (bf16[168,1008]{1,0:T(8,128)(2,1)}, bf16[168,1008]{1,0:T(8,128)(2,1)}, u32[]{:S(2)}, u32[]{:S(2)}) collective-permute-start(bf16[168,1008]{1,0:T(8,128)(2,1)} %collective-permute-done.6), channel_id=1, source_target_pairs={{256,320},{320,384},{384,448},{257,321},{321,385},{385,449},{258,3... | collective-permute-start | bytes 1016072 | tf_op jit(solution)/shard_map/ppermute | solution.py:52
  104.9 16.2 %collective-permute-start.15 = (bf16[168,1008]{1,0:T(8,128)(2,1)}, bf16[168,1008]{1,0:T(8,128)(2,1)}, u32[]{:S(2)}, u32[]{:S(2)}) collective-permute-start(bf16[168,1008]{1,0:T(8,128)(2,1)} %collective-permute-done.12), channel_id=1, source_target_pairs={{64,0},{128,64},{65,1},{129,65},{66,2},{130,66},{67,3},{131,67},{6... | collective-permute-start | bytes 1016072 | tf_op jit(solution)/shard_map/ppermute | solution.py:53
  110.9 11.6 %collective-permute-start.14 = (bf16[168,1008]{1,0:T(8,128)(2,1)}, bf16[168,1008]{1,0:T(8,128)(2,1)}, u32[]{:S(2)}, u32[]{:S(2)}) collective-permute-start(bf16[168,1008]{1,0:T(8,128)(2,1)} %collective-permute-done.11), channel_id=1, source_target_pairs={{384,448},{385,449},{386,450},{387,451},{388,452},{389,453},{390,4... | collective-permute-start | bytes 1016072 | tf_op jit(solution)/shard_map/ppermute | solution.py:52
  121.1 12.0 %collective-permute-start.16 = (bf16[168,1008]{1,0:T(8,128)(2,1)}, bf16[168,1008]{1,0:T(8,128)(2,1)S(1)}, u32[]{:S(2)}, u32[]{:S(2)}) collective-permute-start(bf16[168,1008]{1,0:T(8,128)(2,1)} %collective-permute-done.15), channel_id=1, source_target_pairs={{64,0},{65,1},{66,2},{67,3},{68,4},{69,5},{70,6},{71,7},{72,8},{73... | collective-permute-start | bytes 1016072 | tf_op jit(solution)/shard_map/ppermute | solution.py:53
  157.4 12.7 %collective-permute-start.21 = (bf16[168,1008]{1,0:T(8,128)(2,1)S(1)}, bf16[168,1008]{1,0:T(8,128)(2,1)S(1)}, u32[]{:S(2)}, u32[]{:S(2)}) collective-permute-start(bf16[168,1008]{1,0:T(8,128)(2,1)S(1)} %get-tuple-element.40), channel_id=1, source_target_pairs={{0,64},{1,65},{2,66},{3,67},{4,68},{5,69},{6,70},{7,71},{8,72},{9,... | collective-permute-start | bytes 1016072 | tf_op jit(solution)/shard_map/ppermute | solution.py:70
  162.5 7.6 %collective-permute-start.22 = (bf16[168,1008]{1,0:T(8,128)(2,1)S(1)}, bf16[168,1008]{1,0:T(8,128)(2,1)S(1)}, u32[]{:S(2)}, u32[]{:S(2)}) collective-permute-start(bf16[168,1008]{1,0:T(8,128)(2,1)S(1)} %get-tuple-element.41), channel_id=1, source_target_pairs={{448,384},{449,385},{450,386},{451,387},{452,388},{453,389},{454,3... | collective-permute-start | bytes 1016072 | tf_op jit(solution)/shard_map/ppermute | solution.py:71
  164.9 13.9 %collective-permute-start.19 = (bf16[1344,128]{1,0:T(8,128)(2,1)S(1)}, bf16[1344,128]{1,0:T(8,128)(2,1)S(1)}, u32[]{:S(2)}, u32[]{:S(2)}) collective-permute-start(bf16[1344,128]{1,0:T(8,128)(2,1)S(1)} %slice.109), channel_id=1, source_target_pairs={{0,32},{32,0},{1,33},{33,1},{2,34},{34,2},{3,35},{35,3},{4,36},{36... | collective-permute-start | bytes 1032200 | tf_op jit(solution)/shard_map/ppermute | solution.py:42
  172.3 18.0 %collective-permute-start.23 = (bf16[168,1008]{1,0:T(8,128)(2,1)}, bf16[168,1008]{1,0:T(8,128)(2,1)}, u32[]{:S(2)}, u32[]{:S(2)}) collective-permute-start(bf16[168,1008]{1,0:T(8,128)(2,1)} %get-tuple-element.42), channel_id=1, source_target_pairs={{0,64},{64,128},{1,65},{65,129},{2,66},{66,130},{3,67},{67,131},{4... | collective-permute-start | bytes 1016072 | tf_op jit(solution)/shard_map/ppermute | solution.py:70
  177.5 12.9 %collective-permute-start.24 = (bf16[168,1008]{1,0:T(8,128)(2,1)}, bf16[168,1008]{1,0:T(8,128)(2,1)}, u32[]{:S(2)}, u32[]{:S(2)}) collective-permute-start(bf16[168,1008]{1,0:T(8,128)(2,1)} %get-tuple-element.43), channel_id=1, source_target_pairs={{384,320},{448,384},{385,321},{449,385},{386,322},{450,386},{387,3... | collective-permute-start | bytes 1016072 | tf_op jit(solution)/shard_map/ppermute | solution.py:71
  183.1 17.1 %all-to-all-start.2 = ((bf16[16,2,84,128]{3,1,2,0:T(2,128)(2,1)}), bf16[16,2,84,128]{3,1,2,0:T(2,128)(2,1)S(1)}, u32[]{:S(2)}, u32[]{:S(2)}) async-start(bf16[16,2,84,128]{3,1,2,0:T(2,128)(2,1)} %copy.86), calls=%async_computation.2 | async-start | bytes 1376256 | tf_op jit(solution)/shard_map/all_to_all | solution.py:149
  192.6 8.2 %collective-permute-start.25 = (bf16[168,1008]{1,0:T(8,128)(2,1)}, bf16[168,1008]{1,0:T(8,128)(2,1)}, u32[]{:S(2)}, u32[]{:S(2)}) collective-permute-start(bf16[168,1008]{1,0:T(8,128)(2,1)} %get-tuple-element.44), channel_id=1, source_target_pairs={{0,64},{64,128},{128,192},{1,65},{65,129},{129,193},{2,66},{66,130... | collective-permute-start | bytes 1016072 | tf_op jit(solution)/shard_map/ppermute | solution.py:70
  202.9 9.6 %collective-permute-start.27 = (bf16[168,1008]{1,0:T(8,128)(2,1)}, bf16[168,1008]{1,0:T(8,128)(2,1)S(1)}, u32[]{:S(2)}, u32[]{:S(2)}) collective-permute-start(bf16[168,1008]{1,0:T(8,128)(2,1)} %get-tuple-element.46), channel_id=1, source_target_pairs={{0,64},{64,128},{128,192},{192,256},{1,65},{65,129},{129,193},{193... | collective-permute-start | bytes 1016072 | tf_op jit(solution)/shard_map/ppermute | solution.py:70
  214.4 18.6 %collective-permute-start.29 = (bf16[168,1008]{1,0:T(8,128)(2,1)}, bf16[168,1008]{1,0:T(8,128)(2,1)S(1)}, u32[]{:S(2)}, u32[]{:S(2)}) collective-permute-start(bf16[168,1008]{1,0:T(8,128)(2,1)} %get-tuple-element.48), channel_id=1, source_target_pairs={{0,64},{64,128},{128,192},{192,256},{256,320},{1,65},{65,129},{129... | collective-permute-start | bytes 1016072 | tf_op jit(solution)/shard_map/ppermute | solution.py:70
  218.7 15.1 %collective-permute-start.30 = (bf16[168,1008]{1,0:T(8,128)(2,1)S(1)}, bf16[168,1008]{1,0:T(8,128)(2,1)}, u32[]{:S(2)}, u32[]{:S(2)}) collective-permute-start(bf16[168,1008]{1,0:T(8,128)(2,1)S(1)} %get-tuple-element.49), channel_id=1, source_target_pairs={{192,128},{256,192},{320,256},{384,320},{448,384},{193,129},{257,1... | collective-permute-start | bytes 1016072 | tf_op jit(solution)/shard_map/ppermute | solution.py:71
  220.2 15.1 %collective-permute-start.20 = (bf16[84,128]{1,0:T(8,128)(2,1)S(1)}, bf16[84,128]{1,0:T(8,128)(2,1)S(1)}, u32[]{:S(2)}, u32[]{:S(2)}) collective-permute-start(bf16[84,128]{1,0:T(8,128)(2,1)S(1)} %bitcast.222), channel_id=1, source_target_pairs={{0,4},{4,0},{1,5},{5,1},{2,6},{6,2},{3,7},{7,3},{8,12},{12,8},{9,1... | collective-permute-start | bytes 64520 | tf_op jit(solution)/shard_map/ppermute | solution.py:42
  235.3 7.7 %collective-permute-start.31 = (bf16[168,1008]{1,0:T(8,128)(2,1)S(1)}, bf16[168,1008]{1,0:T(8,128)(2,1)}, u32[]{:S(2)}, u32[]{:S(2)}) collective-permute-start(bf16[168,1008]{1,0:T(8,128)(2,1)S(1)} %get-tuple-element.50), channel_id=1, source_target_pairs={{0,64},{64,128},{128,192},{192,256},{256,320},{320,384},{1,65},{65... | collective-permute-start | bytes 1016072 | tf_op jit(solution)/shard_map/ppermute | solution.py:70
  244.3 25.3 %collective-permute-start.33 = (bf16[168,1008]{1,0:T(8,128)(2,1)S(1)}, bf16[168,1008]{1,0:T(8,128)(2,1)S(1)}, u32[]{:S(2)}, u32[]{:S(2)}) collective-permute-start(bf16[168,1008]{1,0:T(8,128)(2,1)S(1)} %get-tuple-element.52), channel_id=1, source_target_pairs={{0,64},{64,128},{128,192},{192,256},{256,320},{320,384},{384,448},... | collective-permute-start | bytes 1016072 | tf_op jit(solution)/shard_map/ppermute | solution.py:70
  264.9 9.1 %collective-permute-start.34 = (bf16[168,1008]{1,0:T(8,128)(2,1)S(1)}, bf16[168,1008]{1,0:T(8,128)(2,1)S(1)}, u32[]{:S(2)}, u32[]{:S(2)}) collective-permute-start(bf16[168,1008]{1,0:T(8,128)(2,1)S(1)} %get-tuple-element.53), channel_id=1, source_target_pairs={{64,0},{128,64},{192,128},{256,192},{320,256},{384,320},{448,384},... | collective-permute-start | bytes 1016072 | tf_op jit(solution)/shard_map/ppermute | solution.py:71
  (33 other events, 401.8 us)

commit v9 on v8

--- a/solution.py
+++ b/solution.py
@@ -59,6 +59,7 @@
 
 def line_scatter(parts, place, ties):
     right = left = None
+    earlier = ((), ())
     for step in range(ZL - 1):
         to_right = parts[jnp.clip(place + ZL - 1 - step, 0, ZL - 1)]
         to_left = parts[jnp.clip(place - ZL + 1 + step, 0, ZL - 1)]
@@ -66,7 +67,9 @@
             to_right = to_right.astype(jnp.float32) + right.astype(jnp.float32)
             to_left = to_left.astype(jnp.float32) + left.astype(jnp.float32)
         to_right, to_left = to_right.astype(jnp.bfloat16), to_left.astype(jnp.bfloat16)
-        to_right, to_left, _ = lax.optimization_barrier((to_right, to_left, ties.get(step, ())))
+        to_right, _ = lax.optimization_barrier((to_right, (earlier[1], ties.get(step, ()))))
+        to_left, _ = lax.optimization_barrier((to_left, earlier[0]))
+        earlier = (right, left) if step else ((), ())
         right = lax.ppermute(to_right, "zl", [(i, i + 1) for i in range(step + 1)])
         left = lax.ppermute(to_left, "zl", [(i, i - 1) for i in range(ZL - 1 - step, ZL)])
     return (

time: 277 us -> 278 us (level)
  the two profiles are of different devices: /device:TPU:6 before, /device:TPU:96 now
where the time goes in v9:
time: 278 us; the launch traced here: 276 us
  starting transfers between devices  129 us (46%)
  waiting for transfers between devices  74.4 us (27%)
  local copies, waits for them, and re-layouts  37.3 us (13%)
  other arithmetic  24.2 us (9%)
  matrix products  9.37 us (3%)
    ppermute x7, starting transfers between devices, swap(): return lax.ppermute(values, axis_name, [(0, 1), (1, 0)])  36 us
    ppermute x7, starting transfers between devices, line_scatter(): right = lax.ppermute(to_right, 'zl', [(i, i + 1) for i in range(step + 1)])  26.7 us
    ppermute x7, starting transfers between devices, line_gather(): right = lax.ppermute(right, 'zl', [(i, i + 1) for i in range(step, ZL - 1)])  26.2 us
    ppermute x7, waiting for transfers between devices, line_gather(): left = lax.ppermute(left, 'zl', [(i, i - 1) for i in range(1, ZL - step)])  18 us
    ppermute x7, waiting for transfers between devices, line_scatter(): lax.ppermute(to_left, 'zl', [(i, i - 1) for i in range(ZL - 1 - step, ZL)])  15.1 us
    ppermute x7, waiting for transfers between devices, line_scatter(): right = lax.ppermute(to_right, 'zl', [(i, i + 1) for i in range(step + 1)])  14.8 us
    unnamed x65, local copies, waits for them, and re-layouts  14.4 us
    ppermute x7, starting transfers between devices, line_gather(): left = lax.ppermute(left, 'zl', [(i, i - 1) for i in range(1, ZL - step)])  12 us
  transfers between devices with their start and end apart: 38, of which 15 were waited for; matrix products, arithmetic and copies ran while one was open for 15% of the time, Pallas kernels for 0%

profile of v9, /device:TPU:96, one launch (start us, length us, event | category | flops | bytes accessed | tf_op | source)
XLA Modules:
  0.0 275.9 jit_solution(14886851766986449805)
XLA Ops:
  4.1 7.0 %all-to-all-start = ((bf16[16,84,640]{2,1,0:T(8,128)(2,1)}), bf16[16,84,640]{2,1,0:T(8,128)(2,1)S(1)}, u32[]{:S(2)}, u32[]{:S(2)}) async-start(bf16[16,84,640]{2,1,0:T(8,128)(2,1)} %broadcast_in_dim.86), calls=%async_computation | async-start | bytes 3604480 | tf_op jit(solution)/shard_map/all_to_all | solution.py:93
  11.2 13.2 %collective-permute-start.1 = (bf16[84,640]{1,0:T(8,128)(2,1)S(1)}, bf16[84,640]{1,0:T(8,128)(2,1)S(1)}, u32[]{:S(2)}, u32[]{:S(2)}) collective-permute-start(bf16[84,640]{1,0:T(8,128)(2,1)S(1)} %constant_dynamic-update-slice_fusion), channel_id=1, source_target_pairs={{0,4},{4,0},{1,5},{5,1},{2,6},{6,2},{3,7},{7,3},{8,12},{12,8},{9,1... | collective-permute-start | bytes 322568 | tf_op jit(solution)/shard_map/ppermute | solution.py:42
  24.3 8.5 %collective-permute-done.1 = bf16[84,640]{1,0:T(8,128)(2,1)S(1)} collective-permute-done((bf16[84,640]{1,0:T(8,128)(2,1)S(1)}, bf16[84,640]{1,0:T(8,128)(2,1)S(1)}, u32[]{:S(2)}, u32[]{:S(2)}) %collective-permute-start.1) | collective-permute-done | bytes 107552 | tf_op jit(solution)/shard_map/ppermute | solution.py:42
  32.8 5.7 %all-to-all-done = bf16[16,84,640]{2,1,0:T(8,128)(2,1)S(1)} async-done(((bf16[16,84,640]{2,1,0:T(8,128)(2,1)}), bf16[16,84,640]{2,1,0:T(8,128)(2,1)S(1)}, u32[]{:S(2)}, u32[]{:S(2)}) %all-to-all-start) | async-done | bytes 1720352 | tf_op jit(solution)/shard_map/all_to_all | solution.py:93
  40.3 3.7 %all-to-all-start.1 = ((bf16[16,84,640]{2,1,0:T(8,128)(2,1)}), bf16[16,84,640]{2,1,0:T(8,128)(2,1)S(1)}, u32[]{:S(2)}, u32[]{:S(2)}) async-start(bf16[16,84,640]{2,1,0:T(8,128)(2,1)} %broadcast_in_dim.87), calls=%async_computation.1 | async-start | bytes 3604480 | tf_op jit(solution)/shard_map/all_to_all | solution.py:93
  46.3 5.0 %collective-permute-start = (bf16[168,1008]{1,0:T(8,128)(2,1)S(1)}, bf16[168,1008]{1,0:T(8,128)(2,1)S(1)}, u32[]{:S(2)}, u32[]{:S(2)}) collective-permute-start(bf16[168,1008]{1,0:T(8,128)(2,1)S(1)} %pad_maximum_fusion.4), channel_id=1, source_target_pairs={{0,64},{64,128},{128,192},{192,256},{256,320},{320,384},{384,448},... | collective-permute-start | bytes 1016072 | tf_op jit(solution)/shard_map/ppermute | solution.py:52
  51.3 5.3 %collective-permute-done.3 = bf16[168,1008]{1,0:T(8,128)(2,1)S(1)} collective-permute-done((bf16[168,1008]{1,0:T(8,128)(2,1)S(1)}, bf16[168,1008]{1,0:T(8,128)(2,1)S(1)}, u32[]{:S(2)}, u32[]{:S(2)}) %collective-permute-start.3) | collective-permute-done | bytes 338720 | tf_op jit(solution)/shard_map/ppermute | solution.py:53
  58.6 5.1 %collective-permute-start.2 = (bf16[168,1008]{1,0:T(8,128)(2,1)S(1)}, bf16[168,1008]{1,0:T(8,128)(2,1)}, u32[]{:S(2)}, u32[]{:S(2)}) collective-permute-start(bf16[168,1008]{1,0:T(8,128)(2,1)S(1)} %collective-permute-done), channel_id=1, source_target_pairs={{64,128},{128,192},{192,256},{256,320},{320,384},{384,448},{65,129... | collective-permute-start | bytes 1016072 | tf_op jit(solution)/shard_map/ppermute | solution.py:52
  70.5 5.1 %collective-permute-start.4 = (bf16[168,1008]{1,0:T(8,128)(2,1)}, bf16[168,1008]{1,0:T(8,128)(2,1)}, u32[]{:S(2)}, u32[]{:S(2)}) collective-permute-start(bf16[168,1008]{1,0:T(8,128)(2,1)} %collective-permute-done.2), channel_id=1, source_target_pairs={{128,192},{192,256},{256,320},{320,384},{384,448},{129,193},{193,2... | collective-permute-start | bytes 1016072 | tf_op jit(solution)/shard_map/ppermute | solution.py:52
  79.0 3.4 %collective-permute-done.7 = bf16[168,1008]{1,0:T(8,128)(2,1)} collective-permute-done((bf16[168,1008]{1,0:T(8,128)(2,1)}, bf16[168,1008]{1,0:T(8,128)(2,1)}, u32[]{:S(2)}, u32[]{:S(2)}) %collective-permute-start.7) | collective-permute-done | bytes 338720 | tf_op jit(solution)/shard_map/ppermute | solution.py:53
  84.4 6.6 %collective-permute-start.6 = (bf16[168,1008]{1,0:T(8,128)(2,1)}, bf16[168,1008]{1,0:T(8,128)(2,1)}, u32[]{:S(2)}, u32[]{:S(2)}) collective-permute-start(bf16[168,1008]{1,0:T(8,128)(2,1)} %collective-permute-done.4), channel_id=1, source_target_pairs={{192,256},{256,320},{320,384},{384,448},{193,257},{257,321},{321,3... | collective-permute-start | bytes 1016072 | tf_op jit(solution)/shard_map/ppermute | solution.py:52
  91.0 4.6 %collective-permute-done.10 = bf16[168,1008]{1,0:T(8,128)(2,1)} collective-permute-done((bf16[168,1008]{1,0:T(8,128)(2,1)}, bf16[168,1008]{1,0:T(8,128)(2,1)}, u32[]{:S(2)}, u32[]{:S(2)}) %collective-permute-start.10) | collective-permute-done | bytes 338720 | tf_op jit(solution)/shard_map/ppermute | solution.py:53
  99.0 4.7 %collective-permute-done.12 = bf16[168,1008]{1,0:T(8,128)(2,1)} collective-permute-done((bf16[168,1008]{1,0:T(8,128)(2,1)}, bf16[168,1008]{1,0:T(8,128)(2,1)}, u32[]{:S(2)}, u32[]{:S(2)}) %collective-permute-start.12) | collective-permute-done | bytes 338720 | tf_op jit(solution)/shard_map/ppermute | solution.py:53
  110.0 2.1 pad_maximum_fusion
  112.1 3.0 %reshape.181 = bf16[1344,1280]{1,0:T(8,128)(2,1)S(1)} reshape(bf16[4,2,2,84,1280]{4,3,2,1,0:T(8,128)(2,1)} %pad_maximum_fusion) | data formatting | bytes 6881280 | tf_op jit(solution)/shard_map/reshape | solution.py:111
  115.2 3.6 %copy.83 = bf16[1280,1344]{1,0:T(8,128)(2,1)} copy(bf16[1280,1344]{0,1:T(8,128)(2,1)S(1)} %bitcast.203) | data formatting | bytes 6881280 | tf_op jit(solution)/shard_map/dot_general | solution.py:22
  132.1 4.6 %fusion.71 = f32[2,5,128,1008]{2,3,1,0:T(8,128)S(1)} fusion(bf16[2,5,128,1344]{3,2,1,0:T(8,128)(2,1)S(1)} %bitcast.215, bf16[1344,1008,1,1]{1,0,3,2:T(8,128)(2,1)S(1)} %bitcast.218), kind=kOutput, calls=%fused_computation.170 | convolution fusion | flops 3468165120 | bytes 11311104 | tf_op jit(solution)/shard_map/dot_general | solution.py:22
  137.1 2.1 collective-permute-start.17
  151.3 4.0 %convolution_convert_fusion = bf16[1344,1008]{1,0:T(8,128)(2,1)S(1)} fusion(bf16[1344,1280]{1,0:T(8,128)(2,1)S(1)} %reshape.181, bf16[512,1008]{0,1:T(8,128)(2,1)S(1)} %get-tuple-element.100, bf16[128,1008]{0,1:T(8,128)(2,1)S(1)} %broadcast_select_fusion.4, bf16[512,1008]{0,1:T(8,128)(2,1)S(1)} %get-tuple-element.99, bf16[128,1008]{0,1:T(8,128)(2,1)S(1)} %copy-done.22), kind=kOutput, calls=%fused_computation | convolution fusion | flops 3479841792 | bytes 8730624 | tf_op jit(solution)/shard_map/dot_general | solution.py:22
  169.6 6.9 %all-to-all-start.2 = ((bf16[16,2,84,128]{3,1,2,0:T(2,128)(2,1)}), bf16[16,2,84,128]{3,1,2,0:T(2,128)(2,1)S(1)}, u32[]{:S(2)}, u32[]{:S(2)}) async-start(bf16[16,2,84,128]{3,1,2,0:T(2,128)(2,1)} %copy.86), calls=%async_computation.2 | async-start | bytes 1376256 | tf_op jit(solution)/shard_map/all_to_all | solution.py:152
  176.6 2.2 fusion.29
  181.6 8.8 %all-to-all-done.2 = bf16[16,2,84,128]{3,1,2,0:T(2,128)(2,1)S(1)} async-done(((bf16[16,2,84,128]{3,1,2,0:T(2,128)(2,1)}), bf16[16,2,84,128]{3,1,2,0:T(2,128)(2,1)S(1)}, u32[]{:S(2)}, u32[]{:S(2)}) %all-to-all-start.2) | async-done | bytes 688160 | tf_op jit(solution)/shard_map/all_to_all | solution.py:152
  191.0 3.9 %collective-permute-done.24 = bf16[168,1008]{1,0:T(8,128)(2,1)} collective-permute-done((bf16[168,1008]{1,0:T(8,128)(2,1)}, bf16[168,1008]{1,0:T(8,128)(2,1)}, u32[]{:S(2)}, u32[]{:S(2)}) %collective-permute-start.24) | collective-permute-done | bytes 338720 | tf_op jit(solution)/shard_map/ppermute | solution.py:73
  194.9 2.1 fusion.30
  199.6 10.4 %collective-permute-done.26 = bf16[168,1008]{1,0:T(8,128)(2,1)} collective-permute-done((bf16[168,1008]{1,0:T(8,128)(2,1)S(1)}, bf16[168,1008]{1,0:T(8,128)(2,1)}, u32[]{:S(2)}, u32[]{:S(2)}) %collective-permute-start.26) | collective-permute-done | bytes 338720 | tf_op jit(solution)/shard_map/ppermute | solution.py:73
  213.2 10.0 %collective-permute-start.28 = (bf16[168,1008]{1,0:T(8,128)(2,1)S(1)}, bf16[168,1008]{1,0:T(8,128)(2,1)}, u32[]{:S(2)}, u32[]{:S(2)}) collective-permute-start(bf16[168,1008]{1,0:T(8,128)(2,1)S(1)} %get-tuple-element.39), channel_id=1, source_target_pairs={{0,64},{64,128},{128,192},{192,256},{256,320},{1,65},{65,129},{129... | collective-permute-start | bytes 1016072 | tf_op jit(solution)/shard_map/ppermute | solution.py:73
  223.3 12.8 %collective-permute-start.20 = (bf16[84,128]{1,0:T(8,128)(2,1)S(1)}, bf16[84,128]{1,0:T(8,128)(2,1)S(1)}, u32[]{:S(2)}, u32[]{:S(2)}) collective-permute-start(bf16[84,128]{1,0:T(8,128)(2,1)S(1)} %bitcast.223), channel_id=1, source_target_pairs={{0,4},{4,0},{1,5},{5,1},{2,6},{6,2},{3,7},{7,3},{8,12},{12,8},{9,1... | collective-permute-start | bytes 64520 | tf_op jit(solution)/shard_map/ppermute | solution.py:42
  240.1 5.7 %collective-permute-start.30 = (bf16[168,1008]{1,0:T(8,128)(2,1)S(1)}, bf16[168,1008]{1,0:T(8,128)(2,1)}, u32[]{:S(2)}, u32[]{:S(2)}) collective-permute-start(bf16[168,1008]{1,0:T(8,128)(2,1)S(1)} %get-tuple-element.41), channel_id=1, source_target_pairs={{0,64},{64,128},{128,192},{192,256},{256,320},{320,384},{1,65},{65... | collective-permute-start | bytes 1016072 | tf_op jit(solution)/shard_map/ppermute | solution.py:73
  245.9 4.0 %collective-permute-done.31 = bf16[168,1008]{1,0:T(8,128)(2,1)S(1)} collective-permute-done((bf16[168,1008]{1,0:T(8,128)(2,1)}, bf16[168,1008]{1,0:T(8,128)(2,1)S(1)}, u32[]{:S(2)}, u32[]{:S(2)}) %collective-permute-start.31) | collective-permute-done | bytes 338720 | tf_op jit(solution)/shard_map/ppermute | solution.py:74
  254.3 5.7 %collective-permute-start.32 = (bf16[168,1008]{1,0:T(8,128)(2,1)S(1)}, bf16[168,1008]{1,0:T(8,128)(2,1)S(1)}, u32[]{:S(2)}, u32[]{:S(2)}) collective-permute-start(bf16[168,1008]{1,0:T(8,128)(2,1)S(1)} %get-tuple-element.43), channel_id=1, source_target_pairs={{0,64},{64,128},{128,192},{192,256},{256,320},{320,384},{384,448},... | collective-permute-start | bytes 1016072 | tf_op jit(solution)/shard_map/ppermute | solution.py:73
  260.0 3.4 %collective-permute-done.33 = bf16[168,1008]{1,0:T(8,128)(2,1)} collective-permute-done((bf16[168,1008]{1,0:T(8,128)(2,1)S(1)}, bf16[168,1008]{1,0:T(8,128)(2,1)}, u32[]{:S(2)}, u32[]{:S(2)}) %collective-permute-start.33) | collective-permute-done | bytes 338720 | tf_op jit(solution)/shard_map/ppermute | solution.py:74
  267.1 7.8 %collective-permute-done.34 = bf16[168,1008]{1,0:T(8,128)(2,1)S(1)} collective-permute-done((bf16[168,1008]{1,0:T(8,128)(2,1)S(1)}, bf16[168,1008]{1,0:T(8,128)(2,1)S(1)}, u32[]{:S(2)}, u32[]{:S(2)}) %collective-permute-start.34) | collective-permute-done | bytes 338720 | tf_op jit(solution)/shard_map/ppermute | solution.py:74
  (166 shorter events, 93.0 us)
Async XLA Ops:
  4.1 34.5 %all-to-all-start = ((bf16[16,84,640]{2,1,0:T(8,128)(2,1)}), bf16[16,84,640]{2,1,0:T(8,128)(2,1)S(1)}, u32[]{:S(2)}, u32[]{:S(2)}) async-start(bf16[16,84,640]{2,1,0:T(8,128)(2,1)} %broadcast_in_dim.86), calls=%async_computation | async-start | bytes 3604480 | tf_op jit(solution)/shard_map/all_to_all | solution.py:93
  11.2 21.6 %collective-permute-start.1 = (bf16[84,640]{1,0:T(8,128)(2,1)S(1)}, bf16[84,640]{1,0:T(8,128)(2,1)S(1)}, u32[]{:S(2)}, u32[]{:S(2)}) collective-permute-start(bf16[84,640]{1,0:T(8,128)(2,1)S(1)} %constant_dynamic-update-slice_fusion), channel_id=1, source_target_pairs={{0,4},{4,0},{1,5},{5,1},{2,6},{6,2},{3,7},{7,3},{8,12},{12,8},{9,1... | collective-permute-start | bytes 322568 | tf_op jit(solution)/shard_map/ppermute | solution.py:42
  40.3 35.3 %all-to-all-start.1 = ((bf16[16,84,640]{2,1,0:T(8,128)(2,1)}), bf16[16,84,640]{2,1,0:T(8,128)(2,1)S(1)}, u32[]{:S(2)}, u32[]{:S(2)}) async-start(bf16[16,84,640]{2,1,0:T(8,128)(2,1)} %broadcast_in_dim.87), calls=%async_computation.1 | async-start | bytes 3604480 | tf_op jit(solution)/shard_map/all_to_all | solution.py:93
  44.3 12.4 %collective-permute-start.3 = (bf16[168,1008]{1,0:T(8,128)(2,1)S(1)}, bf16[168,1008]{1,0:T(8,128)(2,1)S(1)}, u32[]{:S(2)}, u32[]{:S(2)}) collective-permute-start(bf16[168,1008]{1,0:T(8,128)(2,1)S(1)} %pad_maximum_fusion.4), channel_id=1, source_target_pairs={{64,0},{128,64},{192,128},{256,192},{320,256},{384,320},{448,384},... | collective-permute-start | bytes 1016072 | tf_op jit(solution)/shard_map/ppermute | solution.py:53
  46.3 12.3 %collective-permute-start = (bf16[168,1008]{1,0:T(8,128)(2,1)S(1)}, bf16[168,1008]{1,0:T(8,128)(2,1)S(1)}, u32[]{:S(2)}, u32[]{:S(2)}) collective-permute-start(bf16[168,1008]{1,0:T(8,128)(2,1)S(1)} %pad_maximum_fusion.4), channel_id=1, source_target_pairs={{0,64},{64,128},{128,192},{192,256},{256,320},{320,384},{384,448},... | collective-permute-start | bytes 1016072 | tf_op jit(solution)/shard_map/ppermute | solution.py:52
  56.7 11.9 %collective-permute-start.5 = (bf16[168,1008]{1,0:T(8,128)(2,1)S(1)}, bf16[168,1008]{1,0:T(8,128)(2,1)}, u32[]{:S(2)}, u32[]{:S(2)}) collective-permute-start(bf16[168,1008]{1,0:T(8,128)(2,1)S(1)} %collective-permute-done.3), channel_id=1, source_target_pairs={{64,0},{128,64},{192,128},{256,192},{320,256},{384,320},{65,1},{12... | collective-permute-start | bytes 1016072 | tf_op jit(solution)/shard_map/ppermute | solution.py:53
  58.6 11.9 %collective-permute-start.2 = (bf16[168,1008]{1,0:T(8,128)(2,1)S(1)}, bf16[168,1008]{1,0:T(8,128)(2,1)}, u32[]{:S(2)}, u32[]{:S(2)}) collective-permute-start(bf16[168,1008]{1,0:T(8,128)(2,1)S(1)} %collective-permute-done), channel_id=1, source_target_pairs={{64,128},{128,192},{192,256},{256,320},{320,384},{384,448},{65,129... | collective-permute-start | bytes 1016072 | tf_op jit(solution)/shard_map/ppermute | solution.py:52
  66.6 31.0 %collective-permute-start.8 = (bf16[4,2,84,640]{3,0,2,1:T(4,128)(2,1)}, bf16[4,2,84,640]{3,0,2,1:T(4,128)(2,1)}, u32[]{:S(2)}, u32[]{:S(2)}) collective-permute-start(bf16[4,2,84,640]{3,0,2,1:T(4,128)(2,1)} %copy.79), channel_id=1, source_target_pairs={{0,32},{32,0},{1,33},{33,1},{2,34},{34,2},{3,35},{35,3},{4,36},{36... | collective-permute-start | bytes 2580488 | tf_op jit(solution)/shard_map/ppermute | solution.py:42
  68.5 13.9 %collective-permute-start.7 = (bf16[168,1008]{1,0:T(8,128)(2,1)}, bf16[168,1008]{1,0:T(8,128)(2,1)}, u32[]{:S(2)}, u32[]{:S(2)}) collective-permute-start(bf16[168,1008]{1,0:T(8,128)(2,1)} %collective-permute-done.5), channel_id=1, source_target_pairs={{64,0},{128,64},{192,128},{256,192},{320,256},{65,1},{129,65},{193... | collective-permute-start | bytes 1016072 | tf_op jit(solution)/shard_map/ppermute | solution.py:53
  70.5 13.9 %collective-permute-start.4 = (bf16[168,1008]{1,0:T(8,128)(2,1)}, bf16[168,1008]{1,0:T(8,128)(2,1)}, u32[]{:S(2)}, u32[]{:S(2)}) collective-permute-start(bf16[168,1008]{1,0:T(8,128)(2,1)} %collective-permute-done.2), channel_id=1, source_target_pairs={{128,192},{192,256},{256,320},{320,384},{384,448},{129,193},{193,2... | collective-permute-start | bytes 1016072 | tf_op jit(solution)/shard_map/ppermute | solution.py:52
  77.1 29.3 %collective-permute-start.13 = (bf16[4,2,84,640]{3,0,2,1:T(4,128)(2,1)S(1)}, bf16[4,2,84,640]{3,0,2,1:T(4,128)(2,1)S(1)}, u32[]{:S(2)}, u32[]{:S(2)}) collective-permute-start(bf16[4,2,84,640]{3,0,2,1:T(4,128)(2,1)S(1)} %copy.80), channel_id=1, source_target_pairs={{0,32},{32,0},{1,33},{33,1},{2,34},{34,2},{3,35},{35,3},{4,36},{36... | collective-permute-start | bytes 2580488 | tf_op jit(solution)/shard_map/ppermute | solution.py:42
  82.4 13.1 %collective-permute-start.10 = (bf16[168,1008]{1,0:T(8,128)(2,1)}, bf16[168,1008]{1,0:T(8,128)(2,1)}, u32[]{:S(2)}, u32[]{:S(2)}) collective-permute-start(bf16[168,1008]{1,0:T(8,128)(2,1)} %collective-permute-done.7), channel_id=1, source_target_pairs={{64,0},{128,64},{192,128},{256,192},{65,1},{129,65},{193,129},{257... | collective-permute-start | bytes 1016072 | tf_op jit(solution)/shard_map/ppermute | solution.py:53
  84.4 13.2 %collective-permute-start.6 = (bf16[168,1008]{1,0:T(8,128)(2,1)}, bf16[168,1008]{1,0:T(8,128)(2,1)}, u32[]{:S(2)}, u32[]{:S(2)}) collective-permute-start(bf16[168,1008]{1,0:T(8,128)(2,1)} %collective-permute-done.4), channel_id=1, source_target_pairs={{192,256},{256,320},{320,384},{384,448},{193,257},{257,321},{321,3... | collective-permute-start | bytes 1016072 | tf_op jit(solution)/shard_map/ppermute | solution.py:52
  95.5 8.2 %collective-permute-start.12 = (bf16[168,1008]{1,0:T(8,128)(2,1)}, bf16[168,1008]{1,0:T(8,128)(2,1)}, u32[]{:S(2)}, u32[]{:S(2)}) collective-permute-start(bf16[168,1008]{1,0:T(8,128)(2,1)} %collective-permute-done.10), channel_id=1, source_target_pairs={{64,0},{128,64},{192,128},{65,1},{129,65},{193,129},{66,2},{130,66... | collective-permute-start | bytes 1016072 | tf_op jit(solution)/shard_map/ppermute | solution.py:53
  97.6 8.9 %collective-permute-start.9 = (bf16[168,1008]{1,0:T(8,128)(2,1)}, bf16[168,1008]{1,0:T(8,128)(2,1)}, u32[]{:S(2)}, u32[]{:S(2)}) collective-permute-start(bf16[168,1008]{1,0:T(8,128)(2,1)} %collective-permute-done.6), channel_id=1, source_target_pairs={{256,320},{320,384},{384,448},{257,321},{321,385},{385,449},{258,3... | collective-permute-start | bytes 1016072 | tf_op jit(solution)/shard_map/ppermute | solution.py:52
  103.7 15.1 %collective-permute-start.15 = (bf16[168,1008]{1,0:T(8,128)(2,1)}, bf16[168,1008]{1,0:T(8,128)(2,1)}, u32[]{:S(2)}, u32[]{:S(2)}) collective-permute-start(bf16[168,1008]{1,0:T(8,128)(2,1)} %collective-permute-done.12), channel_id=1, source_target_pairs={{64,0},{128,64},{65,1},{129,65},{66,2},{130,66},{67,3},{131,67},{6... | collective-permute-start | bytes 1016072 | tf_op jit(solution)/shard_map/ppermute | solution.py:53
  108.6 11.0 %collective-permute-start.14 = (bf16[168,1008]{1,0:T(8,128)(2,1)}, bf16[168,1008]{1,0:T(8,128)(2,1)}, u32[]{:S(2)}, u32[]{:S(2)}) collective-permute-start(bf16[168,1008]{1,0:T(8,128)(2,1)} %collective-permute-done.11), channel_id=1, source_target_pairs={{384,448},{385,449},{386,450},{387,451},{388,452},{389,453},{390,4... | collective-permute-start | bytes 1016072 | tf_op jit(solution)/shard_map/ppermute | solution.py:52
  118.8 12.3 %collective-permute-start.16 = (bf16[168,1008]{1,0:T(8,128)(2,1)}, bf16[168,1008]{1,0:T(8,128)(2,1)S(1)}, u32[]{:S(2)}, u32[]{:S(2)}) collective-permute-start(bf16[168,1008]{1,0:T(8,128)(2,1)} %collective-permute-done.15), channel_id=1, source_target_pairs={{64,0},{65,1},{66,2},{67,3},{68,4},{69,5},{70,6},{71,7},{72,8},{73... | collective-permute-start | bytes 1016072 | tf_op jit(solution)/shard_map/ppermute | solution.py:53
  160.7 15.9 %collective-permute-start.23 = (bf16[168,1008]{1,0:T(8,128)(2,1)}, bf16[168,1008]{1,0:T(8,128)(2,1)}, u32[]{:S(2)}, u32[]{:S(2)}) collective-permute-start(bf16[168,1008]{1,0:T(8,128)(2,1)} %get-tuple-element.67), channel_id=1, source_target_pairs={{448,384},{449,385},{450,386},{451,387},{452,388},{453,389},{454,3... | collective-permute-start | bytes 1016072 | tf_op jit(solution)/shard_map/ppermute | solution.py:74
  164.0 12.6 %collective-permute-start.22 = (bf16[168,1008]{1,0:T(8,128)(2,1)}, bf16[168,1008]{1,0:T(8,128)(2,1)}, u32[]{:S(2)}, u32[]{:S(2)}) collective-permute-start(bf16[168,1008]{1,0:T(8,128)(2,1)} %fusion.28), channel_id=1, source_target_pairs={{0,64},{64,128},{1,65},{65,129},{2,66},{66,130},{3,67},{67,131},{4... | collective-permute-start | bytes 1016072 | tf_op jit(solution)/shard_map/ppermute | solution.py:73
  169.6 20.8 %all-to-all-start.2 = ((bf16[16,2,84,128]{3,1,2,0:T(2,128)(2,1)}), bf16[16,2,84,128]{3,1,2,0:T(2,128)(2,1)S(1)}, u32[]{:S(2)}, u32[]{:S(2)}) async-start(bf16[16,2,84,128]{3,1,2,0:T(2,128)(2,1)} %copy.86), calls=%async_computation.2 | async-start | bytes 1376256 | tf_op jit(solution)/shard_map/all_to_all | solution.py:152
  178.9 16.0 %collective-permute-start.24 = (bf16[168,1008]{1,0:T(8,128)(2,1)}, bf16[168,1008]{1,0:T(8,128)(2,1)}, u32[]{:S(2)}, u32[]{:S(2)}) collective-permute-start(bf16[168,1008]{1,0:T(8,128)(2,1)} %get-tuple-element.36), channel_id=1, source_target_pairs={{0,64},{64,128},{128,192},{1,65},{65,129},{129,193},{2,66},{66,130... | collective-permute-start | bytes 1016072 | tf_op jit(solution)/shard_map/ppermute | solution.py:73
  180.2 14.7 %collective-permute-start.25 = (bf16[168,1008]{1,0:T(8,128)(2,1)}, bf16[168,1008]{1,0:T(8,128)(2,1)}, u32[]{:S(2)}, u32[]{:S(2)}) collective-permute-start(bf16[168,1008]{1,0:T(8,128)(2,1)} %get-tuple-element.65), channel_id=1, source_target_pairs={{384,320},{448,384},{385,321},{449,385},{386,322},{450,386},{387,3... | collective-permute-start | bytes 1016072 | tf_op jit(solution)/shard_map/ppermute | solution.py:74
  197.7 12.3 %collective-permute-start.26 = (bf16[168,1008]{1,0:T(8,128)(2,1)S(1)}, bf16[168,1008]{1,0:T(8,128)(2,1)}, u32[]{:S(2)}, u32[]{:S(2)}) collective-permute-start(bf16[168,1008]{1,0:T(8,128)(2,1)S(1)} %get-tuple-element.37), channel_id=1, source_target_pairs={{0,64},{64,128},{128,192},{192,256},{1,65},{65,129},{129,193},{193... | collective-permute-start | bytes 1016072 | tf_op jit(solution)/shard_map/ppermute | solution.py:73
  212.0 24.2 %collective-permute-start.29 = (bf16[168,1008]{1,0:T(8,128)(2,1)}, bf16[168,1008]{1,0:T(8,128)(2,1)S(1)}, u32[]{:S(2)}, u32[]{:S(2)}) collective-permute-start(bf16[168,1008]{1,0:T(8,128)(2,1)} %get-tuple-element.40), channel_id=1, source_target_pairs={{256,192},{320,256},{384,320},{448,384},{257,193},{321,257},{385,3... | collective-permute-start | bytes 1016072 | tf_op jit(solution)/shard_map/ppermute | solution.py:74
  213.2 22.9 %collective-permute-start.28 = (bf16[168,1008]{1,0:T(8,128)(2,1)S(1)}, bf16[168,1008]{1,0:T(8,128)(2,1)}, u32[]{:S(2)}, u32[]{:S(2)}) collective-permute-start(bf16[168,1008]{1,0:T(8,128)(2,1)S(1)} %get-tuple-element.39), channel_id=1, source_target_pairs={{0,64},{64,128},{128,192},{192,256},{256,320},{1,65},{65,129},{129... | collective-permute-start | bytes 1016072 | tf_op jit(solution)/shard_map/ppermute | solution.py:73
  223.3 16.8 %collective-permute-start.20 = (bf16[84,128]{1,0:T(8,128)(2,1)S(1)}, bf16[84,128]{1,0:T(8,128)(2,1)S(1)}, u32[]{:S(2)}, u32[]{:S(2)}) collective-permute-start(bf16[84,128]{1,0:T(8,128)(2,1)S(1)} %bitcast.223), channel_id=1, source_target_pairs={{0,4},{4,0},{1,5},{5,1},{2,6},{6,2},{3,7},{7,3},{8,12},{12,8},{9,1... | collective-permute-start | bytes 64520 | tf_op jit(solution)/shard_map/ppermute | solution.py:42
  238.2 11.7 %collective-permute-start.31 = (bf16[168,1008]{1,0:T(8,128)(2,1)}, bf16[168,1008]{1,0:T(8,128)(2,1)S(1)}, u32[]{:S(2)}, u32[]{:S(2)}) collective-permute-start(bf16[168,1008]{1,0:T(8,128)(2,1)} %get-tuple-element.42), channel_id=1, source_target_pairs={{192,128},{256,192},{320,256},{384,320},{448,384},{193,129},{257,1... | collective-permute-start | bytes 1016072 | tf_op jit(solution)/shard_map/ppermute | solution.py:74
  240.1 11.0 %collective-permute-start.30 = (bf16[168,1008]{1,0:T(8,128)(2,1)S(1)}, bf16[168,1008]{1,0:T(8,128)(2,1)}, u32[]{:S(2)}, u32[]{:S(2)}) collective-permute-start(bf16[168,1008]{1,0:T(8,128)(2,1)S(1)} %get-tuple-element.41), channel_id=1, source_target_pairs={{0,64},{64,128},{128,192},{192,256},{256,320},{320,384},{1,65},{65... | collective-permute-start | bytes 1016072 | tf_op jit(solution)/shard_map/ppermute | solution.py:73
  252.4 11.0 %collective-permute-start.33 = (bf16[168,1008]{1,0:T(8,128)(2,1)S(1)}, bf16[168,1008]{1,0:T(8,128)(2,1)}, u32[]{:S(2)}, u32[]{:S(2)}) collective-permute-start(bf16[168,1008]{1,0:T(8,128)(2,1)S(1)} %get-tuple-element.44), channel_id=1, source_target_pairs={{128,64},{192,128},{256,192},{320,256},{384,320},{448,384},{129,65... | collective-permute-start | bytes 1016072 | tf_op jit(solution)/shard_map/ppermute | solution.py:74
  254.3 12.8 %collective-permute-start.32 = (bf16[168,1008]{1,0:T(8,128)(2,1)S(1)}, bf16[168,1008]{1,0:T(8,128)(2,1)S(1)}, u32[]{:S(2)}, u32[]{:S(2)}) collective-permute-start(bf16[168,1008]{1,0:T(8,128)(2,1)S(1)} %get-tuple-element.43), channel_id=1, source_target_pairs={{0,64},{64,128},{128,192},{192,256},{256,320},{320,384},{384,448},... | collective-permute-start | bytes 1016072 | tf_op jit(solution)/shard_map/ppermute | solution.py:73
  264.5 10.4 %collective-permute-start.34 = (bf16[168,1008]{1,0:T(8,128)(2,1)S(1)}, bf16[168,1008]{1,0:T(8,128)(2,1)S(1)}, u32[]{:S(2)}, u32[]{:S(2)}) collective-permute-start(bf16[168,1008]{1,0:T(8,128)(2,1)S(1)} %fusion.23), channel_id=1, source_target_pairs={{64,0},{128,64},{192,128},{256,192},{320,256},{384,320},{448,384},... | collective-permute-start | bytes 1016072 | tf_op jit(solution)/shard_map/ppermute | solution.py:74
  (31 other events, 326.1 us)
